TPU v7x, 512 devices: a whole 4x8x8 slice. The times are simulated.
512 devices in a mesh: group: 4 (over x_lo, core), expert: 64 (over y, z), tensor: 2 (over x_hi).
Axes of the slice: x: 4 (x_hi: 2, x_lo: 2; x = x_hi * 2 + x_lo), y: 8, z: 8, core: 2. Of those that a mesh axis runs over, the one named last changes fastest.
Arguments:
- hidden_rows: bfloat16 [1024, 3584], P('expert'), may hold values from -6 to 6
- parent_beam: int32 [1024], P('expert'), may hold values from 0 to 3
- norm_gain: float32 [3584], replicated, may hold values from 0.5 to 1.5
- route_ids: int32 [1024, 8], P('expert'), may hold values from 0 to 63, all different within a row; in each aligned block of 16 rows (0 to 15, 16 to 31, ...) at most 4 rows name the same one
- route_weight: float32 [1024, 8], P('expert'), may hold values from 0.05 to 0.5
- expert_weight: bfloat16 [64, 3584, 2, 1024], P('expert', None, None, ('group', 'tensor')), may hold values from -0.09375 to 0.09375
- learn_tokens: bfloat16 [8192, 3584], P('expert'), may hold values from -6 to 6
- learn_live: int32 [8192], P('expert'), may hold values 0 or 1
- cotangent: bfloat16 [8192, 1024], P('expert', ('group', 'tensor')), may hold values from -0.52734375 to 0.52734375
- master: float32 [3584, 2, 1024], P('expert', None, ('group', 'tensor')), may hold values from -0.09375 to 0.09375
- first_moment: float32 [3584, 2, 1024], P('expert', None, ('group', 'tensor')), may hold values from -4 to 4
- second_moment: float32 [3584, 2, 1024], P('expert', None, ('group', 'tensor')), may hold values from 0.05 to 1
Outputs:
- rolled: bfloat16 [1024, 8, 1024], P('expert', None, ('group', 'tensor'))
- new_master: float32 [3584, 2, 1024], P('expert', None, ('group', 'tensor'))
- new_first: float32 [3584, 2, 1024], P('expert', None, ('group', 'tensor'))
- new_second: float32 [3584, 2, 1024], P('expert', None, ('group', 'tensor'))
- fresh: bfloat16 [3584, 2, 1024], P(None, None, ('group', 'tensor'))
Inputs may be any that keep to these rules, and one draw needn't show every extreme that they name: `route_ids`: in each aligned block of 16 rows (the rows of one device) the 8 experts of a row differ, no expert is named by more than 4 rows, a bound that some block reaches. `parent_beam`: rows 4 * q to 4 * q + 3 are the beams of one request.
All inputs are finite; a program needn't handle non-finite values. No bound on the sum of `learn_live` on one device may be relied on, other than what follows from the above.
Results may differ from a plain program's by a relative error of at most 0.0065.
Values may be sent and summed in bfloat16 or wider, within the bound.
No kernel may reach another device: no remote copies, remote signals or barrier semaphores. Data moves between devices by JAX's collectives and lax.ppermute only.
A program may use at most 64 MiB of HBM per device.

v0:
```python
import jax
import jax.numpy as jnp
from jax import lax
from jax.sharding import PartitionSpec as P

EXPERTS = 64
TOP = 8
BEAMS = 4
CAP = 4


beta_one = 0.9
beta_two = 0.95
learn_rate = 0.01
decay_rate = 0.1
epsilon = 1e-08
norm_epsilon = 1e-06
adam_step = 10.0


def shards(
    hidden_rows,
    parent_beam,
    norm_gain,
    route_ids,
    route_weight,
    expert_weight,
    learn_tokens,
    learn_live,
    cotangent,
    master,
    first_moment,
    second_moment,
):
    hid_local = master.shape[2]
    own_rows = master.shape[0]
    weights_low = master.astype(jnp.bfloat16).reshape(own_rows, 2 * hid_local)
    columns = learn_tokens
    projected = jnp.dot(
        columns,
        lax.all_gather(weights_low, "expert", axis=0, tiled=True),
        preferred_element_type=jnp.float32,
    )
    gate_pre = projected[:, :hid_local]
    up_pre = projected[:, hid_local:]
    sigmoid_gate = jax.nn.sigmoid(gate_pre)
    upstream = cotangent.astype(jnp.float32) * learn_live.astype(jnp.float32)[:, None]
    slope = sigmoid_gate * (1.0 + gate_pre * (1.0 - sigmoid_gate))
    grad_pre = jnp.concatenate(
        [upstream * up_pre * slope, upstream * gate_pre * sigmoid_gate], axis=1
    ).astype(jnp.bfloat16)
    columns = learn_tokens
    gradient = lax.psum_scatter(
        lax.dot_general(
            columns, grad_pre, (((0,), (0,)), ((), ())), preferred_element_type=jnp.float32
        ),
        "expert",
        scatter_dimension=0,
        tiled=True,
    ).reshape(master.shape)
    new_first = beta_one * first_moment + (1.0 - beta_one) * gradient
    new_second = beta_two * second_moment + (1.0 - beta_two) * gradient * gradient
    correct_one = 1.0 - beta_one**adam_step
    correct_two = 1.0 - beta_two**adam_step
    update = new_first / correct_one / (jnp.sqrt(new_second / correct_two) + epsilon)
    new_master = master - learn_rate * (update + decay_rate * master)
    fresh = lax.all_gather(new_master.astype(jnp.bfloat16), "expert", axis=0, tiled=True)
    rows_dev = hidden_rows.shape[0]
    width = hidden_rows.shape[1]
    grouped = hidden_rows.reshape(rows_dev // BEAMS, BEAMS, width)
    selector = (
        parent_beam.reshape(rows_dev // BEAMS, BEAMS, 1)
        == jnp.arange(BEAMS, dtype=jnp.int32)[None, None, :]
    ).astype(jnp.bfloat16)
    reordered = jnp.einsum(
        "rbc,rcd->rbd", selector, grouped, preferred_element_type=jnp.float32
    ).reshape(rows_dev, width)
    mean_square = jnp.mean(reordered * reordered, axis=1, keepdims=True)
    normed = (reordered * lax.rsqrt(mean_square + norm_epsilon) * norm_gain[None, :]).astype(
        jnp.bfloat16
    )
    flat_ids = route_ids.reshape(rows_dev * TOP)
    onehot = (flat_ids[:, None] == jnp.arange(EXPERTS, dtype=jnp.int32)[None, :]).astype(jnp.int32)
    earlier = jnp.cumsum(onehot, axis=0) - onehot
    position = jnp.sum(earlier * onehot, axis=1)
    slot_index = flat_ids * CAP + position
    slot_table = (
        slot_index[:, None] == jnp.arange(EXPERTS * CAP, dtype=jnp.int32)[None, :]
    ).astype(jnp.float32)
    row_table = slot_table.reshape(rows_dev, TOP, EXPERTS * CAP).sum(axis=1).astype(jnp.bfloat16)
    outgoing = lax.dot_general(
        row_table, normed, (((0,), (0,)), ((), ())), preferred_element_type=jnp.float32
    ).astype(jnp.bfloat16)
    owners = lax.axis_size("expert")
    local_count = expert_weight.shape[0]
    outgoing = outgoing.reshape(owners, local_count, CAP, width)
    local_weight = expert_weight.reshape(local_count, width, 2 * hid_local)
    projected_rows = jnp.einsum(
        "slcd,ldk->slck",
        lax.all_to_all(outgoing, "expert", split_axis=0, concat_axis=0, tiled=True),
        local_weight,
        preferred_element_type=jnp.float32,
    )
    gate_rows = projected_rows[..., :hid_local]
    activated_rows = (
        gate_rows * jax.nn.sigmoid(gate_rows) * projected_rows[..., hid_local:]
    ).astype(jnp.bfloat16)
    returned = lax.all_to_all(activated_rows, "expert", split_axis=0, concat_axis=0, tiled=True)
    back_slots = returned.reshape(EXPERTS * CAP, hid_local)
    picked = jnp.dot(
        slot_table.astype(jnp.bfloat16), back_slots, preferred_element_type=jnp.float32
    )
    rolled = (
        (picked * route_weight.reshape(rows_dev * TOP, 1))
        .astype(jnp.bfloat16)
        .reshape(rows_dev, TOP, hid_local)
    )
    return (rolled, new_master, new_first, new_second, fresh)


def solution(mesh):
    placed = (
        P("expert", None),
        P("expert"),
        P(),
        P("expert", None),
        P("expert", None),
        P("expert", None, None, ("group", "tensor")),
        P("expert", None),
        P("expert"),
        P("expert", ("group", "tensor")),
        P("expert", None, ("group", "tensor")),
        P("expert", None, ("group", "tensor")),
        P("expert", None, ("group", "tensor")),
    )
    return jax.shard_map(
        shards,
        mesh=mesh,
        in_specs=placed,
        out_specs=(
            P("expert", None, ("group", "tensor")),
            P("expert", None, ("group", "tensor")),
            P("expert", None, ("group", "tensor")),
            P("expert", None, ("group", "tensor")),
            P(None, None, ("group", "tensor")),
        ),
        check_vma=False,
    )
```

profile of v0, /device:TPU:6, one launch (start us, length us, event | category | flops | bytes accessed | tf_op | source)
XLA Modules:
  0.0 398.1 jit_solution(16670707907278651666)
XLA Ops:
  7.2 0.0 all-gather.3.cloned.1.call-start
  7.2 0.9 convert_element_type.52
  8.2 0.6 copy.106
  8.8 0.0 all-gather.3.cloned.1.call-update
  8.8 0.0 all-reduce.3.cloned.1.call-start
  8.8 0.7 convert_element_type.51
  9.5 90.1 %all-gather.3.cloned.1.call-done = bf16[3584,256]{1,0:T(8,128)(2,1)} async-done(((bf16[56,256]{1,0:T(8,128)(2,1)}), bf16[3584,256]{1,0:T(8,128)(2,1)}) %all-gather.3.cloned.1.call-update) | async-done | bytes 1835024 | tf_op jit(solution)/shard_map/all_gather | solution.py:41
  99.6 1.9 fusion.27
  101.5 0.1 fusion.12
  101.6 2.5 convolution_bitcast_fusion
  104.2 0.0 all-reduce.3.cloned.1.call-update
  104.2 0.7 copy-done.8
  104.8 0.1 copy.64
  104.9 0.1 reshape.85
  105.0 0.1 fusion.17
  105.1 0.2 reduce_window_sum.11
  105.3 0.2 select_reduce_fusion
  105.4 0.1 reduce_sum.30
  105.5 0.0 copy-done.3
  105.6 0.1 eq.57
  105.7 0.4 multiply_reduce_fusion
  106.0 0.1 reshape.87
  106.1 0.1 rsqrt.12
  106.2 0.1 convert_reduce_fusion
  106.4 0.7 convolution_convert_fusion
  107.0 1.5 reshape.88
  108.5 9.2 %all-to-all-start = ((bf16[64,1,4,3584]{3,2,1,0:T(4,128)(2,1)}), bf16[64,1,4,3584]{3,2,1,0:T(4,128)(2,1)}, u32[]{:S(2)}, u32[]{:S(2)}) async-start(bf16[64,1,4,3584]{3,2,1,0:T(4,128)(2,1)} %bitcast), calls=%async_computation | async-start | bytes 3670016 | tf_op jit(solution)/shard_map/all_to_all | solution.py:100
  117.7 0.0 all-gather.5.cloned.1.call-start
  117.8 1.3 dynamic-slice
  119.7 184.0 %all-reduce.3.cloned.1.call-done = f32[3584,256]{0,1:T(8,128)} async-done(((f32[3584,256]{0,1:T(8,128)}), f32[3584,256]{0,1:T(8,128)}) %all-reduce.3.cloned.1.call-update) | async-done | bytes 3670032
  303.7 1.0 constant_dynamic-slice_fusion
  304.7 0.1 copy.72
  304.9 0.1 fusion.24
  304.9 0.6 copy.78
  305.6 0.0 all-gather.5.cloned.1.call-update
  305.6 2.1 reshape.95
  307.7 0.1 copy.69
  307.8 0.1 mul.125
  307.9 2.7 fusion.3
  310.7 0.7 copy.68
  311.4 8.5 %all-to-all-start.1 = ((bf16[64,1,4,128]{3,2,1,0:T(4,128)(2,1)}), bf16[64,1,4,128]{3,2,1,0:T(4,128)(2,1)S(1)}, u32[]{:S(2)}, u32[]{:S(2)}) async-start(bf16[64,1,4,128]{3,2,1,0:T(4,128)(2,1)} %copy.68), calls=%async_computation.1 | async-start | bytes 131072 | tf_op jit(solution)/shard_map/all_to_all | solution.py:108
  319.9 12.3 %all-to-all-done.1 = bf16[64,1,4,128]{3,2,1,0:T(4,128)(2,1)S(1)} async-done(((bf16[64,1,4,128]{3,2,1,0:T(4,128)(2,1)}), bf16[64,1,4,128]{3,2,1,0:T(4,128)(2,1)S(1)}, u32[]{:S(2)}, u32[]{:S(2)}) %all-to-all-start.1) | async-done | bytes 65568 | tf_op jit(solution)/shard_map/all_to_all | solution.py:108
  332.2 0.8 fusion.7
  333.0 0.7 copy.79
  333.7 0.7 copy.80
  334.3 0.7 copy.81
  335.0 52.4 %all-gather.5.cloned.1.call-done = bf16[3584,2,128]{2,1,0:T(2,128)(2,1)} async-done(((bf16[56,2,128]{2,1,0:T(2,128)(2,1)}), bf16[3584,2,128]{2,1,0:T(2,128)(2,1)}) %all-gather.5.cloned.1.call-update) | async-done | bytes 1835024 | tf_op jit(solution)/shard_map/all_gather | solution.py:67
  387.3 4.2 %copy.109 = bf16[3584,2,128]{2,1,0:T(2,128)(2,1)} copy(bf16[3584,2,128]{2,1,0:T(2,128)(2,1)} %all-gather.5.cloned.1.call-done) | data formatting | bytes 3670016
  (26 shorter events, 0.1 us)
Async XLA Ops:
  7.2 92.4 %copy-start = (bf16[128,3584]{1,0:T(8,128)(2,1)S(1)}, bf16[128,3584]{1,0:T(8,128)(2,1)}, u32[]{:S(2)}) copy-start(bf16[128,3584]{1,0:T(8,128)(2,1)} %param.18) | copy-start | bytes 2752516
  7.2 94.4 %copy-start.6 = (bf16[128,128]{1,0:T(8,128)(2,1)S(1)}, bf16[128,128]{1,0:T(8,128)(2,1)}, u32[]{:S(2)}) copy-start(bf16[128,128]{1,0:T(8,128)(2,1)} %param.20) | copy-start | bytes 98308
  7.2 92.4 %all-gather.3.cloned.1.call-start = ((), (), s32[]{:S(2)}) async-start(), calls=%async_computation.2 | async-start | bytes 1863680 | tf_op jit(solution)/shard_map/all_gather | solution.py:41
  8.8 294.9 %all-reduce.3.cloned.1.call-start = ((), (), s32[]{:S(2)}) async-start(), calls=%async_computation.4 | async-start | bytes 7340032
  104.1 0.7 copy-start.8
  104.1 1.4 copy-start.3
  104.1 1.4 copy-start.10
  104.1 2.2 copy-start.7
  108.5 196.3 %copy-start.2 = (f32[56,2,128]{2,1,0:T(2,128)S(1)}, f32[56,2,128]{2,1,0:T(2,128)}, u32[]{:S(2)}) copy-start(f32[56,2,128]{2,1,0:T(2,128)} %param.21) | copy-start | bytes 172036
  108.5 196.3 %copy-start.4 = (f32[56,2,128]{2,1,0:T(2,128)S(1)}, f32[56,2,128]{2,1,0:T(2,128)}, u32[]{:S(2)}) copy-start(f32[56,2,128]{2,1,0:T(2,128)} %param.22) | copy-start | bytes 172036
  108.5 196.3 %copy-start.5 = (f32[56,2,128]{2,1,0:T(2,128)S(1)}, f32[56,2,128]{2,1,0:T(2,128)}, u32[]{:S(2)}) copy-start(f32[56,2,128]{2,1,0:T(2,128)} %param.23) | copy-start | bytes 172036
  108.5 197.1 %copy-start.1 = (bf16[1,3584,2,128]{3,2,1,0:T(2,128)(2,1)S(1)}, bf16[1,3584,2,128]{3,2,1,0:T(2,128)(2,1)}, u32[]{:S(2)}) copy-start(bf16[1,3584,2,128]{3,2,1,0:T(2,128)(2,1)} %param.17) | copy-start | bytes 5505028
  108.5 199.4 %all-to-all-start = ((bf16[64,1,4,3584]{3,2,1,0:T(4,128)(2,1)}), bf16[64,1,4,3584]{3,2,1,0:T(4,128)(2,1)}, u32[]{:S(2)}, u32[]{:S(2)}) async-start(bf16[64,1,4,3584]{3,2,1,0:T(4,128)(2,1)} %bitcast), calls=%async_computation | async-start | bytes 3670016 | tf_op jit(solution)/shard_map/all_to_all | solution.py:100
  117.7 269.6 %all-gather.5.cloned.1.call-start = ((), (), s32[]{:S(2)}) async-start(), calls=%async_computation.3 | async-start | bytes 1863680 | tf_op jit(solution)/shard_map/all_gather | solution.py:67
  305.6 2.1 copy-start.9
  311.4 20.8 %all-to-all-start.1 = ((bf16[64,1,4,128]{3,2,1,0:T(4,128)(2,1)}), bf16[64,1,4,128]{3,2,1,0:T(4,128)(2,1)S(1)}, u32[]{:S(2)}, u32[]{:S(2)}) async-start(bf16[64,1,4,128]{3,2,1,0:T(4,128)(2,1)} %copy.68), calls=%async_computation.1 | async-start | bytes 131072 | tf_op jit(solution)/shard_map/all_to_all | solution.py:108
Sparse Core Ops, SparseCore 0:
  11.7 87.8 all-gather.2
  104.3 199.3 all-reduce.2
  307.2 80.0 all-gather.4
where the time goes:
time: 399 us; the launch traced here: 398 us
  waiting for transfers between devices  339 us (85%)
  starting transfers between devices  17.8 us (4%)
  local copies, waits for them, and re-layouts  15.5 us (4%)
  between operations  14.6 us (4%)
  matrix products  8.98 us (2%)
    unnamed x4, waiting for transfers between devices  184 us
    all_gather x1, waiting for transfers between devices, shards(): lax.all_gather(weights_low, 'expert', axis=0, tiled=True)  90.1 us
    all_gather x1, waiting for transfers between devices, shards(): lax.all_gather(new_master.astype(jnp.bfloat16), 'expert', axis=0, tiled=T...  52.4 us
    all_to_all x1, waiting for transfers between devices, shards(): lax.all_to_all(activated_rows, 'expert', split_axis=0, concat_axis=0, til...  12.3 us
    unnamed x31, local copies, waits for them, and re-layouts  9.97 us
    all_to_all x1, starting transfers between devices, shards(): lax.all_to_all(outgoing, 'expert', split_axis=0, concat_axis=0, tiled=True)  9.18 us
    all_to_all x1, starting transfers between devices, shards(): lax.all_to_all(activated_rows, 'expert', split_axis=0, concat_axis=0, til...  8.53 us
  transfers between devices with their start and end apart: 5, of which 4 were waited for; matrix products, arithmetic and copies ran while one was open for 4% of the time, Pallas kernels for 0%

commit v1 on v0

v1 whole, which is shorter than its diff:
```python
import jax
import jax.numpy as jnp
from jax import lax
from jax.sharding import Mesh, PartitionSpec as P

EXPERTS = 64
TOP = 8
BEAMS = 4
CAP = 4

beta_one = 0.9
beta_two = 0.95
learn_rate = 0.01
decay_rate = 0.1
epsilon = 1e-08
norm_epsilon = 1e-06
adam_step = 10.0

ROW = ("y", "z")
COLUMN = ("xl", "core", "xh")
weight_scale = 2.0**19
fresh_scale = 2.0**16


def to_half(values, scale):
    return (values.astype(jnp.bfloat16).astype(jnp.float32) * scale).astype(jnp.float16)


def from_half(values, scale):
    return (values.astype(jnp.float32) * (1.0 / scale)).astype(jnp.bfloat16)


def gather_by_exchange(block, axis):
    count = lax.axis_size(axis)
    return lax.all_to_all(
        jnp.broadcast_to(block[None], (count,) + block.shape), axis, 0, 0, tiled=True
    )


def shards(
    hidden_rows,
    parent_beam,
    norm_gain,
    route_ids,
    route_weight,
    expert_weight,
    learn_tokens,
    learn_live,
    cotangent,
    master,
    first_moment,
    second_moment,
):
    hid_local = master.shape[2]
    own_rows = master.shape[0]
    wide = 2 * hid_local
    n_y, n_z = lax.axis_size("y"), lax.axis_size("z")
    n_x = lax.axis_size(COLUMN)

    token_slice = lax.all_to_all(learn_tokens, "y", split_axis=1, concat_axis=0, tiled=True)

    rows_dev, width = hidden_rows.shape
    grouped = hidden_rows.reshape(rows_dev // BEAMS, BEAMS, width)
    selector = (
        parent_beam.reshape(rows_dev // BEAMS, BEAMS, 1)
        == jnp.arange(BEAMS, dtype=jnp.int32)[None, None, :]
    ).astype(jnp.bfloat16)
    reordered = jnp.einsum(
        "rbc,rcd->rbd", selector, grouped, preferred_element_type=jnp.float32
    ).reshape(rows_dev, width)
    mean_square = jnp.mean(reordered * reordered, axis=1, keepdims=True)
    normed = (reordered * lax.rsqrt(mean_square + norm_epsilon) * norm_gain[None, :]).astype(
        jnp.bfloat16
    )
    flat_ids = route_ids.reshape(rows_dev * TOP)
    onehot = (flat_ids[:, None] == jnp.arange(EXPERTS, dtype=jnp.int32)[None, :]).astype(jnp.int32)
    earlier = jnp.cumsum(onehot, axis=0) - onehot
    position = jnp.sum(earlier * onehot, axis=1)
    slot_index = flat_ids * CAP + position
    slot_table = (
        slot_index[:, None] == jnp.arange(EXPERTS * CAP, dtype=jnp.int32)[None, :]
    ).astype(jnp.float32)
    row_table = slot_table.reshape(rows_dev, TOP, EXPERTS * CAP).sum(axis=1).astype(jnp.bfloat16)
    share = width // n_x
    normed_share = lax.dynamic_index_in_dim(
        normed.reshape(rows_dev, n_x, share), lax.axis_index(COLUMN), axis=1, keepdims=False
    )
    outgoing = lax.dot_general(
        row_table, normed_share, (((0,), (0,)), ((), ())), preferred_element_type=jnp.float32
    ).astype(jnp.bfloat16)
    arrived = lax.all_to_all(
        outgoing.reshape(n_y * n_z, CAP, share), ROW, split_axis=0, concat_axis=0, tiled=True
    )
    arrived = gather_by_exchange(arrived.reshape(EXPERTS * CAP, share), COLUMN)
    arrived = arrived.reshape(n_x, EXPERTS * CAP, share)

    weights = lax.all_gather(
        to_half(master, weight_scale).reshape(own_rows, wide), ROW, axis=0, tiled=True
    )
    projected = jnp.dot(
        learn_tokens, from_half(weights, weight_scale), preferred_element_type=jnp.float32
    )
    gate_pre = projected[:, :hid_local]
    up_pre = projected[:, hid_local:]
    sigmoid_gate = jax.nn.sigmoid(gate_pre)
    upstream = cotangent.astype(jnp.float32) * learn_live.astype(jnp.float32)[:, None]
    slope = sigmoid_gate * (1.0 + gate_pre * (1.0 - sigmoid_gate))
    grad_pre = jnp.concatenate(
        [upstream * up_pre * slope, upstream * gate_pre * sigmoid_gate], axis=1
    ).astype(jnp.bfloat16)

    grad_all = gather_by_exchange(grad_pre, "y").reshape(token_slice.shape[0], wide)
    partial = lax.dot_general(
        token_slice, grad_all, (((0,), (0,)), ((), ())), preferred_element_type=jnp.float32
    ).astype(jnp.bfloat16)
    parts = lax.all_to_all(
        partial.reshape(n_z, own_rows, wide), "z", split_axis=0, concat_axis=0, tiled=True
    )
    gradient = jnp.sum(parts.astype(jnp.float32), axis=0).reshape(master.shape)
    new_first = beta_one * first_moment + (1.0 - beta_one) * gradient
    new_second = beta_two * second_moment + (1.0 - beta_two) * gradient * gradient
    correct_one = 1.0 - beta_one**adam_step
    correct_two = 1.0 - beta_two**adam_step
    update = new_first / correct_one / (jnp.sqrt(new_second / correct_two) + epsilon)
    new_master = master - learn_rate * (update + decay_rate * master)
    fresh_rows = gather_by_exchange(to_half(new_master, fresh_scale), "z")
    fresh_rows = fresh_rows.reshape(n_z * own_rows, 2, hid_local)
    fresh = from_half(lax.all_gather(fresh_rows, "y", axis=0, tiled=True), fresh_scale)

    local_weight = expert_weight.reshape(n_x, share, wide)
    projected_rows = jnp.einsum(
        "jsd,jdk->sk", arrived, local_weight, preferred_element_type=jnp.float32
    )
    gate_rows = projected_rows[:, :hid_local]
    activated_rows = (
        gate_rows * jax.nn.sigmoid(gate_rows) * projected_rows[:, hid_local:]
    ).astype(jnp.bfloat16)
    returned = lax.all_to_all(
        activated_rows.reshape(n_y * n_z, CAP, hid_local), ROW, split_axis=0, concat_axis=0, tiled=True
    )
    back_slots = returned.reshape(EXPERTS * CAP, hid_local)
    picked = jnp.dot(
        slot_table.astype(jnp.bfloat16), back_slots, preferred_element_type=jnp.float32
    )
    rolled = (
        (picked * route_weight.reshape(rows_dev * TOP, 1))
        .astype(jnp.bfloat16)
        .reshape(rows_dev, TOP, hid_local)
    )
    return (rolled, new_master, new_first, new_second, fresh)


def solution(mesh):
    fine = Mesh(mesh.devices.reshape(2, 2, 8, 8, 2), ("xl", "core", "y", "z", "xh"))
    placed = (
        P(ROW, None),
        P(ROW),
        P(),
        P(ROW, None),
        P(ROW, None),
        P(ROW, None, None, COLUMN),
        P(ROW, None),
        P(ROW),
        P(ROW, COLUMN),
        P(ROW, None, COLUMN),
        P(ROW, None, COLUMN),
        P(ROW, None, COLUMN),
    )
    return jax.shard_map(
        shards,
        mesh=fine,
        in_specs=placed,
        out_specs=(
            P(ROW, None, COLUMN),
            P(ROW, None, COLUMN),
            P(ROW, None, COLUMN),
            P(ROW, None, COLUMN),
            P(None, None, COLUMN),
        ),
        check_vma=False,
    )
```

time: 399 us -> 241 us (0.60)
  waiting for transfers between devices: 339 us -> 98.1 us
  blocking collectives: 0 us -> 87.5 us
  starting transfers between devices: 17.8 us -> 31.9 us
  between operations: 14.6 us -> 1 us
  local copies, waits for them, and re-layouts: 15.5 us -> 8.73 us
    unnamed x4 -> x0, waiting for transfers between devices: 184 us -> none
    all_gather x2 -> x0, waiting for transfers between devices: 142 us -> none  [the longest x1 90.1 us: shards(): lax.all_gather(weights_low, 'expert', axis=0, tiled=True)]
    all_gather x0 -> x2, blocking collectives: none -> 87.5 us  [the longest x1 58.9 us: shards(): lax.all_gather(to_half(master, weight_scale).reshape(own_rows, wide), ROW...]
    all_to_all x2 -> x7, waiting for transfers between devices: 12.3 us -> 98.1 us  [the longest x3 47.2 us: gather_by_exchange(): lax.all_to_all(jnp.broadcast_to(block[None], (count,) + block.shape), axi...]
    all_to_all x2 -> x7, starting transfers between devices: 17.7 us -> 31.9 us  [the longest x3 15.7 us: gather_by_exchange(): lax.all_to_all(jnp.broadcast_to(block[None], (count,) + block.shape), axi...]
    unnamed x31 -> x29, local copies, waits for them, and re-layouts: 9.97 us -> 1.6 us
  transfers between devices with their start and end apart: 5 -> 7, of which waited for: 4 -> 7; matrix products, arithmetic and copies ran while one was open for 4% -> 4% of each run, Pallas kernels for 0% -> 0%
where the time goes in v1:
time: 241 us; the launch traced here: 239 us
  waiting for transfers between devices  98.1 us (41%)
  blocking collectives  87.5 us (36%)
  starting transfers between devices  31.9 us (13%)
  local copies, waits for them, and re-layouts  8.73 us (4%)
  matrix products  6.02 us (2%)
  other arithmetic  5.93 us (2%)
    all_gather x1, blocking collectives, shards(): lax.all_gather(to_half(master, weight_scale).reshape(own_rows, wide), ROW...  58.9 us
    all_to_all x3, waiting for transfers between devices, gather_by_exchange(): lax.all_to_all(jnp.broadcast_to(block[None], (count,) + block.shape), axi...  47.2 us
    all_gather x1, blocking collectives, shards(): lax.all_gather(fresh_rows, 'y', axis=0, tiled=True)  28.6 us
    all_to_all x1, waiting for transfers between devices, shards(): lax.all_to_all(learn_tokens, 'y', split_axis=1, concat_axis=0, tiled=True)  17.2 us
    all_to_all x3, starting transfers between devices, gather_by_exchange(): lax.all_to_all(jnp.broadcast_to(block[None], (count,) + block.shape), axi...  15.7 us
    all_to_all x1, waiting for transfers between devices, shards(): lax.all_to_all(outgoing.reshape(n_y * n_z, CAP, share), ROW, split_axis=0...  12.6 us
    all_to_all x1, waiting for transfers between devices, shards(): lax.all_to_all(activated_rows.reshape(n_y * n_z, CAP, hid_local), ROW, sp...  11.4 us
    all_to_all x1, waiting for transfers between devices, shards(): lax.all_to_all(partial.reshape(n_z, own_rows, wide), 'z', split_axis=0, c...  9.76 us
  transfers between devices with their start and end apart: 7, of which 7 were waited for; matrix products, arithmetic and copies ran while one was open for 4% of the time, Pallas kernels for 0%

profile of v1, /device:TPU:6, one launch (start us, length us, event | category | flops | bytes accessed | tf_op | source)
XLA Modules:
  0.0 239.2 jit_solution(3695238069259693284)
XLA Ops:
  0.7 0.9 multiply_convert_fusion.7
  1.6 58.9 %all-gather.2 = f16[3584,256]{1,0:T(8,128)(2,1)S(1)} all-gather(f16[56,256]{1,0:T(8,128)(2,1)S(1)} %bitcast.35), channel_id=1, replica_groups=mesh['xl'=2,'core'=2,'y'=8,'z'=8,'xh'=2] {'y','z'}, dimensions={0}, use_global_device_ids=true | all-gather | bytes 1863680 | tf_op jit(solution)/shard_map/all_gather | solution.py:97
  60.5 0.1 copy.47
  60.7 0.7 fusion.3
  61.4 0.1 copy.48
  61.5 0.8 broadcast_in_dim.10
  62.4 7.4 %all-to-all-start.3 = ((bf16[8,128,256]{2,1,0:T(8,128)(2,1)}), bf16[8,128,256]{2,1,0:T(8,128)(2,1)S(1)}, u32[]{:S(2)}, u32[]{:S(2)}) async-start(bf16[8,128,256]{2,1,0:T(8,128)(2,1)} %broadcast_in_dim.10), calls=%async_computation.3 | async-start | bytes 1048576 | tf_op jit(solution)/shard_map/all_to_all | solution.py:35
  69.8 1.3 copy.49
  71.1 18.5 %all-to-all-done.3 = bf16[8,128,256]{2,1,0:T(8,128)(2,1)S(1)} async-done(((bf16[8,128,256]{2,1,0:T(8,128)(2,1)}), bf16[8,128,256]{2,1,0:T(8,128)(2,1)S(1)}, u32[]{:S(2)}, u32[]{:S(2)}) %all-to-all-start.3) | async-done | bytes 524320 | tf_op jit(solution)/shard_map/all_to_all | solution.py:35
  89.5 3.6 %all-to-all-start.4 = ((bf16[128,8,448]{0,2,1:T(8,128)(2,1)}), bf16[128,8,448]{0,2,1:T(8,128)(2,1)S(1)}, u32[]{:S(2)}, u32[]{:S(2)}) async-start(bf16[128,8,448]{0,2,1:T(8,128)(2,1)} %bitcast.6), calls=%async_computation.4 | async-start | bytes 1835008 | tf_op jit(solution)/shard_map/all_to_all | solution.py:60
  93.1 0.1 eq.57
  93.2 0.4 multiply_reduce_fusion
  93.6 0.2 reshape.123
  93.8 0.1 mul.155
  93.9 0.1 reshape.121
  94.0 0.1 fusion.11
  94.1 0.2 reduce_window_sum.11
  94.3 0.2 select_reduce_fusion
  94.4 0.1 reduce_sum.39
  94.6 0.1 rsqrt.12
  94.7 0.1 convert_reduce_fusion.1
  94.8 0.3 convolution_convert_fusion
  95.2 0.1 copy.44
  95.3 0.8 reshape.124
  96.1 17.2 %all-to-all-done.4 = bf16[128,8,448]{0,2,1:T(8,128)(2,1)S(1)} async-done(((bf16[128,8,448]{0,2,1:T(8,128)(2,1)}), bf16[128,8,448]{0,2,1:T(8,128)(2,1)S(1)}, u32[]{:S(2)}, u32[]{:S(2)}) %all-to-all-start.4) | async-done | bytes 917536 | tf_op jit(solution)/shard_map/all_to_all | solution.py:60
  113.3 4.6 %all-to-all-start = ((bf16[64,4,448]{2,1,0:T(4,128)(2,1)}), bf16[64,4,448]{2,1,0:T(4,128)(2,1)S(1)}, u32[]{:S(2)}, u32[]{:S(2)}) async-start(bf16[64,4,448]{2,1,0:T(4,128)(2,1)} %reshape.124), calls=%async_computation | async-start | bytes 524288 | tf_op jit(solution)/shard_map/all_to_all | solution.py:91
  117.9 1.1 fusion.2
  119.0 12.6 %all-to-all-done = bf16[64,4,448]{2,1,0:T(4,128)(2,1)S(1)} async-done(((bf16[64,4,448]{2,1,0:T(4,128)(2,1)}), bf16[64,4,448]{2,1,0:T(4,128)(2,1)S(1)}, u32[]{:S(2)}, u32[]{:S(2)}) %all-to-all-start) | async-done | bytes 229408 | tf_op jit(solution)/shard_map/all_to_all | solution.py:91
  131.6 3.4 %all-to-all-start.5 = ((bf16[8,56,256]{2,1,0:T(8,128)(2,1)}), bf16[8,56,256]{2,1,0:T(8,128)(2,1)S(1)}, u32[]{:S(2)}, u32[]{:S(2)}) async-start(bf16[8,56,256]{2,1,0:T(8,128)(2,1)} %bitcast.10), calls=%async_computation.5 | async-start | bytes 458752 | tf_op jit(solution)/shard_map/all_to_all | solution.py:116
  135.0 0.1 broadcast_in_dim.8
  135.1 0.1 copy.45
  135.3 9.8 %all-to-all-done.5 = bf16[8,56,256]{2,1,0:T(8,128)(2,1)S(1)} async-done(((bf16[8,56,256]{2,1,0:T(8,128)(2,1)}), bf16[8,56,256]{2,1,0:T(8,128)(2,1)S(1)}, u32[]{:S(2)}, u32[]{:S(2)}) %all-to-all-start.5) | async-done | bytes 229408 | tf_op jit(solution)/shard_map/all_to_all | solution.py:116
  145.0 1.3 broadcast_in_dim.9
  146.4 4.9 %all-to-all-start.1 = ((bf16[8,256,448]{1,2,0:T(8,128)(2,1)}), bf16[8,256,448]{1,2,0:T(8,128)(2,1)}, u32[]{:S(2)}, u32[]{:S(2)}) async-start(bf16[8,256,448]{1,2,0:T(8,128)(2,1)} %broadcast_in_dim.9), calls=%async_computation.1 | async-start | bytes 3670016 | tf_op jit(solution)/shard_map/all_to_all | solution.py:35
  151.3 2.1 reshape.125
  153.5 19.7 %all-to-all-done.1 = bf16[8,256,448]{1,2,0:T(8,128)(2,1)} async-done(((bf16[8,256,448]{1,2,0:T(8,128)(2,1)}), bf16[8,256,448]{1,2,0:T(8,128)(2,1)}, u32[]{:S(2)}, u32[]{:S(2)}) %all-to-all-start.1) | async-done | bytes 1835040 | tf_op jit(solution)/shard_map/all_to_all | solution.py:35
  173.2 2.7 %convolution_bitcast_fusion.1 = f32[256,256]{1,0:T(8,128)S(1)} fusion(bf16[8,256,448]{1,2,0:T(8,128)(2,1)} %all-to-all-done.1, bf16[8,448,256]{2,1,0:T(8,128)(2,1)} %reshape.125), kind=kOutput, calls=%fused_computation.7 | convolution fusion | flops 469762048 | bytes 3932160 | tf_op jit(solution)/shard_map/jsd,jdk->sk/dot_general | solution.py:131
  175.9 0.7 fusion.7
  176.6 4.6 %all-to-all-start.2 = ((bf16[64,4,128]{2,1,0:T(4,128)(2,1)}), bf16[64,4,128]{2,1,0:T(4,128)(2,1)S(1)}, u32[]{:S(2)}, u32[]{:S(2)}) async-start(bf16[64,4,128]{2,1,0:T(4,128)(2,1)} %bitcast.2), calls=%async_computation.2 | async-start | bytes 131072 | tf_op jit(solution)/shard_map/all_to_all | solution.py:138
  181.3 0.9 multiply_convert_fusion.6
  182.1 11.4 %all-to-all-done.2 = bf16[64,4,128]{2,1,0:T(4,128)(2,1)S(1)} async-done(((bf16[64,4,128]{2,1,0:T(4,128)(2,1)}), bf16[64,4,128]{2,1,0:T(4,128)(2,1)S(1)}, u32[]{:S(2)}, u32[]{:S(2)}) %all-to-all-start.2) | async-done | bytes 65568 | tf_op jit(solution)/shard_map/all_to_all | solution.py:138
  193.5 0.8 broadcast_in_dim.11
  194.3 3.4 %all-to-all-start.6 = ((f16[8,56,2,128]{3,2,1,0:T(2,128)(2,1)}), f16[8,56,2,128]{3,2,1,0:T(2,128)(2,1)S(1)}, u32[]{:S(2)}, u32[]{:S(2)}) async-start(f16[8,56,2,128]{3,2,1,0:T(2,128)(2,1)} %broadcast_in_dim.11), calls=%async_computation.6 | async-start | bytes 458752 | tf_op jit(solution)/shard_map/all_to_all | solution.py:35
  197.8 0.1 mul.162
  197.9 0.8 fusion.5
  198.7 9.0 %all-to-all-done.6 = f16[8,56,2,128]{3,2,1,0:T(2,128)(2,1)S(1)} async-done(((f16[8,56,2,128]{3,2,1,0:T(2,128)(2,1)}), f16[8,56,2,128]{3,2,1,0:T(2,128)(2,1)S(1)}, u32[]{:S(2)}, u32[]{:S(2)}) %all-to-all-start.6) | async-done | bytes 229408 | tf_op jit(solution)/shard_map/all_to_all | solution.py:35
  207.8 28.6 %all-gather.3 = f16[3584,2,128]{2,1,0:T(2,128)(2,1)S(1)} all-gather(f16[448,2,128]{2,1,0:T(2,128)(2,1)S(1)} %bitcast.34), channel_id=1, replica_groups=mesh['xl'=2,'core'=2,'y'=8,'z'=8,'xh'=2] {'y'}, dimensions={0}, use_global_device_ids=true | all-gather | bytes 2064384 | tf_op jit(solution)/shard_map/all_gather | solution.py:128
  236.4 2.8 %multiply_convert_fusion = bf16[3584,2,128]{2,1,0:T(2,128)(2,1)} fusion(f16[3584,2,128]{2,1,0:T(2,128)(2,1)S(1)} %all-gather.3), kind=kLoop, calls=%fused_computation | loop fusion | flops 2752512 | bytes 3670016 | tf_op jit(solution)/shard_map/convert_element_type | solution.py:30
  (38 shorter events, 0.4 us)
Async XLA Ops:
  0.6 59.9 %copy-start.6 = (bf16[128,128]{1,0:T(8,128)(2,1)S(1)}, bf16[128,128]{1,0:T(8,128)(2,1)}, u32[]{:S(2)}) copy-start(bf16[128,128]{1,0:T(8,128)(2,1)} %param.20) | copy-start | bytes 98308
  0.6 60.0 %copy-start.11 = (s32[128]{0:T(128)S(1)}, s32[128]{0:T(128)}, u32[]{:S(2)}) copy-start(s32[128]{0:T(128)} %param.19) | copy-start | bytes 1540
  0.7 60.0 %copy-start.1 = (bf16[128,3584]{1,0:T(8,128)(2,1)S(1)}, bf16[128,3584]{1,0:T(8,128)(2,1)}, u32[]{:S(2)}) copy-start(bf16[128,3584]{1,0:T(8,128)(2,1)} %param.18) | copy-start | bytes 2752516
  62.4 27.2 %all-to-all-start.3 = ((bf16[8,128,256]{2,1,0:T(8,128)(2,1)}), bf16[8,128,256]{2,1,0:T(8,128)(2,1)S(1)}, u32[]{:S(2)}, u32[]{:S(2)}) async-start(bf16[8,128,256]{2,1,0:T(8,128)(2,1)} %broadcast_in_dim.10), calls=%async_computation.3 | async-start | bytes 1048576 | tf_op jit(solution)/shard_map/all_to_all | solution.py:35
  69.8 23.3 %copy-start.3 = (bf16[16,3584]{1,0:T(8,128)(2,1)S(1)}, bf16[16,3584]{1,0:T(8,128)(2,1)}, u32[]{:S(2)}) copy-start(bf16[16,3584]{1,0:T(8,128)(2,1)} %param.12) | copy-start | bytes 344068
  69.8 23.4 %copy-start.10 = (s32[16]{0:T(128)S(1)}, s32[16]{0:T(128)}, u32[]{:S(2)}) copy-start(s32[16]{0:T(128)} %param.13) | copy-start | bytes 196
  71.1 22.7 %copy-start.7 = (f32[3584]{0:T(1024)S(1)}, f32[3584]{0:T(1024)}, u32[]{:S(2)}) copy-start(f32[3584]{0:T(1024)} %param.14) | copy-start | bytes 43012
  71.1 22.8 %copy-start.8 = (s32[16,8]{0,1:T(8,128)S(1)}, s32[16,8]{0,1:T(8,128)}, u32[]{:S(2)}) copy-start(s32[16,8]{0,1:T(8,128)} %param.15) | copy-start | bytes 1540
  89.5 23.8 %all-to-all-start.4 = ((bf16[128,8,448]{0,2,1:T(8,128)(2,1)}), bf16[128,8,448]{0,2,1:T(8,128)(2,1)S(1)}, u32[]{:S(2)}, u32[]{:S(2)}) async-start(bf16[128,8,448]{0,2,1:T(8,128)(2,1)} %bitcast.6), calls=%async_computation.4 | async-start | bytes 1835008 | tf_op jit(solution)/shard_map/all_to_all | solution.py:60
  113.3 18.3 %all-to-all-start = ((bf16[64,4,448]{2,1,0:T(4,128)(2,1)}), bf16[64,4,448]{2,1,0:T(4,128)(2,1)S(1)}, u32[]{:S(2)}, u32[]{:S(2)}) async-start(bf16[64,4,448]{2,1,0:T(4,128)(2,1)} %reshape.124), calls=%async_computation | async-start | bytes 524288 | tf_op jit(solution)/shard_map/all_to_all | solution.py:91
  131.6 13.4 %all-to-all-start.5 = ((bf16[8,56,256]{2,1,0:T(8,128)(2,1)}), bf16[8,56,256]{2,1,0:T(8,128)(2,1)S(1)}, u32[]{:S(2)}, u32[]{:S(2)}) async-start(bf16[8,56,256]{2,1,0:T(8,128)(2,1)} %bitcast.10), calls=%async_computation.5 | async-start | bytes 458752 | tf_op jit(solution)/shard_map/all_to_all | solution.py:116
  146.4 4.9 %copy-start = (bf16[1,3584,2,128]{3,2,1,0:T(2,128)(2,1)S(1)}, bf16[1,3584,2,128]{3,2,1,0:T(2,128)(2,1)}, u32[]{:S(2)}) copy-start(bf16[1,3584,2,128]{3,2,1,0:T(2,128)(2,1)} %param.17) | copy-start | bytes 5505028
  146.4 26.8 %all-to-all-start.1 = ((bf16[8,256,448]{1,2,0:T(8,128)(2,1)}), bf16[8,256,448]{1,2,0:T(8,128)(2,1)}, u32[]{:S(2)}, u32[]{:S(2)}) async-start(bf16[8,256,448]{1,2,0:T(8,128)(2,1)} %broadcast_in_dim.9), calls=%async_computation.1 | async-start | bytes 3670016 | tf_op jit(solution)/shard_map/all_to_all | solution.py:35
  153.5 27.8 %copy-start.2 = (f32[56,2,128]{2,1,0:T(2,128)S(1)}, f32[56,2,128]{2,1,0:T(2,128)}, u32[]{:S(2)}) copy-start(f32[56,2,128]{2,1,0:T(2,128)} %param.21) | copy-start | bytes 172036
  153.5 27.8 %copy-start.4 = (f32[56,2,128]{2,1,0:T(2,128)S(1)}, f32[56,2,128]{2,1,0:T(2,128)}, u32[]{:S(2)}) copy-start(f32[56,2,128]{2,1,0:T(2,128)} %param.22) | copy-start | bytes 172036
  153.5 27.8 %copy-start.5 = (f32[56,2,128]{2,1,0:T(2,128)S(1)}, f32[56,2,128]{2,1,0:T(2,128)}, u32[]{:S(2)}) copy-start(f32[56,2,128]{2,1,0:T(2,128)} %param.23) | copy-start | bytes 172036
  153.5 44.2 %copy-start.9 = (f32[16,8]{0,1:T(8,128)S(1)}, f32[16,8]{0,1:T(8,128)}, u32[]{:S(2)}) copy-start(f32[16,8]{0,1:T(8,128)} %param.16) | copy-start | bytes 1540
  176.6 16.9 %all-to-all-start.2 = ((bf16[64,4,128]{2,1,0:T(4,128)(2,1)}), bf16[64,4,128]{2,1,0:T(4,128)(2,1)S(1)}, u32[]{:S(2)}, u32[]{:S(2)}) async-start(bf16[64,4,128]{2,1,0:T(4,128)(2,1)} %bitcast.2), calls=%async_computation.2 | async-start | bytes 131072 | tf_op jit(solution)/shard_map/all_to_all | solution.py:138
  194.3 13.4 %all-to-all-start.6 = ((f16[8,56,2,128]{3,2,1,0:T(2,128)(2,1)}), f16[8,56,2,128]{3,2,1,0:T(2,128)(2,1)S(1)}, u32[]{:S(2)}, u32[]{:S(2)}) async-start(f16[8,56,2,128]{3,2,1,0:T(2,128)(2,1)} %broadcast_in_dim.11), calls=%async_computation.6 | async-start | bytes 458752 | tf_op jit(solution)/shard_map/all_to_all | solution.py:35

commit v2 on v1

--- a/solution.py
+++ b/solution.py
@@ -18,12 +18,14 @@
 
 ROW = ("y", "z")
 COLUMN = ("xl", "core", "xh")
-weight_scale = 2.0**19
+SWAP = [(0, 1), (1, 0)]
+pre_scale = 2.0**7
+grad_scale = 2.0**-7
 fresh_scale = 2.0**16
 
 
 def to_half(values, scale):
-    return (values.astype(jnp.bfloat16).astype(jnp.float32) * scale).astype(jnp.float16)
+    return (values.astype(jnp.float32) * scale).astype(jnp.float16)
 
 
 def from_half(values, scale):
@@ -57,7 +59,31 @@
     n_y, n_z = lax.axis_size("y"), lax.axis_size("z")
     n_x = lax.axis_size(COLUMN)
 
-    token_slice = lax.all_to_all(learn_tokens, "y", split_axis=1, concat_axis=0, tiled=True)
+    half = learn_tokens.shape[0] // 2
+    core = lax.axis_index("core")
+
+    def own_first(block):
+        return jnp.concatenate(
+            [
+                lax.dynamic_slice_in_dim(block, core * half, half, 0),
+                lax.dynamic_slice_in_dim(block, (1 - core) * half, half, 0),
+            ],
+            axis=0,
+        )
+
+    own_slice = lax.all_to_all(
+        lax.dynamic_slice_in_dim(learn_tokens, core * half, half, 0),
+        "y",
+        split_axis=1,
+        concat_axis=0,
+        tiled=True,
+    )
+    weights = lax.all_gather(
+        master.astype(jnp.bfloat16).reshape(own_rows, wide), "z", axis=0, tiled=True
+    )
+    own_slice, weights = lax.optimization_barrier((own_slice, weights))
+    other_slice = lax.ppermute(own_slice, "core", SWAP)
+    token_slice = jnp.concatenate([own_slice, other_slice], axis=0)
 
     rows_dev, width = hidden_rows.shape
     grouped = hidden_rows.reshape(rows_dev // BEAMS, BEAMS, width)
@@ -88,56 +114,82 @@
     outgoing = lax.dot_general(
         row_table, normed_share, (((0,), (0,)), ((), ())), preferred_element_type=jnp.float32
     ).astype(jnp.bfloat16)
+    outgoing, own_slice = lax.optimization_barrier((outgoing, own_slice))
     arrived = lax.all_to_all(
         outgoing.reshape(n_y * n_z, CAP, share), ROW, split_axis=0, concat_axis=0, tiled=True
-    )
-    arrived = gather_by_exchange(arrived.reshape(EXPERTS * CAP, share), COLUMN)
-    arrived = arrived.reshape(n_x, EXPERTS * CAP, share)
-
-    weights = lax.all_gather(
-        to_half(master, weight_scale).reshape(own_rows, wide), ROW, axis=0, tiled=True
-    )
-    projected = jnp.dot(
-        learn_tokens, from_half(weights, weight_scale), preferred_element_type=jnp.float32
+    ).reshape(EXPERTS * CAP, share)
+
+    partial_pre = to_half(
+        jnp.dot(token_slice, weights, preferred_element_type=jnp.float32), pre_scale
+    )
+    partial_pre = partial_pre.reshape(2, n_y, half, wide).transpose(1, 0, 2, 3)
+    partial_pre, arrived = lax.optimization_barrier((partial_pre, arrived))
+    pre_parts = lax.all_to_all(partial_pre, "y", split_axis=0, concat_axis=0, tiled=True)
+    projected = jnp.sum(pre_parts.astype(jnp.float32), axis=0).reshape(2 * half, wide) * (
+        1.0 / pre_scale
     )
     gate_pre = projected[:, :hid_local]
     up_pre = projected[:, hid_local:]
     sigmoid_gate = jax.nn.sigmoid(gate_pre)
-    upstream = cotangent.astype(jnp.float32) * learn_live.astype(jnp.float32)[:, None]
+    upstream = own_first(cotangent).astype(jnp.float32) * own_first(
+        learn_live.astype(jnp.float32)[:, None]
+    )
     slope = sigmoid_gate * (1.0 + gate_pre * (1.0 - sigmoid_gate))
     grad_pre = jnp.concatenate(
         [upstream * up_pre * slope, upstream * gate_pre * sigmoid_gate], axis=1
     ).astype(jnp.bfloat16)
 
-    grad_all = gather_by_exchange(grad_pre, "y").reshape(token_slice.shape[0], wide)
-    partial = lax.dot_general(
-        token_slice, grad_all, (((0,), (0,)), ((), ())), preferred_element_type=jnp.float32
-    ).astype(jnp.bfloat16)
+    pieces = [arrived] + [
+        lax.ppermute(arrived, ("xl", "xh"), [(i, i ^ k) for i in range(4)]) for k in (1, 2, 3)
+    ]
+    pieces = jnp.stack(pieces)
+    pieces = jnp.stack([pieces, lax.ppermute(pieces, "core", SWAP)])
+    local_weight = expert_weight.reshape(2, 2, 2, share, wide)
+    for place, axis in enumerate(COLUMN):
+        local_weight = jnp.where(
+            lax.axis_index(axis) == 1, jnp.flip(local_weight, place), local_weight
+        )
+    local_weight = local_weight.transpose(1, 0, 2, 3, 4)
+
+    grad_all = gather_by_exchange(grad_pre, "y").reshape(n_y, 2, half, wide)
+    grad_all = grad_all.transpose(1, 0, 2, 3).reshape(token_slice.shape[0], wide)
+    partial = to_half(
+        lax.dot_general(
+            token_slice, grad_all, (((0,), (0,)), ((), ())), preferred_element_type=jnp.float32
+        ),
+        grad_scale,
+    )
     parts = lax.all_to_all(
         partial.reshape(n_z, own_rows, wide), "z", split_axis=0, concat_axis=0, tiled=True
     )
-    gradient = jnp.sum(parts.astype(jnp.float32), axis=0).reshape(master.shape)
+    gradient = (jnp.sum(parts.astype(jnp.float32), axis=0) * (1.0 / grad_scale)).reshape(
+        master.shape
+    )
     new_first = beta_one * first_moment + (1.0 - beta_one) * gradient
     new_second = beta_two * second_moment + (1.0 - beta_two) * gradient * gradient
     correct_one = 1.0 - beta_one**adam_step
     correct_two = 1.0 - beta_two**adam_step
     update = new_first / correct_one / (jnp.sqrt(new_second / correct_two) + epsilon)
     new_master = master - learn_rate * (update + decay_rate * master)
-    fresh_rows = gather_by_exchange(to_half(new_master, fresh_scale), "z")
-    fresh_rows = fresh_rows.reshape(n_z * own_rows, 2, hid_local)
-    fresh = from_half(lax.all_gather(fresh_rows, "y", axis=0, tiled=True), fresh_scale)
-
-    local_weight = expert_weight.reshape(n_x, share, wide)
+    fresh_rows = to_half(new_master.astype(jnp.bfloat16), fresh_scale)
+
     projected_rows = jnp.einsum(
-        "jsd,jdk->sk", arrived, local_weight, preferred_element_type=jnp.float32
+        "cjsd,cjdk->sk",
+        pieces,
+        local_weight.reshape(2, 4, share, wide),
+        preferred_element_type=jnp.float32,
     )
     gate_rows = projected_rows[:, :hid_local]
     activated_rows = (
         gate_rows * jax.nn.sigmoid(gate_rows) * projected_rows[:, hid_local:]
     ).astype(jnp.bfloat16)
+    activated_rows, fresh_rows = lax.optimization_barrier((activated_rows, fresh_rows))
     returned = lax.all_to_all(
         activated_rows.reshape(n_y * n_z, CAP, hid_local), ROW, split_axis=0, concat_axis=0, tiled=True
     )
+    fresh = lax.all_gather(fresh_rows, ROW, axis=0, tiled=True)
+    returned, fresh = lax.optimization_barrier((returned, fresh))
+    fresh = from_half(fresh, fresh_scale)
     back_slots = returned.reshape(EXPERTS * CAP, hid_local)
     picked = jnp.dot(
         slot_table.astype(jnp.bfloat16), back_slots, preferred_element_type=jnp.float32

time: 241 us -> 204 us (0.85)
  waiting for transfers between devices: 98.1 us -> 28.4 us
  starting transfers between devices: 31.9 us -> 50.6 us
  other arithmetic: 5.93 us -> 14.6 us
  local copies, waits for them, and re-layouts: 8.73 us -> 14.6 us
    all_to_all x3 -> x1, waiting for transfers between devices: 47.2 us -> 6 us  [gather_by_exchange(): lax.all_to_all(jnp.broadcast_to(block[None], (count,) + block.shape), axi...]
    all_to_all x1 -> x2, waiting for transfers between devices: 17.2 us -> 0.01 us  [the longest x1 0.01 us: shards(): lax.all_to_all(lax.dynamic_slice_in_dim(learn_tokens, core * half, half,...]
    ppermute x0 -> x5, starting transfers between devices: none -> 14.4 us  [the longest x3 10.4 us: shards(): lax.ppermute(arrived, ('xl', 'xh'), [(i, i ^ k) for i in range(4)])]
    all_to_all x1, waiting for transfers between devices: 11.4 us -> 0.01 us  [shards(): lax.all_to_all(activated_rows.reshape(n_y * n_z, CAP, hid_local), ROW, sp...]
    all_to_all x3 -> x1, starting transfers between devices: 15.7 us -> 7.24 us  [gather_by_exchange(): lax.all_to_all(jnp.broadcast_to(block[None], (count,) + block.shape), axi...]
    all_to_all x1 -> x2, starting transfers between devices: 3.55 us -> 10.6 us  [the longest x1 7.1 us: shards(): lax.all_to_all(lax.dynamic_slice_in_dim(learn_tokens, core * half, half,...]
    all_to_all x1, starting transfers between devices: 4.61 us -> 10.3 us  [shards(): lax.all_to_all(outgoing.reshape(n_y * n_z, CAP, share), ROW, split_axis=0...]
    another operation x1 -> x2, other arithmetic: 0.05 us -> 3.38 us  [the longest x1 2.55 us: shards(): pieces = jnp.stack([pieces, lax.ppermute(pieces, 'core', SWAP)])]
  transfers between devices with their start and end apart: 7 -> 11, of which waited for: 7 -> 3; matrix products, arithmetic and copies ran while one was open for 4% -> 13% of each run, Pallas kernels for 0% -> 0%
where the time goes in v2:
time: 204 us; the launch traced here: 203 us
  blocking collectives  85.3 us (42%)
  starting transfers between devices  50.6 us (25%)
  waiting for transfers between devices  28.4 us (14%)
  local copies, waits for them, and re-layouts  14.6 us (7%)
  other arithmetic  14.6 us (7%)
  matrix products  7.85 us (4%)
    all_gather x1, blocking collectives, shards(): fresh = lax.all_gather(fresh_rows, ROW, axis=0, tiled=True)  52.2 us
    all_gather x1, blocking collectives, shards(): lax.all_gather(master.astype(jnp.bfloat16).reshape(own_rows, wide), 'z',...  33.2 us
    all_to_all x1, waiting for transfers between devices, shards(): lax.all_to_all(outgoing.reshape(n_y * n_z, CAP, share), ROW, split_axis=0...  15.2 us
    ppermute x3, starting transfers between devices, shards(): lax.ppermute(arrived, ('xl', 'xh'), [(i, i ^ k) for i in range(4)])  10.4 us
    all_to_all x1, starting transfers between devices, shards(): lax.all_to_all(outgoing.reshape(n_y * n_z, CAP, share), ROW, split_axis=0...  10.3 us
    all_to_all x1, starting transfers between devices, gather_by_exchange(): lax.all_to_all(jnp.broadcast_to(block[None], (count,) + block.shape), axi...  7.24 us
    all_to_all x1, waiting for transfers between devices, shards(): lax.all_to_all(partial.reshape(n_z, own_rows, wide), 'z', split_axis=0, c...  7.19 us
    all_to_all x1, starting transfers between devices, shards(): lax.all_to_all(lax.dynamic_slice_in_dim(learn_tokens, core * half, half,...  7.1 us
  transfers between devices with their start and end apart: 11, of which 3 were waited for; matrix products, arithmetic and copies ran while one was open for 13% of the time, Pallas kernels for 0%

profile of v2, /device:TPU:6, one launch (start us, length us, event | category | flops | bytes accessed | tf_op | source)
XLA Modules:
  0.0 202.6 jit_solution(3816132900251565228)
XLA Ops:
  0.7 1.2 copy-done
  1.9 0.6 all_to_all.29
  2.5 1.0 copy.57
  3.5 7.1 %all-to-all-start = ((bf16[64,8,448]{2,0,1:T(8,128)(2,1)}), bf16[64,8,448]{2,0,1:T(8,128)(2,1)S(1)}, u32[]{:S(2)}, u32[]{:S(2)}) async-start(bf16[64,8,448]{2,0,1:T(8,128)(2,1)} %copy.57), calls=%async_computation | async-start | bytes 1048576 | tf_op jit(solution)/shard_map/all_to_all | solution.py:74
  11.1 0.2 reduce_window_sum.11
  11.2 0.1 copy-done.9
  11.3 0.2 select_reduce_fusion
  11.5 0.5 copy-done.13
  12.2 0.4 multiply_reduce_fusion
  12.6 0.2 reshape.144
  12.8 33.2 %all_gather.6 = bf16[448,256]{1,0:T(8,128)(2,1)} all-gather(bf16[56,256]{1,0:T(8,128)(2,1)S(1)} %bitcast.60), channel_id=1, replica_groups=mesh['xl'=2,'core'=2,'y'=8,'z'=8,'xh'=2] {'z'}, dimensions={0}, use_global_device_ids=true | all-gather | bytes 258048 | tf_op jit(solution)/shard_map/all_gather | solution.py:81
  46.2 1.9 collective-permute-start
  48.1 0.3 convolution_convert_fusion
  48.4 0.1 copy.61
  48.6 0.8 reshape.145
  49.4 10.3 %all-to-all-start.1 = ((bf16[64,4,448]{2,1,0:T(4,128)(2,1)}), bf16[64,4,448]{2,1,0:T(4,128)(2,1)S(1)}, u32[]{:S(2)}, u32[]{:S(2)}) async-start(bf16[64,4,448]{2,1,0:T(4,128)(2,1)} %reshape.145), calls=%async_computation.1 | async-start | bytes 524288 | tf_op jit(solution)/shard_map/all_to_all | solution.py:118
  59.7 15.2 %all-to-all-done.1 = bf16[64,4,448]{2,1,0:T(4,128)(2,1)S(1)} async-done(((bf16[64,4,448]{2,1,0:T(4,128)(2,1)}), bf16[64,4,448]{2,1,0:T(4,128)(2,1)S(1)}, u32[]{:S(2)}, u32[]{:S(2)}) %all-to-all-start.1) | async-done | bytes 229408 | tf_op jit(solution)/shard_map/all_to_all | solution.py:118
  74.9 0.1 reshape.146
  75.1 1.7 fusion.5
  76.8 0.9 copy.82
  77.7 3.5 %all-to-all-start.2 = ((f16[8,2,64,256]{3,2,1,0:T(8,128)(2,1)}), f16[8,2,64,256]{3,2,1,0:T(8,128)(2,1)S(1)}, u32[]{:S(2)}, u32[]{:S(2)}) async-start(f16[8,2,64,256]{3,2,1,0:T(8,128)(2,1)} %bitcast.50), calls=%async_computation.2 | async-start | bytes 1048576 | tf_op jit(solution)/shard_map/all_to_all | solution.py:127
  81.3 4.4 %reshape.147 = bf16[2,2,2,448,256]{4,3,2,1,0:T(8,128)(2,1)S(1)} reshape(bf16[1,3584,2,128]{3,2,1,0:T(2,128)(2,1)} %param.17) | data formatting | bytes 3670016 | tf_op jit(solution)/shard_map/reshape | solution.py:147
  85.8 0.6 maximum_bitcast_fusion
  86.3 1.3 constant_dynamic-slice_fusion.1
  87.7 1.6 reverse_select_fusion.2
  89.3 0.8 copy.62
  90.1 2.4 %collective-permute-start.3 = (bf16[256,448]{0,1:T(8,128)(2,1)}, bf16[256,448]{0,1:T(8,128)(2,1)S(1)}, u32[]{:S(2)}, u32[]{:S(2)}) collective-permute-start(bf16[256,448]{0,1:T(8,128)(2,1)} %copy.62), channel_id=1, source_target_pairs={{0,257},{1,256},{256,1},{257,0},{2,259},{3,258},{258,3},{259,2},{4... | collective-permute-start | bytes 688136 | tf_op jit(solution)/shard_map/ppermute | solution.py:143
  92.5 2.8 %collective-permute-start.2 = (bf16[256,448]{0,1:T(8,128)(2,1)}, bf16[256,448]{0,1:T(8,128)(2,1)}, u32[]{:S(2)}, u32[]{:S(2)}) collective-permute-start(bf16[256,448]{0,1:T(8,128)(2,1)} %copy.62), channel_id=1, source_target_pairs={{0,256},{1,257},{256,0},{257,1},{2,258},{3,259},{258,2},{259,3},{4... | collective-permute-start | bytes 688136 | tf_op jit(solution)/shard_map/ppermute | solution.py:143
  95.3 5.2 %collective-permute-start.1 = (bf16[256,448]{0,1:T(8,128)(2,1)}, bf16[256,448]{0,1:T(8,128)(2,1)}, u32[]{:S(2)}, u32[]{:S(2)}) collective-permute-start(bf16[256,448]{0,1:T(8,128)(2,1)} %copy.62), channel_id=1, source_target_pairs={{0,1},{1,0},{256,257},{257,256},{2,3},{3,2},{258,259},{259,258},{4... | collective-permute-start | bytes 688136 | tf_op jit(solution)/shard_map/ppermute | solution.py:143
  100.6 0.8 fusion.14
  101.5 0.8 broadcast_in_dim.2
  102.3 7.2 %all-to-all-start.3 = ((bf16[8,128,256]{2,1,0:T(8,128)(2,1)}), bf16[8,128,256]{2,1,0:T(8,128)(2,1)S(1)}, u32[]{:S(2)}, u32[]{:S(2)}) async-start(bf16[8,128,256]{2,1,0:T(8,128)(2,1)} %broadcast_in_dim.2), calls=%async_computation.3 | async-start | bytes 1048576 | tf_op jit(solution)/shard_map/all_to_all | solution.py:37
  109.6 2.6 %fusion.27 = (bf16[1,4,256,448]{2,3,1,0:T(8,128)(2,1)}, bf16[4,256,448]{1,2,0:T(8,128)(2,1)}) fusion(bf16[1,256,448]{1,2,0:T(8,128)(2,1)S(1)} %bitcast.59, bf16[1,256,448]{1,2,0:T(8,128)(2,1)} %bitcast.7, bf16[1,256,448]{1,2,0:T(8,128)(2,1)} %bitcast.6, bf16[1,256,448]{1,2,0:T(8,128)(2,1)} %bitcast.5), kind=kLoop, calls=%fused_computation.73 | loop fusion | flops 1376256 | bytes 2752512 | tf_op jit(solution)/shard_map/stack | solution.py:146
  112.1 2.0 %collective-permute-start.4 = (bf16[4,256,448]{1,2,0:T(8,128)(2,1)}, bf16[4,256,448]{1,2,0:T(8,128)(2,1)}, u32[]{:S(2)}, u32[]{:S(2)}) collective-permute-start(bf16[4,256,448]{1,2,0:T(8,128)(2,1)} %get-tuple-element.28), channel_id=1, source_target_pairs={{0,128},{128,0},{1,129},{129,1},{2,130},{130,2},{3,131},{131,3},{4... | collective-permute-start | bytes 2752520 | tf_op jit(solution)/shard_map/ppermute | solution.py:146
  114.2 1.5 reverse_select_fusion.1
  115.9 2.5 %fusion = bf16[2,2,2,448,256]{4,3,2,0,1:T(8,128)(2,1)S(1)} fusion(bf16[2,2,2,448,256]{4,3,2,1,0:T(8,128)(2,1)} %reverse_select_fusion.1, pred[]{:T(512)S(6)} %eq.70), kind=kLoop, calls=%fused_computation.4 | loop fusion | flops 917504 | bytes 3670017 | tf_op jit(solution)/shard_map/transpose | solution.py:152
  118.5 0.5 copy-done.10
  119.1 6.0 %all-to-all-done.3 = bf16[8,128,256]{2,1,0:T(8,128)(2,1)S(1)} async-done(((bf16[8,128,256]{2,1,0:T(8,128)(2,1)}), bf16[8,128,256]{2,1,0:T(8,128)(2,1)S(1)}, u32[]{:S(2)}, u32[]{:S(2)}) %all-to-all-start.3) | async-done | bytes 524320 | tf_op jit(solution)/shard_map/all_to_all | solution.py:37
  125.1 2.4 %fusion.6 = f16[448,256]{1,0:T(8,128)(2,1)} fusion(bf16[1024,448]{1,0:T(8,128)(2,1)} %copy-done.2, bf16[1024,256]{1,0:T(8,128)(2,1)S(1)} %bitcast.57), kind=kOutput, calls=%fused_computation.12 | convolution fusion | flops 235110400 | bytes 1671168 | tf_op jit(solution)/shard_map/dot_general | solution.py:157
  127.5 3.6 %all-to-all-start.4 = ((f16[8,56,256]{2,1,0:T(8,128)(2,1)}), f16[8,56,256]{2,1,0:T(8,128)(2,1)S(1)}, u32[]{:S(2)}, u32[]{:S(2)}) async-start(f16[8,56,256]{2,1,0:T(8,128)(2,1)} %bitcast.23), calls=%async_computation.4 | async-start | bytes 458752 | tf_op jit(solution)/shard_map/all_to_all | solution.py:162
  131.1 2.2 %fusion.7 = f32[256,256]{1,0:T(8,128)S(1)} fusion(bf16[2,4,448,256]{3,2,1,0:T(8,128)(2,1)S(1)} %bitcast.55, bf16[1,4,256,448]{2,3,1,0:T(8,128)(2,1)} %bitcast.10, bf16[1,4,256,448]{2,3,1,0:T(8,128)(2,1)} %get-tuple-element.27), kind=kOutput, calls=%fused_computation.14 | convolution fusion | flops 470679552 | bytes 3932160 | tf_op jit(solution)/shard_map/cjsd,cjdk->sk/dot_general | solution.py:176
  133.4 0.7 fusion.12
  134.0 7.2 %all-to-all-done.4 = f16[8,56,256]{2,1,0:T(8,128)(2,1)S(1)} async-done(((f16[8,56,256]{2,1,0:T(8,128)(2,1)}), f16[8,56,256]{2,1,0:T(8,128)(2,1)S(1)}, u32[]{:S(2)}, u32[]{:S(2)}) %all-to-all-start.4) | async-done | bytes 229408 | tf_op jit(solution)/shard_map/all_to_all | solution.py:162
  141.4 0.8 multiply_convert_fusion.2
  142.2 4.6 %all-to-all-start.5 = ((bf16[64,4,128]{2,1,0:T(4,128)(2,1)}), bf16[64,4,128]{2,1,0:T(4,128)(2,1)S(1)}, u32[]{:S(2)}, u32[]{:S(2)}) async-start(bf16[64,4,128]{2,1,0:T(4,128)(2,1)} %bitcast.24), calls=%async_computation.5 | async-start | bytes 131072 | tf_op jit(solution)/shard_map/all_to_all | solution.py:187
  146.8 52.2 %all-gather.1 = f16[3584,2,128]{2,1,0:T(2,128)(2,1)S(1)} all-gather(f16[56,2,128]{2,1,0:T(2,128)(2,1)S(1)} %get-tuple-element.20), channel_id=1, replica_groups=mesh['xl'=2,'core'=2,'y'=8,'z'=8,'xh'=2] {'y','z'}, dimensions={0}, use_global_device_ids=true | all-gather | bytes 1863680 | tf_op jit(solution)/shard_map/all_gather | solution.py:190
  199.0 2.8 %multiply_convert_fusion = bf16[3584,2,128]{2,1,0:T(2,128)(2,1)} fusion(f16[3584,2,128]{2,1,0:T(2,128)(2,1)S(1)} %all-gather.1), kind=kLoop, calls=%fused_computation | loop fusion | flops 2752512 | bytes 3670016 | tf_op jit(solution)/shard_map/convert_element_type | solution.py:32
  201.8 0.8 fusion.11
  (70 shorter events, 1.6 us)
Async XLA Ops:
  0.6 1.2 copy-start
  1.8 8.8 %copy-start.15 = (s32[16]{0:T(128)S(1)}, s32[16]{0:T(128)}, u32[]{:S(2)}) copy-start(s32[16]{0:T(128)} %param.13) | copy-start | bytes 196
  1.8 8.8 %copy-start.11 = (s32[16,8]{0,1:T(8,128)S(1)}, s32[16,8]{0,1:T(8,128)}, u32[]{:S(2)}) copy-start(s32[16,8]{0,1:T(8,128)} %param.15) | copy-start | bytes 1540
  1.8 9.0 %copy-start.8 = (f32[3584]{0:T(1024)S(1)}, f32[3584]{0:T(1024)}, u32[]{:S(2)}) copy-start(f32[3584]{0:T(1024)} %param.14) | copy-start | bytes 43012
  1.8 9.1 %copy-start.3 = (f32[56,2,128]{2,1,0:T(2,128)S(1)}, f32[56,2,128]{2,1,0:T(2,128)}, u32[]{:S(2)}) copy-start(f32[56,2,128]{2,1,0:T(2,128)} %param.21) | copy-start | bytes 172036
  1.9 10.2 %copy-start.5 = (bf16[16,3584]{1,0:T(8,128)(2,1)S(1)}, bf16[16,3584]{1,0:T(8,128)(2,1)}, u32[]{:S(2)}) copy-start(bf16[16,3584]{1,0:T(8,128)(2,1)} %param.12) | copy-start | bytes 344068
  3.5 42.7 %all-to-all-start = ((bf16[64,8,448]{2,0,1:T(8,128)(2,1)}), bf16[64,8,448]{2,0,1:T(8,128)(2,1)S(1)}, u32[]{:S(2)}, u32[]{:S(2)}) async-start(bf16[64,8,448]{2,0,1:T(8,128)(2,1)} %copy.57), calls=%async_computation | async-start | bytes 1048576 | tf_op jit(solution)/shard_map/all_to_all | solution.py:74
  10.8 0.5 copy-start.9
  11.5 0.5 copy-start.13
  46.2 28.9 %collective-permute-start = (bf16[512,448]{1,0:T(8,128)(2,1)S(1)}, bf16[512,448]{1,0:T(8,128)(2,1)S(1)}, u32[]{:S(2)}, u32[]{:S(2)}) collective-permute-start(bf16[512,448]{1,0:T(8,128)(2,1)S(1)} %bitcast.52), channel_id=1, source_target_pairs={{0,128},{128,0},{1,129},{129,1},{2,130},{130,2},{3,131},{131,3},{4... | collective-permute-start | bytes 1376264 | tf_op jit(solution)/shard_map/ppermute | solution.py:85
  49.4 25.5 %all-to-all-start.1 = ((bf16[64,4,448]{2,1,0:T(4,128)(2,1)}), bf16[64,4,448]{2,1,0:T(4,128)(2,1)S(1)}, u32[]{:S(2)}, u32[]{:S(2)}) async-start(bf16[64,4,448]{2,1,0:T(4,128)(2,1)} %reshape.145), calls=%async_computation.1 | async-start | bytes 524288 | tf_op jit(solution)/shard_map/all_to_all | solution.py:118
  75.1 2.6 %copy-start.2 = (bf16[1024,448]{1,0:T(8,128)(2,1)}, bf16[1024,448]{1,0:T(8,128)(2,1)S(1)}, u32[]{:S(2)}) copy-start(bf16[1024,448]{1,0:T(8,128)(2,1)S(1)} %constant_dynamic-update-slice_fusion) | copy-start | bytes 2752516
  75.1 6.1 %copy-start.16 = (s32[128]{0:T(128)S(1)}, s32[128]{0:T(128)}, u32[]{:S(2)}) copy-start(s32[128]{0:T(128)} %param.19) | copy-start | bytes 1540
  77.7 22.8 %all-to-all-start.2 = ((f16[8,2,64,256]{3,2,1,0:T(8,128)(2,1)}), f16[8,2,64,256]{3,2,1,0:T(8,128)(2,1)S(1)}, u32[]{:S(2)}, u32[]{:S(2)}) async-start(f16[8,2,64,256]{3,2,1,0:T(8,128)(2,1)} %bitcast.50), calls=%async_computation.2 | async-start | bytes 1048576 | tf_op jit(solution)/shard_map/all_to_all | solution.py:127
  90.1 19.5 %collective-permute-start.3 = (bf16[256,448]{0,1:T(8,128)(2,1)}, bf16[256,448]{0,1:T(8,128)(2,1)S(1)}, u32[]{:S(2)}, u32[]{:S(2)}) collective-permute-start(bf16[256,448]{0,1:T(8,128)(2,1)} %copy.62), channel_id=1, source_target_pairs={{0,257},{1,256},{256,1},{257,0},{2,259},{3,258},{258,3},{259,2},{4... | collective-permute-start | bytes 688136 | tf_op jit(solution)/shard_map/ppermute | solution.py:143
  92.5 17.1 %collective-permute-start.2 = (bf16[256,448]{0,1:T(8,128)(2,1)}, bf16[256,448]{0,1:T(8,128)(2,1)}, u32[]{:S(2)}, u32[]{:S(2)}) collective-permute-start(bf16[256,448]{0,1:T(8,128)(2,1)} %copy.62), channel_id=1, source_target_pairs={{0,256},{1,257},{256,0},{257,1},{2,258},{3,259},{258,2},{259,3},{4... | collective-permute-start | bytes 688136 | tf_op jit(solution)/shard_map/ppermute | solution.py:143
  95.3 14.3 %collective-permute-start.1 = (bf16[256,448]{0,1:T(8,128)(2,1)}, bf16[256,448]{0,1:T(8,128)(2,1)}, u32[]{:S(2)}, u32[]{:S(2)}) collective-permute-start(bf16[256,448]{0,1:T(8,128)(2,1)} %copy.62), channel_id=1, source_target_pairs={{0,1},{1,0},{256,257},{257,256},{2,3},{3,2},{258,259},{259,258},{4... | collective-permute-start | bytes 688136 | tf_op jit(solution)/shard_map/ppermute | solution.py:143
  102.3 11.9 %copy-start.1 = (bf16[2,2,2,448,256]{4,3,2,1,0:T(8,128)(2,1)S(1)}, bf16[2,2,2,448,256]{4,3,2,1,0:T(8,128)(2,1)}, u32[]{:S(2)}) copy-start(bf16[2,2,2,448,256]{4,3,2,1,0:T(8,128)(2,1)} %reverse_select_fusion.2) | copy-start | bytes 5505028
  102.3 22.8 %all-to-all-start.3 = ((bf16[8,128,256]{2,1,0:T(8,128)(2,1)}), bf16[8,128,256]{2,1,0:T(8,128)(2,1)S(1)}, u32[]{:S(2)}, u32[]{:S(2)}) async-start(bf16[8,128,256]{2,1,0:T(8,128)(2,1)} %broadcast_in_dim.2), calls=%async_computation.3 | async-start | bytes 1048576 | tf_op jit(solution)/shard_map/all_to_all | solution.py:37
  112.1 3.6 %copy-start.12 = (f32[16,8]{0,1:T(8,128)S(1)}, f32[16,8]{0,1:T(8,128)}, u32[]{:S(2)}) copy-start(f32[16,8]{0,1:T(8,128)} %param.16) | copy-start | bytes 1540
  112.1 19.0 %collective-permute-start.4 = (bf16[4,256,448]{1,2,0:T(8,128)(2,1)}, bf16[4,256,448]{1,2,0:T(8,128)(2,1)}, u32[]{:S(2)}, u32[]{:S(2)}) collective-permute-start(bf16[4,256,448]{1,2,0:T(8,128)(2,1)} %get-tuple-element.28), channel_id=1, source_target_pairs={{0,128},{128,0},{1,129},{129,1},{2,130},{130,2},{3,131},{131,3},{4... | collective-permute-start | bytes 2752520 | tf_op jit(solution)/shard_map/ppermute | solution.py:146
  118.4 0.7 copy-start.10
  118.4 0.7 copy-start.14
  127.5 13.7 %all-to-all-start.4 = ((f16[8,56,256]{2,1,0:T(8,128)(2,1)}), f16[8,56,256]{2,1,0:T(8,128)(2,1)S(1)}, u32[]{:S(2)}, u32[]{:S(2)}) async-start(f16[8,56,256]{2,1,0:T(8,128)(2,1)} %bitcast.23), calls=%async_computation.4 | async-start | bytes 458752 | tf_op jit(solution)/shard_map/all_to_all | solution.py:162
  131.1 10.3 %copy-start.4 = (f32[56,2,128]{2,1,0:T(2,128)S(1)}, f32[56,2,128]{2,1,0:T(2,128)}, u32[]{:S(2)}) copy-start(f32[56,2,128]{2,1,0:T(2,128)} %param.21) | copy-start | bytes 172036
  131.1 10.3 %copy-start.6 = (f32[56,2,128]{2,1,0:T(2,128)S(1)}, f32[56,2,128]{2,1,0:T(2,128)}, u32[]{:S(2)}) copy-start(f32[56,2,128]{2,1,0:T(2,128)} %param.22) | copy-start | bytes 172036
  131.1 10.3 %copy-start.7 = (f32[56,2,128]{2,1,0:T(2,128)S(1)}, f32[56,2,128]{2,1,0:T(2,128)}, u32[]{:S(2)}) copy-start(f32[56,2,128]{2,1,0:T(2,128)} %param.23) | copy-start | bytes 172036
  142.2 56.8 %all-to-all-start.5 = ((bf16[64,4,128]{2,1,0:T(4,128)(2,1)}), bf16[64,4,128]{2,1,0:T(4,128)(2,1)S(1)}, u32[]{:S(2)}, u32[]{:S(2)}) async-start(bf16[64,4,128]{2,1,0:T(4,128)(2,1)} %bitcast.24), calls=%async_computation.5 | async-start | bytes 131072 | tf_op jit(solution)/shard_map/all_to_all | solution.py:187

commit v3 on v2

--- a/solution.py
+++ b/solution.py
@@ -18,6 +18,7 @@
 
 ROW = ("y", "z")
 COLUMN = ("xl", "core", "xh")
+ALONG_X = ("xl", "xh")
 SWAP = [(0, 1), (1, 0)]
 pre_scale = 2.0**7
 grad_scale = 2.0**-7
@@ -57,7 +58,6 @@
     own_rows = master.shape[0]
     wide = 2 * hid_local
     n_y, n_z = lax.axis_size("y"), lax.axis_size("z")
-    n_x = lax.axis_size(COLUMN)
 
     half = learn_tokens.shape[0] // 2
     core = lax.axis_index("core")
@@ -71,20 +71,6 @@
             axis=0,
         )
 
-    own_slice = lax.all_to_all(
-        lax.dynamic_slice_in_dim(learn_tokens, core * half, half, 0),
-        "y",
-        split_axis=1,
-        concat_axis=0,
-        tiled=True,
-    )
-    weights = lax.all_gather(
-        master.astype(jnp.bfloat16).reshape(own_rows, wide), "z", axis=0, tiled=True
-    )
-    own_slice, weights = lax.optimization_barrier((own_slice, weights))
-    other_slice = lax.ppermute(own_slice, "core", SWAP)
-    token_slice = jnp.concatenate([own_slice, other_slice], axis=0)
-
     rows_dev, width = hidden_rows.shape
     grouped = hidden_rows.reshape(rows_dev // BEAMS, BEAMS, width)
     selector = (
@@ -106,18 +92,38 @@
     slot_table = (
         slot_index[:, None] == jnp.arange(EXPERTS * CAP, dtype=jnp.int32)[None, :]
     ).astype(jnp.float32)
-    row_table = slot_table.reshape(rows_dev, TOP, EXPERTS * CAP).sum(axis=1).astype(jnp.bfloat16)
-    share = width // n_x
-    normed_share = lax.dynamic_index_in_dim(
-        normed.reshape(rows_dev, n_x, share), lax.axis_index(COLUMN), axis=1, keepdims=False
-    )
+    row_table = slot_table.reshape(rows_dev, TOP, EXPERTS, CAP).sum(axis=1)
+    slot_row = lax.axis_index(ALONG_X)
+    row_table = lax.dynamic_index_in_dim(row_table, slot_row, axis=2, keepdims=False)
+    span = width // 2
+    normed_half = lax.dynamic_slice_in_dim(normed, core * span, span, 1)
     outgoing = lax.dot_general(
-        row_table, normed_share, (((0,), (0,)), ((), ())), preferred_element_type=jnp.float32
-    ).astype(jnp.bfloat16)
-    outgoing, own_slice = lax.optimization_barrier((outgoing, own_slice))
-    arrived = lax.all_to_all(
-        outgoing.reshape(n_y * n_z, CAP, share), ROW, split_axis=0, concat_axis=0, tiled=True
-    ).reshape(EXPERTS * CAP, share)
+        row_table.astype(jnp.bfloat16),
+        normed_half,
+        (((0,), (0,)), ((), ())),
+        preferred_element_type=jnp.float32,
+    ).astype(jnp.bfloat16)
+    features = width // n_y
+    chunks = span // features
+    tokens_half = lax.dynamic_slice_in_dim(learn_tokens, core * half, half, 0)
+    along_y = jnp.concatenate(
+        [
+            tokens_half.reshape(half, n_y, features).transpose(1, 0, 2),
+            outgoing.reshape(n_y, n_z * chunks, features),
+        ],
+        axis=1,
+    )
+    along_y = lax.all_to_all(along_y, "y", split_axis=0, concat_axis=0, tiled=True)
+    weights = lax.all_gather(
+        master.astype(jnp.bfloat16).reshape(own_rows, wide), "z", axis=0, tiled=True
+    )
+    along_y, weights = lax.optimization_barrier((along_y, weights))
+    own_slice = along_y[:, :half].reshape(n_y * half, features)
+    other_slice = lax.ppermute(own_slice, "core", SWAP)
+    token_slice = jnp.concatenate([own_slice, other_slice], axis=0)
+    along_z = along_y[:, half:].reshape(n_y, n_z, chunks, features).transpose(1, 0, 2, 3)
+    arrived = lax.all_to_all(along_z, "z", split_axis=0, concat_axis=0, tiled=True)
+    arrived = arrived.reshape(n_z * n_y, span)
 
     partial_pre = to_half(
         jnp.dot(token_slice, weights, preferred_element_type=jnp.float32), pre_scale
@@ -140,16 +146,11 @@
     ).astype(jnp.bfloat16)
 
     pieces = [arrived] + [
-        lax.ppermute(arrived, ("xl", "xh"), [(i, i ^ k) for i in range(4)]) for k in (1, 2, 3)
+        lax.ppermute(arrived, ALONG_X, [(i, i ^ k) for i in range(CAP)]) for k in range(1, CAP)
     ]
-    pieces = jnp.stack(pieces)
-    pieces = jnp.stack([pieces, lax.ppermute(pieces, "core", SWAP)])
-    local_weight = expert_weight.reshape(2, 2, 2, share, wide)
-    for place, axis in enumerate(COLUMN):
-        local_weight = jnp.where(
-            lax.axis_index(axis) == 1, jnp.flip(local_weight, place), local_weight
-        )
-    local_weight = local_weight.transpose(1, 0, 2, 3, 4)
+    pieces = jnp.concatenate(pieces, axis=0)
+    other_pieces = lax.ppermute(pieces, "core", SWAP)
+    local_weight = expert_weight.reshape(width, wide)
 
     grad_all = gather_by_exchange(grad_pre, "y").reshape(n_y, 2, half, wide)
     grad_all = grad_all.transpose(1, 0, 2, 3).reshape(token_slice.shape[0], wide)
@@ -173,23 +174,33 @@
     new_master = master - learn_rate * (update + decay_rate * master)
     fresh_rows = to_half(new_master.astype(jnp.bfloat16), fresh_scale)
 
-    projected_rows = jnp.einsum(
-        "cjsd,cjdk->sk",
-        pieces,
-        local_weight.reshape(2, 4, share, wide),
+    projected_rows = jnp.dot(
+        jnp.where(core == 0, pieces, other_pieces),
+        local_weight[:span],
+        preferred_element_type=jnp.float32,
+    ) + jnp.dot(
+        jnp.where(core == 0, other_pieces, pieces),
+        local_weight[span:],
         preferred_element_type=jnp.float32,
     )
     gate_rows = projected_rows[:, :hid_local]
     activated_rows = (
         gate_rows * jax.nn.sigmoid(gate_rows) * projected_rows[:, hid_local:]
     ).astype(jnp.bfloat16)
+    activated_rows = activated_rows.reshape(2, 2, n_z, n_y, hid_local)
+    for place, axis in enumerate(ALONG_X):
+        activated_rows = jnp.where(
+            lax.axis_index(axis) == 1, jnp.flip(activated_rows, place), activated_rows
+        )
+    activated_rows = activated_rows.transpose(3, 2, 0, 1, 4).reshape(n_y * n_z, CAP, hid_local)
+    fresh_rows = gather_by_exchange(fresh_rows.reshape(own_rows, wide), "z")
     activated_rows, fresh_rows = lax.optimization_barrier((activated_rows, fresh_rows))
     returned = lax.all_to_all(
-        activated_rows.reshape(n_y * n_z, CAP, hid_local), ROW, split_axis=0, concat_axis=0, tiled=True
-    )
-    fresh = lax.all_gather(fresh_rows, ROW, axis=0, tiled=True)
+        activated_rows, ROW, split_axis=0, concat_axis=0, tiled=True
+    )
+    fresh = lax.all_gather(fresh_rows.reshape(n_z * own_rows, wide), "y", axis=0, tiled=True)
     returned, fresh = lax.optimization_barrier((returned, fresh))
-    fresh = from_half(fresh, fresh_scale)
+    fresh = from_half(fresh, fresh_scale).reshape(n_y * n_z * own_rows, 2, hid_local)
     back_slots = returned.reshape(EXPERTS * CAP, hid_local)
     picked = jnp.dot(
         slot_table.astype(jnp.bfloat16), back_slots, preferred_element_type=jnp.float32

time: 204 us -> 198 us (0.971)
  waiting for transfers between devices: 28.4 us -> 52.8 us
  blocking collectives: 85.3 us -> 63.7 us
  other arithmetic: 14.6 us -> 3.93 us
  local copies, waits for them, and re-layouts: 14.6 us -> 19.3 us
  starting transfers between devices: 50.6 us -> 47.4 us
    all_gather x1, blocking collectives: 52.2 us -> 32.6 us  [shards(): lax.all_gather(fresh_rows.reshape(n_z * own_rows, wide), 'y', axis=0, til...]
    all_to_all x1 -> x2, waiting for transfers between devices: 6 us -> 22 us  [gather_by_exchange(): lax.all_to_all(jnp.broadcast_to(block[None], (count,) + block.shape), axi...]
    all_to_all x1, waiting for transfers between devices: 0.01 us -> 9.81 us  [shards(): lax.all_to_all(partial_pre, 'y', split_axis=0, concat_axis=0, tiled=True)]
    all_to_all x3, starting transfers between devices: 22 us -> 15.7 us  [the longest x1 7.1 us: shards(): lax.all_to_all(along_y, 'y', split_axis=0, concat_axis=0, tiled=True)]
    all_to_all x1, starting transfers between devices: 3.49 us -> 7.21 us  [shards(): lax.all_to_all(partial_pre, 'y', split_axis=0, concat_axis=0, tiled=True)]
    another operation x2 -> x1, other arithmetic: 3.38 us -> 0.09 us  [the longest x1 2.55 us: shards(): pieces = jnp.stack([pieces, lax.ppermute(pieces, 'core', SWAP)])]
    select_n x2, other arithmetic: 3.11 us -> 0.04 us  [shards(): jnp.where(lax.axis_index(axis) == 1, jnp.flip(activated_rows, place), act...]
    all_to_all x3, waiting for transfers between devices: 15.2 us -> 12.4 us  [the longest x1 12.4 us: shards(): lax.all_to_all(along_z, 'z', split_axis=0, concat_axis=0, tiled=True)]
  transfers between devices with their start and end apart: 11 -> 12, of which waited for: 3 -> 6; matrix products, arithmetic and copies ran while one was open for 13% -> 7% of each run, Pallas kernels for 0% -> 0%
where the time goes in v3:
time: 198 us; the launch traced here: 197 us
  blocking collectives  63.7 us (32%)
  waiting for transfers between devices  52.8 us (27%)
  starting transfers between devices  47.4 us (24%)
  local copies, waits for them, and re-layouts  19.3 us (10%)
  matrix products  8.55 us (4%)
  other arithmetic  3.93 us (2%)
    all_gather x1, blocking collectives, shards(): lax.all_gather(fresh_rows.reshape(n_z * own_rows, wide), 'y', axis=0, til...  32.6 us
    all_gather x1, blocking collectives, shards(): lax.all_gather(master.astype(jnp.bfloat16).reshape(own_rows, wide), 'z',...  31.1 us
    all_to_all x2, waiting for transfers between devices, gather_by_exchange(): lax.all_to_all(jnp.broadcast_to(block[None], (count,) + block.shape), axi...  22 us
    all_to_all x1, waiting for transfers between devices, shards(): lax.all_to_all(along_z, 'z', split_axis=0, concat_axis=0, tiled=True)  12.4 us
    ppermute x3, starting transfers between devices, shards(): lax.ppermute(arrived, ALONG_X, [(i, i ^ k) for i in range(CAP)])  10.4 us
    all_to_all x1, waiting for transfers between devices, shards(): lax.all_to_all(partial_pre, 'y', split_axis=0, concat_axis=0, tiled=True)  9.81 us
    all_to_all x1, waiting for transfers between devices, shards(): lax.all_to_all(partial.reshape(n_z, own_rows, wide), 'z', split_axis=0, c...  8.27 us
    all_to_all x1, starting transfers between devices, shards(): lax.all_to_all(partial_pre, 'y', split_axis=0, concat_axis=0, tiled=True)  7.21 us
  transfers between devices with their start and end apart: 12, of which 6 were waited for; matrix products, arithmetic and copies ran while one was open for 7% of the time, Pallas kernels for 0%

profile of v3, /device:TPU:6, one launch (start us, length us, event | category | flops | bytes accessed | tf_op | source)
XLA Modules:
  0.0 196.8 jit_solution(4102730165218070982)
XLA Ops:
  0.7 0.8 eq.79
  1.5 0.8 copy.48
  2.9 0.9 reshape.150
  3.8 0.4 multiply_reduce_fusion
  4.4 0.8 dynamic-slice.8
  5.4 0.3 convolution_convert_fusion
  5.6 0.3 reshape.152
  6.1 0.6 reshape.149
  6.9 1.1 copy.51
  8.0 7.1 %all-to-all-start = ((bf16[8,96,448]{2,1,0:T(8,128)(2,1)}), bf16[8,96,448]{2,1,0:T(8,128)(2,1)S(1)}, u32[]{:S(2)}, u32[]{:S(2)}) async-start(bf16[8,96,448]{2,1,0:T(8,128)(2,1)} %copy.51), calls=%async_computation | async-start | bytes 1572864 | tf_op jit(solution)/shard_map/all_to_all | solution.py:116
  15.1 31.1 %all_gather.6 = bf16[448,256]{1,0:T(8,128)(2,1)S(1)} all-gather(bf16[56,256]{1,0:T(8,128)(2,1)S(1)} %bitcast.67), channel_id=1, replica_groups=mesh['xl'=2,'core'=2,'y'=8,'z'=8,'xh'=2] {'z'}, dimensions={0}, use_global_device_ids=true | all-gather | bytes 258048 | tf_op jit(solution)/shard_map/all_gather | solution.py:117
  46.3 1.9 collective-permute-start
  48.2 0.4 copy.53
  48.7 0.7 slice.40
  49.4 4.0 %all-to-all-start.1 = ((bf16[8,8,4,448]{3,1,2,0:T(8,128)(2,1)}), bf16[8,8,4,448]{3,1,2,0:T(8,128)(2,1)S(1)}, u32[]{:S(2)}, u32[]{:S(2)}) async-start(bf16[8,8,4,448]{3,1,2,0:T(8,128)(2,1)} %bitcast.5), calls=%async_computation.1 | async-start | bytes 524288 | tf_op jit(solution)/shard_map/all_to_all | solution.py:125
  53.5 12.4 %all-to-all-done.1 = bf16[8,8,4,448]{3,1,2,0:T(8,128)(2,1)S(1)} async-done(((bf16[8,8,4,448]{3,1,2,0:T(8,128)(2,1)}), bf16[8,8,4,448]{3,1,2,0:T(8,128)(2,1)S(1)}, u32[]{:S(2)}, u32[]{:S(2)}) %all-to-all-start.1) | async-done | bytes 229408 | tf_op jit(solution)/shard_map/all_to_all | solution.py:125
  66.3 1.5 fusion
  67.8 0.9 copy.80
  68.7 2.4 %collective-permute-start.3 = (bf16[64,1792]{1,0:T(8,128)(2,1)S(1)}, bf16[64,1792]{1,0:T(8,128)(2,1)}, u32[]{:S(2)}, u32[]{:S(2)}) collective-permute-start(bf16[64,1792]{1,0:T(8,128)(2,1)S(1)} %reshape.157), channel_id=1, source_target_pairs={{0,257},{1,256},{256,1},{257,0},{2,259},{3,258},{258,3},{259,2},{4... | collective-permute-start | bytes 688136 | tf_op jit(solution)/shard_map/ppermute | solution.py:149
  71.1 2.8 %collective-permute-start.2 = (bf16[64,1792]{1,0:T(8,128)(2,1)S(1)}, bf16[64,1792]{1,0:T(8,128)(2,1)}, u32[]{:S(2)}, u32[]{:S(2)}) collective-permute-start(bf16[64,1792]{1,0:T(8,128)(2,1)S(1)} %reshape.157), channel_id=1, source_target_pairs={{0,256},{1,257},{256,0},{257,1},{2,258},{3,259},{258,2},{259,3},{4... | collective-permute-start | bytes 688136 | tf_op jit(solution)/shard_map/ppermute | solution.py:149
  73.9 5.2 %collective-permute-start.1 = (bf16[64,1792]{1,0:T(8,128)(2,1)S(1)}, bf16[64,1792]{1,0:T(8,128)(2,1)S(1)}, u32[]{:S(2)}, u32[]{:S(2)}) collective-permute-start(bf16[64,1792]{1,0:T(8,128)(2,1)S(1)} %reshape.157), channel_id=1, source_target_pairs={{0,1},{1,0},{256,257},{257,256},{2,3},{3,2},{258,259},{259,258},{4... | collective-permute-start | bytes 688136 | tf_op jit(solution)/shard_map/ppermute | solution.py:149
  79.1 7.2 %all-to-all-start.2 = ((f16[8,2,64,256]{3,2,1,0:T(8,128)(2,1)}), f16[8,2,64,256]{3,2,1,0:T(8,128)(2,1)S(1)}, u32[]{:S(2)}, u32[]{:S(2)}) async-start(f16[8,2,64,256]{3,2,1,0:T(8,128)(2,1)} %bitcast.51), calls=%async_computation.2 | async-start | bytes 1048576 | tf_op jit(solution)/shard_map/all_to_all | solution.py:133
  86.4 0.7 constant_dynamic-update-slice_fusion.3
  87.1 0.3 collective-permute-done.1
  87.4 0.7 constant_dynamic-update-slice_fusion.2
  88.1 1.8 constant_dynamic-update-slice_fusion.1
  89.8 1.6 constant_dynamic-update-slice_fusion
  91.5 1.9 collective-permute-start.4
  93.4 9.8 %all-to-all-done.2 = f16[8,2,64,256]{3,2,1,0:T(8,128)(2,1)S(1)} async-done(((f16[8,2,64,256]{3,2,1,0:T(8,128)(2,1)}), f16[8,2,64,256]{3,2,1,0:T(8,128)(2,1)S(1)}, u32[]{:S(2)}, u32[]{:S(2)}) %all-to-all-start.2) | async-done | bytes 524320 | tf_op jit(solution)/shard_map/all_to_all | solution.py:133
  103.4 0.8 broadcast_in_dim.6
  104.2 3.5 %all-to-all-start.3 = ((bf16[8,128,256]{2,1,0:T(8,128)(2,1)}), bf16[8,128,256]{2,1,0:T(8,128)(2,1)S(1)}, u32[]{:S(2)}, u32[]{:S(2)}) async-start(bf16[8,128,256]{2,1,0:T(8,128)(2,1)} %broadcast_in_dim.6), calls=%async_computation.3 | async-start | bytes 1048576 | tf_op jit(solution)/shard_map/all_to_all | solution.py:38
  107.9 2.1 %fusion.30 = (bf16[1,1792,2,128]{3,2,1,0:T(2,128)(2,1)}, bf16[1,1792,2,128]{3,2,1,0:T(2,128)(2,1)S(1)}) fusion(bf16[1,3584,2,128]{3,2,1,0:T(2,128)(2,1)S(1)} %copy-done.1), kind=kLoop, calls=%fused_computation.81 | loop fusion | bytes 3670016 | tf_op jit(solution)/shard_map/slice | solution.py:179
  110.0 1.7 fusion.4
  111.7 12.0 %all-to-all-done.3 = bf16[8,128,256]{2,1,0:T(8,128)(2,1)S(1)} async-done(((bf16[8,128,256]{2,1,0:T(8,128)(2,1)}), bf16[8,128,256]{2,1,0:T(8,128)(2,1)S(1)}, u32[]{:S(2)}, u32[]{:S(2)}) %all-to-all-start.3) | async-done | bytes 524320 | tf_op jit(solution)/shard_map/all_to_all | solution.py:38
  123.8 2.3 %fusion.1 = f16[448,256]{1,0:T(8,128)(2,1)} fusion(bf16[1024,256]{1,0:T(8,128)(2,1)S(1)} %bitcast.63, bf16[512,448]{1,0:T(8,128)(2,1)} %collective-permute-done, bf16[512,448]{1,0:T(8,128)(2,1)S(1)} %bitcast.62), kind=kOutput, calls=%fused_computation.5 | convolution fusion | flops 236945408 | bytes 1671168 | tf_op jit(solution)/shard_map/dot_general | solution.py:158
  126.1 3.4 %all-to-all-start.4 = ((f16[8,56,256]{2,1,0:T(8,128)(2,1)}), f16[8,56,256]{2,1,0:T(8,128)(2,1)S(1)}, u32[]{:S(2)}, u32[]{:S(2)}) async-start(f16[8,56,256]{2,1,0:T(8,128)(2,1)} %bitcast.16), calls=%async_computation.4 | async-start | bytes 458752 | tf_op jit(solution)/shard_map/all_to_all | solution.py:163
  129.5 1.6 convolution_add_fusion
  131.3 8.3 %all-to-all-done.4 = f16[8,56,256]{2,1,0:T(8,128)(2,1)S(1)} async-done(((f16[8,56,256]{2,1,0:T(8,128)(2,1)}), f16[8,56,256]{2,1,0:T(8,128)(2,1)S(1)}, u32[]{:S(2)}, u32[]{:S(2)}) %all-to-all-start.4) | async-done | bytes 229408 | tf_op jit(solution)/shard_map/all_to_all | solution.py:163
  139.7 0.8 multiply_convert_fusion.2
  140.6 0.7 broadcast_in_dim.8
  141.3 3.4 %all-to-all-start.5 = ((f16[8,56,256]{2,1,0:T(8,128)(2,1)}), f16[8,56,256]{2,1,0:T(8,128)(2,1)S(1)}, u32[]{:S(2)}, u32[]{:S(2)}) async-start(f16[8,56,256]{2,1,0:T(8,128)(2,1)} %broadcast_in_dim.8), calls=%async_computation.5 | async-start | bytes 458752 | tf_op jit(solution)/shard_map/all_to_all | solution.py:38
  144.7 10.0 %all-to-all-done.5 = f16[8,56,256]{2,1,0:T(8,128)(2,1)S(1)} async-done(((f16[8,56,256]{2,1,0:T(8,128)(2,1)}), f16[8,56,256]{2,1,0:T(8,128)(2,1)S(1)}, u32[]{:S(2)}, u32[]{:S(2)}) %all-to-all-start.5) | async-done | bytes 229408 | tf_op jit(solution)/shard_map/all_to_all | solution.py:38
  154.7 0.7 copy.58
  155.4 4.6 %all-to-all-start.6 = ((bf16[64,4,128]{2,1,0:T(4,128)(2,1)}), bf16[64,4,128]{2,1,0:T(4,128)(2,1)S(1)}, u32[]{:S(2)}, u32[]{:S(2)}) async-start(bf16[64,4,128]{2,1,0:T(4,128)(2,1)} %copy.58), calls=%async_computation.6 | async-start | bytes 131072 | tf_op jit(solution)/shard_map/all_to_all | solution.py:198
  160.0 32.6 %all-gather.1 = f16[3584,256]{1,0:T(8,128)(2,1)} all-gather(f16[448,256]{1,0:T(8,128)(2,1)S(1)} %bitcast.58), channel_id=1, replica_groups=mesh['xl'=2,'core'=2,'y'=8,'z'=8,'xh'=2] {'y'}, dimensions={0}, use_global_device_ids=true | all-gather | bytes 2064384 | tf_op jit(solution)/shard_map/all_gather | solution.py:201
  192.6 1.9 multiply_convert_fusion
  194.6 1.5 reshape.166
  196.0 0.8 fusion.3
  (71 shorter events, 2.6 us)
Async XLA Ops:
  0.6 5.5 %copy-start = (bf16[128,3584]{1,0:T(8,128)(2,1)S(1)}, bf16[128,3584]{1,0:T(8,128)(2,1)}, u32[]{:S(2)}) copy-start(bf16[128,3584]{1,0:T(8,128)(2,1)} %param.18) | copy-start | bytes 2752516
  6.8 8.2 %copy-start.5 = (f32[56,2,128]{2,1,0:T(2,128)S(1)}, f32[56,2,128]{2,1,0:T(2,128)}, u32[]{:S(2)}) copy-start(f32[56,2,128]{2,1,0:T(2,128)} %param.21) | copy-start | bytes 172036
  8.0 38.3 %all-to-all-start = ((bf16[8,96,448]{2,1,0:T(8,128)(2,1)}), bf16[8,96,448]{2,1,0:T(8,128)(2,1)S(1)}, u32[]{:S(2)}, u32[]{:S(2)}) async-start(bf16[8,96,448]{2,1,0:T(8,128)(2,1)} %copy.51), calls=%async_computation | async-start | bytes 1572864 | tf_op jit(solution)/shard_map/all_to_all | solution.py:116
  46.2 7.1 %copy-start.11 = (s32[128]{0:T(128)S(1)}, s32[128]{0:T(128)}, u32[]{:S(2)}) copy-start(s32[128]{0:T(128)} %param.19) | copy-start | bytes 1540
  46.2 7.3 %copy-start.9 = (bf16[128,128]{1,0:T(8,128)(2,1)S(1)}, bf16[128,128]{1,0:T(8,128)(2,1)}, u32[]{:S(2)}) copy-start(bf16[128,128]{1,0:T(8,128)(2,1)} %param.20) | copy-start | bytes 98308
  46.3 20.0 %copy-start.3 = (bf16[8,64,448]{2,1,0:T(8,128)(2,1)}, bf16[8,64,448]{2,1,0:T(8,128)(2,1)S(1)}, u32[]{:S(2)}) copy-start(bf16[8,64,448]{2,1,0:T(8,128)(2,1)S(1)} %slice.30) | copy-start | bytes 1376260
  46.3 20.0 %collective-permute-start = (bf16[512,448]{1,0:T(8,128)(2,1)S(1)}, bf16[512,448]{1,0:T(8,128)(2,1)}, u32[]{:S(2)}, u32[]{:S(2)}) collective-permute-start(bf16[512,448]{1,0:T(8,128)(2,1)S(1)} %bitcast.60), channel_id=1, source_target_pairs={{0,128},{128,0},{1,129},{129,1},{2,130},{130,2},{3,131},{131,3},{4... | collective-permute-start | bytes 1376264 | tf_op jit(solution)/shard_map/ppermute | solution.py:122
  49.4 16.5 %all-to-all-start.1 = ((bf16[8,8,4,448]{3,1,2,0:T(8,128)(2,1)}), bf16[8,8,4,448]{3,1,2,0:T(8,128)(2,1)S(1)}, u32[]{:S(2)}, u32[]{:S(2)}) async-start(bf16[8,8,4,448]{3,1,2,0:T(8,128)(2,1)} %bitcast.5), calls=%async_computation.1 | async-start | bytes 524288 | tf_op jit(solution)/shard_map/all_to_all | solution.py:125
  68.7 21.1 %collective-permute-start.3 = (bf16[64,1792]{1,0:T(8,128)(2,1)S(1)}, bf16[64,1792]{1,0:T(8,128)(2,1)}, u32[]{:S(2)}, u32[]{:S(2)}) collective-permute-start(bf16[64,1792]{1,0:T(8,128)(2,1)S(1)} %reshape.157), channel_id=1, source_target_pairs={{0,257},{1,256},{256,1},{257,0},{2,259},{3,258},{258,3},{259,2},{4... | collective-permute-start | bytes 688136 | tf_op jit(solution)/shard_map/ppermute | solution.py:149
  71.1 17.0 %collective-permute-start.2 = (bf16[64,1792]{1,0:T(8,128)(2,1)S(1)}, bf16[64,1792]{1,0:T(8,128)(2,1)}, u32[]{:S(2)}, u32[]{:S(2)}) collective-permute-start(bf16[64,1792]{1,0:T(8,128)(2,1)S(1)} %reshape.157), channel_id=1, source_target_pairs={{0,256},{1,257},{256,0},{257,1},{2,258},{3,259},{258,2},{259,3},{4... | collective-permute-start | bytes 688136 | tf_op jit(solution)/shard_map/ppermute | solution.py:149
  73.9 13.5 %collective-permute-start.1 = (bf16[64,1792]{1,0:T(8,128)(2,1)S(1)}, bf16[64,1792]{1,0:T(8,128)(2,1)S(1)}, u32[]{:S(2)}, u32[]{:S(2)}) collective-permute-start(bf16[64,1792]{1,0:T(8,128)(2,1)S(1)} %reshape.157), channel_id=1, source_target_pairs={{0,1},{1,0},{256,257},{257,256},{2,3},{3,2},{258,259},{259,258},{4... | collective-permute-start | bytes 688136 | tf_op jit(solution)/shard_map/ppermute | solution.py:149
  79.1 24.1 %all-to-all-start.2 = ((f16[8,2,64,256]{3,2,1,0:T(8,128)(2,1)}), f16[8,2,64,256]{3,2,1,0:T(8,128)(2,1)S(1)}, u32[]{:S(2)}, u32[]{:S(2)}) async-start(f16[8,2,64,256]{3,2,1,0:T(8,128)(2,1)} %bitcast.51), calls=%async_computation.2 | async-start | bytes 1048576 | tf_op jit(solution)/shard_map/all_to_all | solution.py:133
  88.1 19.7 %copy-start.10 = (f32[16,8]{0,1:T(8,128)S(1)}, f32[16,8]{0,1:T(8,128)}, u32[]{:S(2)}) copy-start(f32[16,8]{0,1:T(8,128)} %param.16) | copy-start | bytes 1540
  88.1 19.9 %copy-start.1 = (bf16[1,3584,2,128]{3,2,1,0:T(2,128)(2,1)S(1)}, bf16[1,3584,2,128]{3,2,1,0:T(2,128)(2,1)}, u32[]{:S(2)}) copy-start(bf16[1,3584,2,128]{3,2,1,0:T(2,128)(2,1)} %param.17) | copy-start | bytes 5505028
  91.5 18.5 %collective-permute-start.4 = (bf16[256,1792]{1,0:T(8,128)(2,1)}, bf16[256,1792]{1,0:T(8,128)(2,1)}, u32[]{:S(2)}, u32[]{:S(2)}) collective-permute-start(bf16[256,1792]{1,0:T(8,128)(2,1)} %constant_dynamic-update-slice_fusion), channel_id=1, source_target_pairs={{0,128},{128,0},{1,129},{129,1},{2,130},{130,2},{3,131},{131,3},{4... | collective-permute-start | bytes 2752520 | tf_op jit(solution)/shard_map/ppermute | solution.py:152
  104.2 19.5 %all-to-all-start.3 = ((bf16[8,128,256]{2,1,0:T(8,128)(2,1)}), bf16[8,128,256]{2,1,0:T(8,128)(2,1)S(1)}, u32[]{:S(2)}, u32[]{:S(2)}) async-start(bf16[8,128,256]{2,1,0:T(8,128)(2,1)} %broadcast_in_dim.6), calls=%async_computation.3 | async-start | bytes 1048576 | tf_op jit(solution)/shard_map/all_to_all | solution.py:38
  110.0 13.7 %copy-start.4 = (bf16[8,64,448]{2,1,0:T(8,128)(2,1)S(1)}, bf16[8,64,448]{2,1,0:T(8,128)(2,1)}, u32[]{:S(2)}) copy-start(bf16[8,64,448]{2,1,0:T(8,128)(2,1)} %copy-done.3) | copy-start | bytes 1376260
  123.8 5.7 %copy-start.2 = (bf16[1,1792,2,128]{3,2,1,0:T(2,128)(2,1)S(1)}, bf16[1,1792,2,128]{3,2,1,0:T(2,128)(2,1)}, u32[]{:S(2)}) copy-start(bf16[1,1792,2,128]{3,2,1,0:T(2,128)(2,1)} %get-tuple-element.25) | copy-start | bytes 2752516
  126.1 13.4 %all-to-all-start.4 = ((f16[8,56,256]{2,1,0:T(8,128)(2,1)}), f16[8,56,256]{2,1,0:T(8,128)(2,1)S(1)}, u32[]{:S(2)}, u32[]{:S(2)}) async-start(f16[8,56,256]{2,1,0:T(8,128)(2,1)} %bitcast.16), calls=%async_computation.4 | async-start | bytes 458752 | tf_op jit(solution)/shard_map/all_to_all | solution.py:163
  129.5 10.2 %copy-start.6 = (f32[56,2,128]{2,1,0:T(2,128)S(1)}, f32[56,2,128]{2,1,0:T(2,128)}, u32[]{:S(2)}) copy-start(f32[56,2,128]{2,1,0:T(2,128)} %param.21) | copy-start | bytes 172036
  129.5 10.2 %copy-start.7 = (f32[56,2,128]{2,1,0:T(2,128)S(1)}, f32[56,2,128]{2,1,0:T(2,128)}, u32[]{:S(2)}) copy-start(f32[56,2,128]{2,1,0:T(2,128)} %param.22) | copy-start | bytes 172036
  129.5 10.2 %copy-start.8 = (f32[56,2,128]{2,1,0:T(2,128)S(1)}, f32[56,2,128]{2,1,0:T(2,128)}, u32[]{:S(2)}) copy-start(f32[56,2,128]{2,1,0:T(2,128)} %param.23) | copy-start | bytes 172036
  141.3 13.4 %all-to-all-start.5 = ((f16[8,56,256]{2,1,0:T(8,128)(2,1)}), f16[8,56,256]{2,1,0:T(8,128)(2,1)S(1)}, u32[]{:S(2)}, u32[]{:S(2)}) async-start(f16[8,56,256]{2,1,0:T(8,128)(2,1)} %broadcast_in_dim.8), calls=%async_computation.5 | async-start | bytes 458752 | tf_op jit(solution)/shard_map/all_to_all | solution.py:38
  155.4 37.2 %all-to-all-start.6 = ((bf16[64,4,128]{2,1,0:T(4,128)(2,1)}), bf16[64,4,128]{2,1,0:T(4,128)(2,1)S(1)}, u32[]{:S(2)}, u32[]{:S(2)}) async-start(bf16[64,4,128]{2,1,0:T(4,128)(2,1)} %copy.58), calls=%async_computation.6 | async-start | bytes 131072 | tf_op jit(solution)/shard_map/all_to_all | solution.py:198

commit v4 on v3

--- a/solution.py
+++ b/solution.py
@@ -131,6 +131,11 @@
     partial_pre = partial_pre.reshape(2, n_y, half, wide).transpose(1, 0, 2, 3)
     partial_pre, arrived = lax.optimization_barrier((partial_pre, arrived))
     pre_parts = lax.all_to_all(partial_pre, "y", split_axis=0, concat_axis=0, tiled=True)
+    pieces = [arrived] + [
+        lax.ppermute(arrived, ALONG_X, [(i, i ^ k) for i in range(CAP)]) for k in range(1, CAP)
+    ]
+    pre_parts, pieces = lax.optimization_barrier((pre_parts, pieces))
+
     projected = jnp.sum(pre_parts.astype(jnp.float32), axis=0).reshape(2 * half, wide) * (
         1.0 / pre_scale
     )
@@ -145,14 +150,10 @@
         [upstream * up_pre * slope, upstream * gate_pre * sigmoid_gate], axis=1
     ).astype(jnp.bfloat16)
 
-    pieces = [arrived] + [
-        lax.ppermute(arrived, ALONG_X, [(i, i ^ k) for i in range(CAP)]) for k in range(1, CAP)
-    ]
+    grad_all = gather_by_exchange(grad_pre, "y").reshape(n_y, 2, half, wide)
     pieces = jnp.concatenate(pieces, axis=0)
     other_pieces = lax.ppermute(pieces, "core", SWAP)
-    local_weight = expert_weight.reshape(width, wide)
-
-    grad_all = gather_by_exchange(grad_pre, "y").reshape(n_y, 2, half, wide)
+    grad_all, other_pieces = lax.optimization_barrier((grad_all, other_pieces))
     grad_all = grad_all.transpose(1, 0, 2, 3).reshape(token_slice.shape[0], wide)
     partial = to_half(
         lax.dot_general(
@@ -172,8 +173,9 @@
     correct_two = 1.0 - beta_two**adam_step
     update = new_first / correct_one / (jnp.sqrt(new_second / correct_two) + epsilon)
     new_master = master - learn_rate * (update + decay_rate * master)
-    fresh_rows = to_half(new_master.astype(jnp.bfloat16), fresh_scale)
-
+    fresh_rows = new_master.astype(jnp.bfloat16).reshape(own_rows, wide)
+
+    local_weight = expert_weight.reshape(width, wide)
     projected_rows = jnp.dot(
         jnp.where(core == 0, pieces, other_pieces),
         local_weight[:span],
@@ -192,16 +194,19 @@
         activated_rows = jnp.where(
             lax.axis_index(axis) == 1, jnp.flip(activated_rows, place), activated_rows
         )
-    activated_rows = activated_rows.transpose(3, 2, 0, 1, 4).reshape(n_y * n_z, CAP, hid_local)
-    fresh_rows = gather_by_exchange(fresh_rows.reshape(own_rows, wide), "z")
-    activated_rows, fresh_rows = lax.optimization_barrier((activated_rows, fresh_rows))
-    returned = lax.all_to_all(
-        activated_rows, ROW, split_axis=0, concat_axis=0, tiled=True
-    )
-    fresh = lax.all_gather(fresh_rows.reshape(n_z * own_rows, wide), "y", axis=0, tiled=True)
+    activated_rows = activated_rows.transpose(2, 3, 1, 0, 4).reshape(n_z, n_y * 2, wide)
+    along_z = jnp.concatenate(
+        [jnp.broadcast_to(fresh_rows[None], (n_z,) + fresh_rows.shape), activated_rows], axis=1
+    )
+    along_z = lax.all_to_all(along_z, "z", split_axis=0, concat_axis=0, tiled=True)
+    fresh_rows = to_half(along_z[:, :own_rows].reshape(n_z * own_rows, wide), fresh_scale)
+    along_y = along_z[:, own_rows:].reshape(n_z, n_y, 2, wide).transpose(1, 0, 2, 3)
+    returned = lax.all_to_all(along_y, "y", split_axis=0, concat_axis=0, tiled=True)
+    fresh = lax.all_gather(fresh_rows, "y", axis=0, tiled=True)
     returned, fresh = lax.optimization_barrier((returned, fresh))
     fresh = from_half(fresh, fresh_scale).reshape(n_y * n_z * own_rows, 2, hid_local)
-    back_slots = returned.reshape(EXPERTS * CAP, hid_local)
+    back_slots = returned.reshape(EXPERTS, 2, 2, hid_local).transpose(0, 2, 1, 3)
+    back_slots = back_slots.reshape(EXPERTS * CAP, hid_local)
     picked = jnp.dot(
         slot_table.astype(jnp.bfloat16), back_slots, preferred_element_type=jnp.float32
     )

time: 198 us -> 191 us (0.965)
  waiting for transfers between devices: 52.8 us -> 29.8 us
  blocking collectives: 63.7 us -> 79.9 us
    all_to_all x0 -> x1, blocking collectives: none -> 16.3 us  [shards(): lax.all_to_all(along_z, 'z', split_axis=0, concat_axis=0, tiled=True)]
    all_to_all x2 -> x1, waiting for transfers between devices: 22 us -> 6.11 us  [gather_by_exchange(): lax.all_to_all(jnp.broadcast_to(block[None], (count,) + block.shape), axi...]
    all_to_all x1, waiting for transfers between devices: 9.81 us -> 0.01 us  [shards(): lax.all_to_all(partial_pre, 'y', split_axis=0, concat_axis=0, tiled=True)]
    ppermute x3, waiting for transfers between devices: 0.3 us -> 7.19 us  [shards(): lax.ppermute(arrived, ALONG_X, [(i, i ^ k) for i in range(CAP)])]
    all_to_all x1 -> x0, starting transfers between devices: 4.62 us -> none  [shards(): lax.all_to_all(activated_rows, ROW, split_axis=0, concat_axis=0, tiled=True)]
    all_to_all x1 -> x2, starting transfers between devices: 7.1 us -> 11.2 us  [shards(): lax.all_to_all(along_y, 'y', split_axis=0, concat_axis=0, tiled=True)]
    all_to_all x1, waiting for transfers between devices: 8.27 us -> 5.95 us  [shards(): lax.all_to_all(partial.reshape(n_z, own_rows, wide), 'z', split_axis=0, c...]
    unnamed x31 -> x38, local copies, waits for them, and re-layouts: 4.1 us -> 6.27 us
  transfers between devices with their start and end apart: 12 -> 11, of which waited for: 6 -> 5; matrix products, arithmetic and copies ran while one was open for 7% -> 7% of each run, Pallas kernels for 0% -> 0%
where the time goes in v4:
time: 191 us; the launch traced here: 190 us
  blocking collectives  79.9 us (42%)
  starting transfers between devices  46.4 us (24%)
  waiting for transfers between devices  29.8 us (16%)
  local copies, waits for them, and re-layouts  20.1 us (11%)
  matrix products  7.67 us (4%)
  other arithmetic  4.84 us (3%)
    all_gather x1, blocking collectives, shards(): fresh = lax.all_gather(fresh_rows, 'y', axis=0, tiled=True)  32.4 us
    all_gather x1, blocking collectives, shards(): lax.all_gather(master.astype(jnp.bfloat16).reshape(own_rows, wide), 'z',...  31.1 us
    all_to_all x1, blocking collectives, shards(): lax.all_to_all(along_z, 'z', split_axis=0, concat_axis=0, tiled=True)  16.3 us
    all_to_all x2, starting transfers between devices, shards(): lax.all_to_all(along_y, 'y', split_axis=0, concat_axis=0, tiled=True)  11.2 us
    all_to_all x1, waiting for transfers between devices, shards(): lax.all_to_all(along_z, 'z', split_axis=0, concat_axis=0, tiled=True)  10.6 us
    ppermute x3, starting transfers between devices, shards(): lax.ppermute(arrived, ALONG_X, [(i, i ^ k) for i in range(CAP)])  10.4 us
    all_to_all x1, starting transfers between devices, shards(): lax.all_to_all(partial_pre, 'y', split_axis=0, concat_axis=0, tiled=True)  7.2 us
    ppermute x3, waiting for transfers between devices, shards(): lax.ppermute(arrived, ALONG_X, [(i, i ^ k) for i in range(CAP)])  7.19 us
  transfers between devices with their start and end apart: 11, of which 5 were waited for; matrix products, arithmetic and copies ran while one was open for 7% of the time, Pallas kernels for 0%

profile of v4, /device:TPU:6, one launch (start us, length us, event | category | flops | bytes accessed | tf_op | source)
XLA Modules:
  0.0 189.9 jit_solution(14767720171119415153)
XLA Ops:
  0.7 0.8 eq.76
  1.5 0.8 copy.66
  2.9 0.9 reshape.158
  3.8 0.4 multiply_reduce_fusion
  4.4 0.8 dynamic-slice.8
  5.4 0.3 convolution_convert_fusion
  5.6 0.3 reshape.160
  6.1 0.6 reshape.157
  6.9 1.1 copy.69
  8.0 7.1 %all-to-all-start = ((bf16[8,96,448]{2,1,0:T(8,128)(2,1)}), bf16[8,96,448]{2,1,0:T(8,128)(2,1)S(1)}, u32[]{:S(2)}, u32[]{:S(2)}) async-start(bf16[8,96,448]{2,1,0:T(8,128)(2,1)} %copy.69), calls=%async_computation | async-start | bytes 1572864 | tf_op jit(solution)/shard_map/all_to_all | solution.py:116
  15.1 31.1 %all_gather.6 = bf16[448,256]{1,0:T(8,128)(2,1)S(1)} all-gather(bf16[56,256]{1,0:T(8,128)(2,1)S(1)} %bitcast.75), channel_id=1, replica_groups=mesh['xl'=2,'core'=2,'y'=8,'z'=8,'xh'=2] {'z'}, dimensions={0}, use_global_device_ids=true | all-gather | bytes 258048 | tf_op jit(solution)/shard_map/all_gather | solution.py:117
  46.3 1.9 %collective-permute-start = (bf16[512,448]{1,0:T(8,128)(2,1)S(1)}, bf16[512,448]{1,0:T(8,128)(2,1)S(1)}, u32[]{:S(2)}, u32[]{:S(2)}) collective-permute-start(bf16[512,448]{1,0:T(8,128)(2,1)S(1)} %bitcast.69), channel_id=1, source_target_pairs={{0,128},{128,0},{1,129},{129,1},{2,130},{130,2},{3,131},{131,3},{4... | collective-permute-start | bytes 1376264 | tf_op jit(solution)/shard_map/ppermute | solution.py:122
  48.2 0.4 copy.71
  48.7 16.3 %all_to_all.35 = bf16[8,8,4,448]{3,1,2,0:T(8,128)(2,1)S(1)} all-to-all(bf16[8,8,4,448]{3,1,2,0:T(8,128)(2,1)S(1)} %bitcast.62), channel_id=1, replica_groups=mesh['xl'=2,'core'=2,'y'=8,'z'=8,'xh'=2] {'z'}, dimensions={0} | all-to-all | bytes 458752 | tf_op jit(solution)/shard_map/all_to_all | solution.py:125
  65.4 0.4 fusion
  65.9 0.9 copy.102
  66.8 7.2 %all-to-all-start.2 = ((f16[8,2,64,256]{3,2,1,0:T(8,128)(2,1)}), f16[8,2,64,256]{3,2,1,0:T(8,128)(2,1)S(1)}, u32[]{:S(2)}, u32[]{:S(2)}) async-start(f16[8,2,64,256]{3,2,1,0:T(8,128)(2,1)} %bitcast.57), calls=%async_computation.2 | async-start | bytes 1048576 | tf_op jit(solution)/shard_map/all_to_all | solution.py:133
  74.0 2.4 %collective-permute-start.3 = (bf16[64,1792]{1,0:T(8,128)(2,1)S(1)}, bf16[64,1792]{1,0:T(8,128)(2,1)S(1)}, u32[]{:S(2)}, u32[]{:S(2)}) collective-permute-start(bf16[64,1792]{1,0:T(8,128)(2,1)S(1)} %reshape.165), channel_id=1, source_target_pairs={{0,257},{1,256},{256,1},{257,0},{2,259},{3,258},{258,3},{259,2},{4... | collective-permute-start | bytes 688136 | tf_op jit(solution)/shard_map/ppermute | solution.py:135
  76.4 2.8 %collective-permute-start.2 = (bf16[64,1792]{1,0:T(8,128)(2,1)S(1)}, bf16[64,1792]{1,0:T(8,128)(2,1)S(1)}, u32[]{:S(2)}, u32[]{:S(2)}) collective-permute-start(bf16[64,1792]{1,0:T(8,128)(2,1)S(1)} %reshape.165), channel_id=1, source_target_pairs={{0,256},{1,257},{256,0},{257,1},{2,258},{3,259},{258,2},{259,3},{4... | collective-permute-start | bytes 688136 | tf_op jit(solution)/shard_map/ppermute | solution.py:135
  79.2 5.3 %collective-permute-start.1 = (bf16[64,1792]{1,0:T(8,128)(2,1)S(1)}, bf16[64,1792]{1,0:T(8,128)(2,1)}, u32[]{:S(2)}, u32[]{:S(2)}) collective-permute-start(bf16[64,1792]{1,0:T(8,128)(2,1)S(1)} %reshape.165), channel_id=1, source_target_pairs={{0,1},{1,0},{256,257},{257,256},{2,3},{3,2},{258,259},{259,258},{4... | collective-permute-start | bytes 688136 | tf_op jit(solution)/shard_map/ppermute | solution.py:135
  84.7 2.0 %collective-permute-done.2 = bf16[64,1792]{1,0:T(8,128)(2,1)S(1)} collective-permute-done((bf16[64,1792]{1,0:T(8,128)(2,1)S(1)}, bf16[64,1792]{1,0:T(8,128)(2,1)S(1)}, u32[]{:S(2)}, u32[]{:S(2)}) %collective-permute-start.2) | collective-permute-done | bytes 229408 | tf_op jit(solution)/shard_map/ppermute | solution.py:135
  86.6 0.7 copy-done.6
  87.3 5.2 %collective-permute-done.1 = bf16[64,1792]{1,0:T(8,128)(2,1)} collective-permute-done((bf16[64,1792]{1,0:T(8,128)(2,1)S(1)}, bf16[64,1792]{1,0:T(8,128)(2,1)}, u32[]{:S(2)}, u32[]{:S(2)}) %collective-permute-start.1) | collective-permute-done | bytes 229408 | tf_op jit(solution)/shard_map/ppermute | solution.py:135
  92.7 0.8 broadcast_in_dim.6
  93.6 6.9 %all-to-all-start.3 = ((bf16[8,128,256]{2,1,0:T(8,128)(2,1)}), bf16[8,128,256]{2,1,0:T(8,128)(2,1)S(1)}, u32[]{:S(2)}, u32[]{:S(2)}) async-start(bf16[8,128,256]{2,1,0:T(8,128)(2,1)} %broadcast_in_dim.6), calls=%async_computation.3 | async-start | bytes 1048576 | tf_op jit(solution)/shard_map/all_to_all | solution.py:38
  100.5 0.7 constant_dynamic-update-slice_fusion.3
  101.2 1.6 constant_dynamic-update-slice_fusion.2
  102.8 1.6 constant_dynamic-update-slice_fusion.1
  104.5 1.7 constant_dynamic-update-slice_fusion
  106.1 1.9 %collective-permute-start.4 = (bf16[256,1792]{1,0:T(8,128)(2,1)}, bf16[256,1792]{1,0:T(8,128)(2,1)}, u32[]{:S(2)}, u32[]{:S(2)}) collective-permute-start(bf16[256,1792]{1,0:T(8,128)(2,1)} %constant_dynamic-update-slice_fusion), channel_id=1, source_target_pairs={{0,128},{128,0},{1,129},{129,1},{2,130},{130,2},{3,131},{131,3},{4... | collective-permute-start | bytes 2752520 | tf_op jit(solution)/shard_map/ppermute | solution.py:155
  108.1 2.2 %fusion.32 = (bf16[1,1792,2,128]{3,2,1,0:T(2,128)(2,1)}, bf16[1,1792,2,128]{3,2,1,0:T(2,128)(2,1)}) fusion(bf16[1,3584,2,128]{3,2,1,0:T(2,128)(2,1)S(1)} %copy-done.1), kind=kLoop, calls=%fused_computation.84 | loop fusion | bytes 3670016 | tf_op jit(solution)/shard_map/slice | solution.py:181
  110.3 6.1 %all-to-all-done.3 = bf16[8,128,256]{2,1,0:T(8,128)(2,1)S(1)} async-done(((bf16[8,128,256]{2,1,0:T(8,128)(2,1)}), bf16[8,128,256]{2,1,0:T(8,128)(2,1)S(1)}, u32[]{:S(2)}, u32[]{:S(2)}) %all-to-all-start.3) | async-done | bytes 524320 | tf_op jit(solution)/shard_map/all_to_all | solution.py:38
  116.5 2.5 %fusion.1 = f16[448,256]{1,0:T(8,128)(2,1)} fusion(bf16[1024,256]{1,0:T(8,128)(2,1)S(1)} %bitcast.72, bf16[512,448]{1,0:T(8,128)(2,1)} %copy-done.13, bf16[512,448]{1,0:T(8,128)(2,1)} %bitcast.71), kind=kOutput, calls=%fused_computation.5 | convolution fusion | flops 236945408 | bytes 1671168 | tf_op jit(solution)/shard_map/dot_general | solution.py:159
  118.9 3.4 %all-to-all-start.4 = ((f16[8,56,256]{2,1,0:T(8,128)(2,1)}), f16[8,56,256]{2,1,0:T(8,128)(2,1)S(1)}, u32[]{:S(2)}, u32[]{:S(2)}) async-start(f16[8,56,256]{2,1,0:T(8,128)(2,1)} %bitcast.13), calls=%async_computation.4 | async-start | bytes 458752 | tf_op jit(solution)/shard_map/all_to_all | solution.py:164
  122.4 1.7 fusion.4
  124.1 1.6 convolution_add_fusion
  125.9 0.3 rev.8
  126.4 5.9 %all-to-all-done.4 = f16[8,56,256]{2,1,0:T(8,128)(2,1)S(1)} async-done(((f16[8,56,256]{2,1,0:T(8,128)(2,1)}), f16[8,56,256]{2,1,0:T(8,128)(2,1)S(1)}, u32[]{:S(2)}, u32[]{:S(2)}) %all-to-all-start.4) | async-done | bytes 229408 | tf_op jit(solution)/shard_map/all_to_all | solution.py:164
  132.6 0.8 fusion.31
  133.4 0.7 pad_maximum_fusion.4
  134.1 3.4 %all-to-all-start.5 = ((bf16[8,72,256]{2,1,0:T(8,128)(2,1)}), bf16[8,72,256]{2,1,0:T(8,128)(2,1)S(1)}, u32[]{:S(2)}, u32[]{:S(2)}) async-start(bf16[8,72,256]{2,1,0:T(8,128)(2,1)} %pad_maximum_fusion.4), calls=%async_computation.5 | async-start | bytes 589824 | tf_op jit(solution)/shard_map/all_to_all | solution.py:201
  137.8 10.6 %all-to-all-done.5 = bf16[8,72,256]{2,1,0:T(8,128)(2,1)S(1)} async-done(((bf16[8,72,256]{2,1,0:T(8,128)(2,1)}), bf16[8,72,256]{2,1,0:T(8,128)(2,1)S(1)}, u32[]{:S(2)}, u32[]{:S(2)}) %all-to-all-start.5) | async-done | bytes 294944 | tf_op jit(solution)/shard_map/all_to_all | solution.py:201
  148.3 0.7 copy.81
  149.0 4.1 %all-to-all-start.6 = ((bf16[8,8,2,256]{3,1,2,0:T(8,128)(2,1)}), bf16[8,8,2,256]{3,1,2,0:T(8,128)(2,1)S(1)}, u32[]{:S(2)}, u32[]{:S(2)}) async-start(bf16[8,8,2,256]{3,1,2,0:T(8,128)(2,1)} %bitcast.17), calls=%async_computation.6 | async-start | bytes 131072 | tf_op jit(solution)/shard_map/all_to_all | solution.py:204
  153.2 32.4 %all-gather.1 = f16[3584,256]{1,0:T(8,128)(2,1)} all-gather(f16[448,256]{1,0:T(8,128)(2,1)S(1)} %bitcast.65), channel_id=1, replica_groups=mesh['xl'=2,'core'=2,'y'=8,'z'=8,'xh'=2] {'y'}, dimensions={0}, use_global_device_ids=true | all-gather | bytes 2064384 | tf_op jit(solution)/shard_map/all_gather | solution.py:205
  185.7 1.9 %multiply_convert_fusion = bf16[3584,256]{1,0:T(8,128)(2,1)S(1)} fusion(f16[3584,256]{1,0:T(8,128)(2,1)} %all-gather.1), kind=kLoop, calls=%fused_computation | loop fusion | flops 2752512 | bytes 3670016 | tf_op jit(solution)/shard_map/convert_element_type | solution.py:33
  187.6 1.5 reshape.175
  189.1 0.8 fusion.3
  (84 shorter events, 3.0 us)
Async XLA Ops:
  0.6 5.5 %copy-start = (bf16[128,3584]{1,0:T(8,128)(2,1)S(1)}, bf16[128,3584]{1,0:T(8,128)(2,1)}, u32[]{:S(2)}) copy-start(bf16[128,3584]{1,0:T(8,128)(2,1)} %param.18) | copy-start | bytes 2752516
  6.9 8.2 %copy-start.7 = (f32[56,2,128]{2,1,0:T(2,128)S(1)}, f32[56,2,128]{2,1,0:T(2,128)}, u32[]{:S(2)}) copy-start(f32[56,2,128]{2,1,0:T(2,128)} %param.21) | copy-start | bytes 172036
  8.0 38.2 %all-to-all-start = ((bf16[8,96,448]{2,1,0:T(8,128)(2,1)}), bf16[8,96,448]{2,1,0:T(8,128)(2,1)S(1)}, u32[]{:S(2)}, u32[]{:S(2)}) async-start(bf16[8,96,448]{2,1,0:T(8,128)(2,1)} %copy.69), calls=%async_computation | async-start | bytes 1572864 | tf_op jit(solution)/shard_map/all_to_all | solution.py:116
  46.3 19.6 %copy-start.4 = (bf16[8,64,448]{2,1,0:T(8,128)(2,1)}, bf16[8,64,448]{2,1,0:T(8,128)(2,1)S(1)}, u32[]{:S(2)}) copy-start(bf16[8,64,448]{2,1,0:T(8,128)(2,1)S(1)} %slice.36) | copy-start | bytes 1376260
  46.3 19.1 %collective-permute-start = (bf16[512,448]{1,0:T(8,128)(2,1)S(1)}, bf16[512,448]{1,0:T(8,128)(2,1)S(1)}, u32[]{:S(2)}, u32[]{:S(2)}) collective-permute-start(bf16[512,448]{1,0:T(8,128)(2,1)S(1)} %bitcast.69), channel_id=1, source_target_pairs={{0,128},{128,0},{1,129},{129,1},{2,130},{130,2},{3,131},{131,3},{4... | collective-permute-start | bytes 1376264 | tf_op jit(solution)/shard_map/ppermute | solution.py:122
  65.4 8.6 %copy-start.14 = (s32[128]{0:T(128)S(1)}, s32[128]{0:T(128)}, u32[]{:S(2)}) copy-start(s32[128]{0:T(128)} %param.19) | copy-start | bytes 1540
  65.4 19.2 %copy-start.11 = (bf16[128,128]{1,0:T(8,128)(2,1)S(1)}, bf16[128,128]{1,0:T(8,128)(2,1)}, u32[]{:S(2)}) copy-start(bf16[128,128]{1,0:T(8,128)(2,1)} %param.20) | copy-start | bytes 98308
  65.4 1.4 copy-start.13
  66.8 25.7 %all-to-all-start.2 = ((f16[8,2,64,256]{3,2,1,0:T(8,128)(2,1)}), f16[8,2,64,256]{3,2,1,0:T(8,128)(2,1)S(1)}, u32[]{:S(2)}, u32[]{:S(2)}) async-start(f16[8,2,64,256]{3,2,1,0:T(8,128)(2,1)} %bitcast.57), calls=%async_computation.2 | async-start | bytes 1048576 | tf_op jit(solution)/shard_map/all_to_all | solution.py:133
  74.0 10.6 %collective-permute-start.3 = (bf16[64,1792]{1,0:T(8,128)(2,1)S(1)}, bf16[64,1792]{1,0:T(8,128)(2,1)S(1)}, u32[]{:S(2)}, u32[]{:S(2)}) collective-permute-start(bf16[64,1792]{1,0:T(8,128)(2,1)S(1)} %reshape.165), channel_id=1, source_target_pairs={{0,257},{1,256},{256,1},{257,0},{2,259},{3,258},{258,3},{259,2},{4... | collective-permute-start | bytes 688136 | tf_op jit(solution)/shard_map/ppermute | solution.py:135
  76.4 10.2 %collective-permute-start.2 = (bf16[64,1792]{1,0:T(8,128)(2,1)S(1)}, bf16[64,1792]{1,0:T(8,128)(2,1)S(1)}, u32[]{:S(2)}, u32[]{:S(2)}) collective-permute-start(bf16[64,1792]{1,0:T(8,128)(2,1)S(1)} %reshape.165), channel_id=1, source_target_pairs={{0,256},{1,257},{256,0},{257,1},{2,258},{3,259},{258,2},{259,3},{4... | collective-permute-start | bytes 688136 | tf_op jit(solution)/shard_map/ppermute | solution.py:135
  79.2 13.3 %collective-permute-start.1 = (bf16[64,1792]{1,0:T(8,128)(2,1)S(1)}, bf16[64,1792]{1,0:T(8,128)(2,1)}, u32[]{:S(2)}, u32[]{:S(2)}) collective-permute-start(bf16[64,1792]{1,0:T(8,128)(2,1)S(1)} %reshape.165), channel_id=1, source_target_pairs={{0,1},{1,0},{256,257},{257,256},{2,3},{3,2},{258,259},{259,258},{4... | collective-permute-start | bytes 688136 | tf_op jit(solution)/shard_map/ppermute | solution.py:135
  84.6 2.0 %copy-start.5 = (bf16[64,1792]{1,0:T(8,128)(2,1)}, bf16[64,1792]{1,0:T(8,128)(2,1)S(1)}, u32[]{:S(2)}) copy-start(bf16[64,1792]{1,0:T(8,128)(2,1)S(1)} %collective-permute-done.3) | copy-start | bytes 688132
  86.6 0.7 copy-start.6
  92.7 15.4 %copy-start.1 = (bf16[1,3584,2,128]{3,2,1,0:T(2,128)(2,1)S(1)}, bf16[1,3584,2,128]{3,2,1,0:T(2,128)(2,1)}, u32[]{:S(2)}) copy-start(bf16[1,3584,2,128]{3,2,1,0:T(2,128)(2,1)} %param.17) | copy-start | bytes 5505028
  93.6 22.9 %all-to-all-start.3 = ((bf16[8,128,256]{2,1,0:T(8,128)(2,1)}), bf16[8,128,256]{2,1,0:T(8,128)(2,1)S(1)}, u32[]{:S(2)}, u32[]{:S(2)}) async-start(bf16[8,128,256]{2,1,0:T(8,128)(2,1)} %broadcast_in_dim.6), calls=%async_computation.3 | async-start | bytes 1048576 | tf_op jit(solution)/shard_map/all_to_all | solution.py:38
  106.1 10.3 %collective-permute-start.4 = (bf16[256,1792]{1,0:T(8,128)(2,1)}, bf16[256,1792]{1,0:T(8,128)(2,1)}, u32[]{:S(2)}, u32[]{:S(2)}) collective-permute-start(bf16[256,1792]{1,0:T(8,128)(2,1)} %constant_dynamic-update-slice_fusion), channel_id=1, source_target_pairs={{0,128},{128,0},{1,129},{129,1},{2,130},{130,2},{3,131},{131,3},{4... | collective-permute-start | bytes 2752520 | tf_op jit(solution)/shard_map/ppermute | solution.py:155
  116.5 5.9 %copy-start.3 = (bf16[1,1792,2,128]{3,2,1,0:T(2,128)(2,1)S(1)}, bf16[1,1792,2,128]{3,2,1,0:T(2,128)(2,1)}, u32[]{:S(2)}) copy-start(bf16[1,1792,2,128]{3,2,1,0:T(2,128)(2,1)} %get-tuple-element.36) | copy-start | bytes 2752516
  118.9 13.4 %all-to-all-start.4 = ((f16[8,56,256]{2,1,0:T(8,128)(2,1)}), f16[8,56,256]{2,1,0:T(8,128)(2,1)S(1)}, u32[]{:S(2)}, u32[]{:S(2)}) async-start(f16[8,56,256]{2,1,0:T(8,128)(2,1)} %bitcast.13), calls=%async_computation.4 | async-start | bytes 458752 | tf_op jit(solution)/shard_map/all_to_all | solution.py:164
  122.3 1.7 copy-start.2
  124.1 8.5 %copy-start.8 = (f32[56,2,128]{2,1,0:T(2,128)S(1)}, f32[56,2,128]{2,1,0:T(2,128)}, u32[]{:S(2)}) copy-start(f32[56,2,128]{2,1,0:T(2,128)} %param.21) | copy-start | bytes 172036
  124.1 8.5 %copy-start.9 = (f32[56,2,128]{2,1,0:T(2,128)S(1)}, f32[56,2,128]{2,1,0:T(2,128)}, u32[]{:S(2)}) copy-start(f32[56,2,128]{2,1,0:T(2,128)} %param.22) | copy-start | bytes 172036
  124.1 8.5 %copy-start.10 = (f32[56,2,128]{2,1,0:T(2,128)S(1)}, f32[56,2,128]{2,1,0:T(2,128)}, u32[]{:S(2)}) copy-start(f32[56,2,128]{2,1,0:T(2,128)} %param.23) | copy-start | bytes 172036
  125.8 11.8 %copy-start.12 = (f32[16,8]{0,1:T(8,128)S(1)}, f32[16,8]{0,1:T(8,128)}, u32[]{:S(2)}) copy-start(f32[16,8]{0,1:T(8,128)} %param.16) | copy-start | bytes 1540
  134.1 14.2 %all-to-all-start.5 = ((bf16[8,72,256]{2,1,0:T(8,128)(2,1)}), bf16[8,72,256]{2,1,0:T(8,128)(2,1)S(1)}, u32[]{:S(2)}, u32[]{:S(2)}) async-start(bf16[8,72,256]{2,1,0:T(8,128)(2,1)} %pad_maximum_fusion.4), calls=%async_computation.5 | async-start | bytes 589824 | tf_op jit(solution)/shard_map/all_to_all | solution.py:201
  149.0 36.6 %all-to-all-start.6 = ((bf16[8,8,2,256]{3,1,2,0:T(8,128)(2,1)}), bf16[8,8,2,256]{3,1,2,0:T(8,128)(2,1)S(1)}, u32[]{:S(2)}, u32[]{:S(2)}) async-start(bf16[8,8,2,256]{3,1,2,0:T(8,128)(2,1)} %bitcast.17), calls=%async_computation.6 | async-start | bytes 131072 | tf_op jit(solution)/shard_map/all_to_all | solution.py:204

commit v5 on v4

v5 whole, which is shorter than its diff:
```python
import jax
import jax.numpy as jnp
from jax import lax
from jax.experimental import pallas as pl
from jax.experimental.pallas import tpu as pltpu
from jax.sharding import Mesh, PartitionSpec as P

EXPERTS = 64
TOP = 8
BEAMS = 4
CAP = 4

beta_one = 0.9
beta_two = 0.95
learn_rate = 0.01
decay_rate = 0.1
epsilon = 1e-08
norm_epsilon = 1e-06
adam_step = 10.0

ROW = ("y", "z")
COLUMN = ("xl", "core", "xh")
ALONG_X = ("xl", "xh")
SWAP = [(0, 1), (1, 0)]
pre_scale = 2.0**7
fresh_scale = 2.0**16


def to_half(values, scale):
    return (values.astype(jnp.float32) * scale).astype(jnp.float16)


def from_half(values, scale):
    return (values.astype(jnp.float32) * (1.0 / scale)).astype(jnp.bfloat16)


def gather_by_exchange(block, axis):
    count = lax.axis_size(axis)
    return lax.all_to_all(
        jnp.broadcast_to(block[None], (count,) + block.shape), axis, 0, 0, tiled=True
    )


def stack_kernel(*refs):
    blocks, stacked = refs[:-1], refs[-1]
    rows = blocks[0].shape[0]
    for k, block in enumerate(blocks):
        stacked[k * rows : (k + 1) * rows] = block[...]


def stack_rows(blocks):
    rows, columns = blocks[0].shape
    count = len(blocks)
    return pl.pallas_call(
        stack_kernel,
        out_shape=jax.ShapeDtypeStruct((count * rows, columns), blocks[0].dtype),
        in_specs=[pl.BlockSpec(memory_space=pltpu.VMEM)] * count,
        out_specs=pl.BlockSpec(memory_space=pltpu.VMEM),
        compiler_params=pltpu.CompilerParams(vmem_limit_bytes=16 * 1024 * 1024),
        name="stack_rows",
        cost_estimate=pl.CostEstimate(
            flops=0, bytes_accessed=4 * count * rows * columns, transcendentals=0
        ),
    )(*blocks)


def route_kernel(hidden_ref, beam_ref, gain_ref, ids_ref, out_ref):
    rows, width = hidden_ref.shape
    core = lax.axis_index("core")
    slot = (lax.axis_index("xl") * 2 + lax.axis_index("xh")).astype(jnp.float32)
    hidden = hidden_ref[...].astype(jnp.float32)
    mean_square = jnp.mean(hidden * hidden, axis=1, keepdims=True)
    normed = (hidden * lax.rsqrt(mean_square + norm_epsilon) * gain_ref[...]).astype(jnp.bfloat16)
    ids = ids_ref[...]
    expert = lax.broadcasted_iota(jnp.int32, (EXPERTS, rows), 0)
    named = jnp.zeros((EXPERTS, rows), jnp.float32)
    for k in range(TOP):
        named = named + (expert == ids[k : k + 1, :]).astype(jnp.float32)
    first = lax.broadcasted_iota(jnp.int32, (rows, rows), 0)
    second = lax.broadcasted_iota(jnp.int32, (rows, rows), 1)
    earlier = jnp.dot(
        named, (first < second).astype(jnp.float32), preferred_element_type=jnp.float32
    )
    sends = jnp.where(earlier == slot, named, 0.0)
    parent = second - (second & (BEAMS - 1)) + beam_ref[...]
    source = (first == parent).astype(jnp.float32)
    table = lax.dot_general(
        sends, source, (((1,), (1,)), ((), ())), preferred_element_type=jnp.float32
    ).astype(jnp.bfloat16)

    @pl.when(core == 0)
    def _():
        out_ref[...] = jnp.dot(
            table, normed[:, : width // 2], preferred_element_type=jnp.float32
        ).astype(jnp.bfloat16)

    @pl.when(core != 0)
    def _():
        out_ref[...] = jnp.dot(
            table, normed[:, width // 2 :], preferred_element_type=jnp.float32
        ).astype(jnp.bfloat16)


def route_rows(hidden_rows, parent_beam, norm_gain, route_ids):
    rows, width = hidden_rows.shape
    return pl.pallas_call(
        route_kernel,
        out_shape=jax.ShapeDtypeStruct((EXPERTS, width // 2), jnp.bfloat16),
        in_specs=[pl.BlockSpec(memory_space=pltpu.VMEM)] * 4,
        out_specs=pl.BlockSpec(memory_space=pltpu.VMEM),
        compiler_params=pltpu.CompilerParams(vmem_limit_bytes=16 * 1024 * 1024),
        name="route_rows",
        cost_estimate=pl.CostEstimate(
            flops=2 * EXPERTS * rows * width, bytes_accessed=1 << 19, transcendentals=rows
        ),
    )(hidden_rows, parent_beam.reshape(1, rows), norm_gain.reshape(1, width), route_ids.T)


def shards(
    hidden_rows,
    parent_beam,
    norm_gain,
    route_ids,
    route_weight,
    expert_weight,
    learn_tokens,
    learn_live,
    cotangent,
    master,
    first_moment,
    second_moment,
):
    hid_local = master.shape[2]
    own_rows = master.shape[0]
    wide = 2 * hid_local
    n_y, n_z = lax.axis_size("y"), lax.axis_size("z")

    half = learn_tokens.shape[0] // 2
    core = lax.axis_index("core")

    def own_first(block):
        return jnp.concatenate(
            [
                lax.dynamic_slice_in_dim(block, core * half, half, 0),
                lax.dynamic_slice_in_dim(block, (1 - core) * half, half, 0),
            ],
            axis=0,
        )

    rows_dev, width = hidden_rows.shape
    flat_ids = route_ids.reshape(rows_dev * TOP)
    onehot = (flat_ids[:, None] == jnp.arange(EXPERTS, dtype=jnp.int32)[None, :]).astype(jnp.int32)
    earlier = jnp.cumsum(onehot, axis=0) - onehot
    position = jnp.sum(earlier * onehot, axis=1)
    slot_index = flat_ids * CAP + position
    slot_table = (
        slot_index[:, None] == jnp.arange(EXPERTS * CAP, dtype=jnp.int32)[None, :]
    ).astype(jnp.float32)
    span = width // 2
    outgoing = route_rows(hidden_rows, parent_beam, norm_gain, route_ids)
    features = width // n_y
    chunks = span // features
    tokens_half = lax.dynamic_slice_in_dim(learn_tokens, core * half, half, 0)
    along_y = jnp.concatenate(
        [
            tokens_half.reshape(half, n_y, features).transpose(1, 0, 2),
            outgoing.reshape(n_y, n_z * chunks, features),
        ],
        axis=1,
    )
    along_y = lax.all_to_all(along_y, "y", split_axis=0, concat_axis=0, tiled=True)
    local_weight = expert_weight.reshape(width, wide)
    along_y, local_weight = lax.optimization_barrier((along_y, local_weight))
    own_slice = along_y[:, :half]
    other_slice = lax.ppermute(own_slice, "core", SWAP)
    token_slice = jnp.concatenate([own_slice, other_slice], axis=1)
    token_slice = token_slice.reshape(n_y * 2 * half, features)
    lanes = 2 * wide
    tall = n_z * chunks
    routed = along_y[:, half:].reshape(n_y, n_z, chunks, features).transpose(1, 0, 2, 3)
    routed = jnp.pad(
        routed.reshape(n_z, n_y * chunks, features), ((0, 0), (0, 0), (0, lanes - features))
    )
    low = master.astype(jnp.bfloat16).reshape(own_rows, wide)
    low = jnp.concatenate(
        [low[:tall], jnp.pad(low[tall:], ((0, 2 * tall - own_rows), (0, 0)))], axis=1
    )
    along_z = jnp.concatenate([routed, jnp.broadcast_to(low[None], (n_z,) + low.shape)], axis=1)
    along_z = lax.all_to_all(along_z, "z", split_axis=0, concat_axis=0, tiled=True)
    arrived = along_z[:, : n_y * chunks, :features].reshape(n_z * n_y, span)
    weights = jnp.concatenate(
        [
            along_z[:, n_y * chunks :, :wide],
            along_z[:, n_y * chunks : n_y * chunks + own_rows - tall, wide:],
        ],
        axis=1,
    ).reshape(n_z * own_rows, wide)

    partial_pre = to_half(
        jnp.dot(token_slice, weights, preferred_element_type=jnp.float32), pre_scale
    )
    partial_pre = partial_pre.reshape(n_y, 2 * half, wide)
    pre_parts = lax.all_to_all(partial_pre, "y", split_axis=0, concat_axis=0, tiled=True)
    pieces = [arrived] + [
        lax.ppermute(arrived, ALONG_X, [(i, i ^ k) for i in range(CAP)]) for k in range(1, CAP)
    ]
    projected = jnp.sum(pre_parts.astype(jnp.float32), axis=0) * (1.0 / pre_scale)
    gate_pre = projected[:, :hid_local]
    up_pre = projected[:, hid_local:]
    sigmoid_gate = jax.nn.sigmoid(gate_pre)
    upstream = own_first(cotangent).astype(jnp.float32) * own_first(
        learn_live.astype(jnp.float32)[:, None]
    )
    slope = sigmoid_gate * (1.0 + gate_pre * (1.0 - sigmoid_gate))
    grad_pre = jnp.concatenate(
        [upstream * up_pre * slope, upstream * gate_pre * sigmoid_gate], axis=1
    ).astype(jnp.bfloat16)

    grad_all = gather_by_exchange(grad_pre, "y").reshape(token_slice.shape[0], wide)
    pieces, _ = lax.optimization_barrier((pieces, grad_pre))
    pieces = stack_rows(pieces)
    other_pieces = lax.ppermute(pieces, "core", SWAP)
    projected_rows = jnp.dot(
        jnp.where(core == 0, pieces, other_pieces),
        local_weight[:span],
        preferred_element_type=jnp.float32,
    ) + jnp.dot(
        jnp.where(core == 0, other_pieces, pieces),
        local_weight[span:],
        preferred_element_type=jnp.float32,
    )
    gate_rows = projected_rows[:, :hid_local]
    activated_rows = (
        gate_rows * jax.nn.sigmoid(gate_rows) * projected_rows[:, hid_local:]
    ).astype(jnp.bfloat16)
    activated_rows = activated_rows.reshape(2, 2, n_z, n_y, hid_local)
    for place, axis in enumerate(ALONG_X):
        activated_rows = jnp.where(
            lax.axis_index(axis) == 1, jnp.flip(activated_rows, place), activated_rows
        )
    activated_rows = activated_rows.transpose(2, 3, 1, 0, 4).reshape(n_z, n_y * 2, wide)
    grad_all, activated_rows = lax.optimization_barrier((grad_all, activated_rows))
    partial = lax.dot_general(
        token_slice, grad_all, (((0,), (0,)), ((), ())), preferred_element_type=jnp.float32
    ).astype(jnp.bfloat16)
    along_z = jnp.concatenate([partial.reshape(n_z, own_rows, wide), activated_rows], axis=1)
    along_z = lax.all_to_all(along_z, "z", split_axis=0, concat_axis=0, tiled=True)
    gradient = jnp.sum(along_z[:, :own_rows].astype(jnp.float32), axis=0).reshape(master.shape)
    returned = along_z[:, own_rows:].reshape(n_z, n_y, 2, wide).transpose(1, 0, 2, 3)
    new_first = beta_one * first_moment + (1.0 - beta_one) * gradient
    new_second = beta_two * second_moment + (1.0 - beta_two) * gradient * gradient
    correct_one = 1.0 - beta_one**adam_step
    correct_two = 1.0 - beta_two**adam_step
    update = new_first / correct_one / (jnp.sqrt(new_second / correct_two) + epsilon)
    new_master = master - learn_rate * (update + decay_rate * master)
    fresh_rows = new_master.astype(jnp.bfloat16).reshape(own_rows, wide)

    along_y = jnp.concatenate(
        [
            jnp.broadcast_to(fresh_rows[None], (n_y,) + fresh_rows.shape),
            returned.reshape(n_y, n_z * 2, wide),
        ],
        axis=1,
    )
    along_y = lax.all_to_all(along_y, "y", split_axis=0, concat_axis=0, tiled=True)
    fresh_rows = to_half(along_y[:, :own_rows].reshape(n_y * own_rows, wide), fresh_scale)
    returned = along_y[:, own_rows:]
    fresh = lax.all_gather(fresh_rows, "z", axis=0, tiled=True)
    fresh = from_half(fresh, fresh_scale).reshape(n_z, n_y, own_rows, wide)
    fresh = fresh.transpose(1, 0, 2, 3).reshape(n_y * n_z * own_rows, wide)
    fresh = lax.optimization_barrier(fresh).reshape(n_y * n_z * own_rows, 2, hid_local)
    back_slots = returned.reshape(EXPERTS, 2, 2, hid_local).transpose(0, 2, 1, 3)
    back_slots = back_slots.reshape(EXPERTS * CAP, hid_local)
    picked = jnp.dot(
        slot_table.astype(jnp.bfloat16), back_slots, preferred_element_type=jnp.float32
    )
    rolled = (
        (picked * route_weight.reshape(rows_dev * TOP, 1))
        .astype(jnp.bfloat16)
        .reshape(rows_dev, TOP, hid_local)
    )
    return (rolled, new_master, new_first, new_second, fresh)


def solution(mesh):
    fine = Mesh(mesh.devices.reshape(2, 2, 8, 8, 2), ("xl", "core", "y", "z", "xh"))
    placed = (
        P(ROW, None),
        P(ROW),
        P(),
        P(ROW, None),
        P(ROW, None),
        P(ROW, None, None, COLUMN),
        P(ROW, None),
        P(ROW),
        P(ROW, COLUMN),
        P(ROW, None, COLUMN),
        P(ROW, None, COLUMN),
        P(ROW, None, COLUMN),
    )
    return jax.shard_map(
        shards,
        mesh=fine,
        in_specs=placed,
        out_specs=(
            P(ROW, None, COLUMN),
            P(ROW, None, COLUMN),
            P(ROW, None, COLUMN),
            P(ROW, None, COLUMN),
            P(None, None, COLUMN),
        ),
        check_vma=False,
    )
```

time: 191 us -> 185 us (0.969)
  waiting for transfers between devices: 29.8 us -> 82.7 us
  blocking collectives: 79.9 us -> 29.2 us
  local copies, waits for them, and re-layouts: 20.1 us -> 10.3 us
  starting transfers between devices: 46.4 us -> 48.7 us
    all_gather x2 -> x1, blocking collectives: 63.5 us -> 29.2 us  [shards(): fresh = lax.all_gather(fresh_rows, 'z', axis=0, tiled=True)]
    all_to_all x2, waiting for transfers between devices: 0.01 us -> 33.1 us  [shards(): lax.all_to_all(along_y, 'y', split_axis=0, concat_axis=0, tiled=True)]
    all_to_all x1 -> x0, blocking collectives: 16.3 us -> none  [shards(): lax.all_to_all(along_z, 'z', split_axis=0, concat_axis=0, tiled=True)]
    all_to_all x1 -> x2, waiting for transfers between devices: 10.6 us -> 26.5 us  [shards(): lax.all_to_all(along_z, 'z', split_axis=0, concat_axis=0, tiled=True)]
    all_to_all x1 -> x2, starting transfers between devices: 3.42 us -> 13.9 us  [shards(): lax.all_to_all(along_z, 'z', split_axis=0, concat_axis=0, tiled=True)]
    all_to_all x1, waiting for transfers between devices: 6.11 us -> 15 us  [gather_by_exchange(): lax.all_to_all(jnp.broadcast_to(block[None], (count,) + block.shape), axi...]
    all_to_all x1 -> x0, waiting for transfers between devices: 5.95 us -> none  [shards(): lax.all_to_all(partial.reshape(n_z, own_rows, wide), 'z', split_axis=0, c...]
    all_to_all x1, starting transfers between devices: 7.2 us -> 3.62 us  [shards(): lax.all_to_all(partial_pre, 'y', split_axis=0, concat_axis=0, tiled=True)]
  transfers between devices with their start and end apart: 11 -> 11, of which waited for: 5 -> 9; matrix products, arithmetic and copies ran while one was open for 7% -> 4% of each run, Pallas kernels for 0% -> 0%
where the time goes in v5:
time: 185 us; the launch traced here: 184 us
  waiting for transfers between devices  82.7 us (45%)
  starting transfers between devices  48.7 us (26%)
  blocking collectives  29.2 us (16%)
  local copies, waits for them, and re-layouts  10.3 us (6%)
  matrix products  6.27 us (3%)
  other arithmetic  4.93 us (3%)
    all_to_all x2, waiting for transfers between devices, shards(): lax.all_to_all(along_y, 'y', split_axis=0, concat_axis=0, tiled=True)  33.1 us
    all_gather x1, blocking collectives, shards(): fresh = lax.all_gather(fresh_rows, 'z', axis=0, tiled=True)  29.2 us
    all_to_all x2, waiting for transfers between devices, shards(): lax.all_to_all(along_z, 'z', split_axis=0, concat_axis=0, tiled=True)  26.5 us
    all_to_all x1, waiting for transfers between devices, gather_by_exchange(): lax.all_to_all(jnp.broadcast_to(block[None], (count,) + block.shape), axi...  15 us
    all_to_all x2, starting transfers between devices, shards(): lax.all_to_all(along_z, 'z', split_axis=0, concat_axis=0, tiled=True)  13.9 us
    all_to_all x2, starting transfers between devices, shards(): lax.all_to_all(along_y, 'y', split_axis=0, concat_axis=0, tiled=True)  10.5 us
    ppermute x3, starting transfers between devices, shards(): lax.ppermute(arrived, ALONG_X, [(i, i ^ k) for i in range(CAP)])  9.82 us
    all_to_all x1, starting transfers between devices, gather_by_exchange(): lax.all_to_all(jnp.broadcast_to(block[None], (count,) + block.shape), axi...  7 us
  transfers between devices with their start and end apart: 11, of which 9 were waited for; matrix products, arithmetic and copies ran while one was open for 4% of the time, Pallas kernels for 0%

profile of v5, /device:TPU:6, one launch (start us, length us, event | category | flops | bytes accessed | tf_op | source)
XLA Modules:
  0.0 183.8 jit_solution(5142939471809494646)
XLA Ops:
  0.7 1.1 copy-done
  1.9 0.6 reshape.124
  2.5 0.4 route_rows.1
  3.0 0.3 reshape.127
  3.3 0.2 copy.70
  3.5 1.1 copy.71
  4.6 7.1 %all-to-all-start = ((bf16[8,96,448]{2,1,0:T(8,128)(2,1)}), bf16[8,96,448]{2,1,0:T(8,128)(2,1)S(1)}, u32[]{:S(2)}, u32[]{:S(2)}) async-start(bf16[8,96,448]{2,1,0:T(8,128)(2,1)} %copy.71), calls=%async_computation | async-start | bytes 1572864 | tf_op jit(solution)/shard_map/all_to_all | solution.py:171
  11.7 0.8 convert_element_type.69
  12.6 1.5 copy.95
  14.1 20.7 %all-to-all-done = bf16[8,96,448]{2,1,0:T(8,128)(2,1)S(1)} async-done(((bf16[8,96,448]{2,1,0:T(8,128)(2,1)}), bf16[8,96,448]{2,1,0:T(8,128)(2,1)S(1)}, u32[]{:S(2)}, u32[]{:S(2)}) %all-to-all-start) | async-done | bytes 688160 | tf_op jit(solution)/shard_map/all_to_all | solution.py:171
  34.9 0.4 copy.73
  35.3 0.2 copy.74
  35.6 1.0 copy.75
  36.5 10.3 %all-to-all-start.1 = ((bf16[8,64,512]{2,1,0:T(8,128)(2,1)}), bf16[8,64,512]{2,1,0:T(8,128)(2,1)S(1)}, u32[]{:S(2)}, u32[]{:S(2)}) async-start(bf16[8,64,512]{2,1,0:T(8,128)(2,1)} %copy.75), calls=%async_computation.1 | async-start | bytes 1048576 | tf_op jit(solution)/shard_map/all_to_all | solution.py:189
  46.9 1.9 %collective-permute-start = (bf16[8,64,448]{2,1,0:T(8,128)(2,1)S(1)}, bf16[8,64,448]{2,1,0:T(8,128)(2,1)S(1)}, u32[]{:S(2)}, u32[]{:S(2)}) collective-permute-start(bf16[8,64,448]{2,1,0:T(8,128)(2,1)S(1)} %slice.57), channel_id=1, source_target_pairs={{0,128},{128,0},{1,129},{129,1},{2,130},{130,2},{3,131},{131,3},{4... | collective-permute-start | bytes 1376264 | tf_op jit(solution)/shard_map/ppermute | solution.py:175
  48.8 1.9 %collective-permute-done = bf16[8,64,448]{2,1,0:T(8,128)(2,1)S(1)} collective-permute-done((bf16[8,64,448]{2,1,0:T(8,128)(2,1)S(1)}, bf16[8,64,448]{2,1,0:T(8,128)(2,1)S(1)}, u32[]{:S(2)}, u32[]{:S(2)}) %collective-permute-start) | collective-permute-done | bytes 458784 | tf_op jit(solution)/shard_map/ppermute | solution.py:175
  50.7 0.1 pad_maximum_fusion
  50.9 13.7 %all-to-all-done.1 = bf16[8,64,512]{2,1,0:T(8,128)(2,1)S(1)} async-done(((bf16[8,64,512]{2,1,0:T(8,128)(2,1)}), bf16[8,64,512]{2,1,0:T(8,128)(2,1)S(1)}, u32[]{:S(2)}, u32[]{:S(2)}) %all-to-all-start.1) | async-done | bytes 524320 | tf_op jit(solution)/shard_map/all_to_all | solution.py:189
  64.6 1.2 fusion
  65.9 3.6 %all-to-all-start.2 = ((f16[8,128,256]{2,1,0:T(8,128)(2,1)}), f16[8,128,256]{2,1,0:T(8,128)(2,1)S(1)}, u32[]{:S(2)}, u32[]{:S(2)}) async-start(f16[8,128,256]{2,1,0:T(8,128)(2,1)} %bitcast.71), calls=%async_computation.2 | async-start | bytes 1048576 | tf_op jit(solution)/shard_map/all_to_all | solution.py:203
  69.5 0.3 reshape.135.refs_0_
  69.8 3.3 %collective-permute-start.1 = (bf16[64,1792]{1,0:T(8,128)(2,1)S(1)}, bf16[64,1792]{1,0:T(8,128)(2,1)S(1)}, u32[]{:S(2)}, u32[]{:S(2)}) collective-permute-start(bf16[64,1792]{1,0:T(8,128)(2,1)S(1)} %reshape.135.refs_0_), channel_id=1, source_target_pairs={{0,1},{1,0},{256,257},{257,256},{2,3},{3,2},{258,259},{259,258},{4... | collective-permute-start | bytes 688136 | tf_op jit(solution)/shard_map/ppermute | solution.py:205
  73.1 1.9 %collective-permute-start.2 = (bf16[64,1792]{1,0:T(8,128)(2,1)S(1)}, bf16[64,1792]{1,0:T(8,128)(2,1)S(1)}, u32[]{:S(2)}, u32[]{:S(2)}) collective-permute-start(bf16[64,1792]{1,0:T(8,128)(2,1)S(1)} %reshape.135.refs_0_), channel_id=1, source_target_pairs={{0,256},{1,257},{256,0},{257,1},{2,258},{3,259},{258,2},{259,3},{4... | collective-permute-start | bytes 688136 | tf_op jit(solution)/shard_map/ppermute | solution.py:205
  75.0 4.6 %collective-permute-start.3 = (bf16[64,1792]{1,0:T(8,128)(2,1)S(1)}, bf16[64,1792]{1,0:T(8,128)(2,1)S(1)}, u32[]{:S(2)}, u32[]{:S(2)}) collective-permute-start(bf16[64,1792]{1,0:T(8,128)(2,1)S(1)} %reshape.135.refs_0_), channel_id=1, source_target_pairs={{0,257},{1,256},{256,1},{257,0},{2,259},{3,258},{258,3},{259,2},{4... | collective-permute-start | bytes 688136 | tf_op jit(solution)/shard_map/ppermute | solution.py:205
  79.7 1.9 %collective-permute-done.1.refs_1_ = bf16[64,1792]{1,0:T(8,128)(2,1)S(1)} collective-permute-done((bf16[64,1792]{1,0:T(8,128)(2,1)S(1)}, bf16[64,1792]{1,0:T(8,128)(2,1)S(1)}, u32[]{:S(2)}, u32[]{:S(2)}) %collective-permute-start.1) | collective-permute-done | bytes 229408 | tf_op jit(solution)/shard_map/ppermute | solution.py:205
  81.6 1.8 collective-permute-done.2.refs_2_
  83.4 2.5 %collective-permute-done.3.refs_3_ = bf16[64,1792]{1,0:T(8,128)(2,1)S(1)} collective-permute-done((bf16[64,1792]{1,0:T(8,128)(2,1)S(1)}, bf16[64,1792]{1,0:T(8,128)(2,1)S(1)}, u32[]{:S(2)}, u32[]{:S(2)}) %collective-permute-start.3) | collective-permute-done | bytes 229408 | tf_op jit(solution)/shard_map/ppermute | solution.py:205
  86.0 1.9 %collective-permute-start.4 = (bf16[256,1792]{1,0:T(8,128)(2,1)S(1)}, bf16[256,1792]{1,0:T(8,128)(2,1)}, u32[]{:S(2)}, u32[]{:S(2)}) collective-permute-start(bf16[256,1792]{1,0:T(8,128)(2,1)S(1)} %stack_rows.1), channel_id=1, source_target_pairs={{0,128},{128,0},{1,129},{129,1},{2,130},{130,2},{3,131},{131,3},{4... | collective-permute-start | bytes 2752520 | tf_op jit(solution)/shard_map/ppermute | solution.py:222
  88.3 0.8 broadcast_in_dim.9
  89.1 7.0 %all-to-all-start.3 = ((bf16[8,128,256]{2,1,0:T(8,128)(2,1)}), bf16[8,128,256]{2,1,0:T(8,128)(2,1)S(1)}, u32[]{:S(2)}, u32[]{:S(2)}) async-start(bf16[8,128,256]{2,1,0:T(8,128)(2,1)} %broadcast_in_dim.9), calls=%async_computation.3 | async-start | bytes 1048576 | tf_op jit(solution)/shard_map/all_to_all | solution.py:39
  96.1 2.0 %fusion.4 = f32[256,256]{1,0:T(8,128)S(1)} fusion(bf16[3584,256]{1,0:T(8,128)(2,1)} %bitcast.62, bf16[256,1792]{1,0:T(8,128)(2,1)} %collective-permute-done.4, bf16[256,1792]{1,0:T(8,128)(2,1)S(1)} %stack_rows.1, pred[]{:T(512)S(6)} %eq.44), kind=kOutput, calls=%fused_computation.13 | convolution fusion | flops 235339776 | bytes 3014657 | tf_op jit(solution)/shard_map/dot_general | solution.py:227
  98.1 0.4 convolution_add_fusion
  98.7 0.3 rev.8
  99.3 15.0 %all-to-all-done.3 = bf16[8,128,256]{2,1,0:T(8,128)(2,1)S(1)} async-done(((bf16[8,128,256]{2,1,0:T(8,128)(2,1)}), bf16[8,128,256]{2,1,0:T(8,128)(2,1)S(1)}, u32[]{:S(2)}, u32[]{:S(2)}) %all-to-all-start.3) | async-done | bytes 524320 | tf_op jit(solution)/shard_map/all_to_all | solution.py:39
  114.3 1.7 convolution_convert_fusion
  116.0 0.7 pad_maximum_fusion.2
  116.8 3.6 %all-to-all-start.4 = ((bf16[8,72,256]{2,1,0:T(8,128)(2,1)}), bf16[8,72,256]{2,1,0:T(8,128)(2,1)S(1)}, u32[]{:S(2)}, u32[]{:S(2)}) async-start(bf16[8,72,256]{2,1,0:T(8,128)(2,1)} %pad_maximum_fusion.2), calls=%async_computation.4 | async-start | bytes 589824 | tf_op jit(solution)/shard_map/all_to_all | solution.py:247
  120.5 12.8 %all-to-all-done.4 = bf16[8,72,256]{2,1,0:T(8,128)(2,1)S(1)} async-done(((bf16[8,72,256]{2,1,0:T(8,128)(2,1)}), bf16[8,72,256]{2,1,0:T(8,128)(2,1)S(1)}, u32[]{:S(2)}, u32[]{:S(2)}) %all-to-all-start.4) | async-done | bytes 294944 | tf_op jit(solution)/shard_map/all_to_all | solution.py:247
  133.4 0.8 fusion.21
  134.4 0.7 pad_maximum_fusion.3
  135.1 3.4 %all-to-all-start.5 = ((bf16[8,72,256]{2,1,0:T(8,128)(2,1)}), bf16[8,72,256]{2,1,0:T(8,128)(2,1)S(1)}, u32[]{:S(2)}, u32[]{:S(2)}) async-start(bf16[8,72,256]{2,1,0:T(8,128)(2,1)} %pad_maximum_fusion.3), calls=%async_computation.5 | async-start | bytes 589824 | tf_op jit(solution)/shard_map/all_to_all | solution.py:265
  138.7 0.2 reduce_window_sum.11
  139.0 0.2 select_reduce_fusion
  139.2 12.3 %all-to-all-done.5 = bf16[8,72,256]{2,1,0:T(8,128)(2,1)S(1)} async-done(((bf16[8,72,256]{2,1,0:T(8,128)(2,1)}), bf16[8,72,256]{2,1,0:T(8,128)(2,1)S(1)}, u32[]{:S(2)}, u32[]{:S(2)}) %all-to-all-start.5) | async-done | bytes 294944 | tf_op jit(solution)/shard_map/all_to_all | solution.py:265
  151.6 29.2 %all-gather.1 = f16[3584,256]{1,0:T(8,128)(2,1)S(1)} all-gather(f16[448,256]{1,0:T(8,128)(2,1)S(1)} %bitcast.68), channel_id=1, replica_groups=mesh['xl'=2,'core'=2,'y'=8,'z'=8,'xh'=2] {'z'}, dimensions={0}, use_global_device_ids=true | all-gather | bytes 2064384 | tf_op jit(solution)/shard_map/all_gather | solution.py:268
  180.8 0.5 multiply_convert_fusion
  181.4 1.5 reshape.147
  182.9 0.8 fusion.2
  (78 shorter events, 2.0 us)
Async XLA Ops:
  0.6 1.2 copy-start
  0.6 1.8 copy-start.11
  0.7 1.9 %copy-start.3 = (s32[16]{0:T(128)S(1)}, s32[16]{0:T(128)}, u32[]{:S(2)}) copy-start(s32[16]{0:T(128)} %param.13) | copy-start | bytes 196
  0.7 1.9 %copy-start.2 = (s32[16,8]{0,1:T(8,128)S(1)}, s32[16,8]{0,1:T(8,128)}, u32[]{:S(2)}) copy-start(s32[16,8]{0,1:T(8,128)} %param.15) | copy-start | bytes 1540
  0.7 1.9 %copy-start.1 = (bf16[16,3584]{1,0:T(8,128)(2,1)S(1)}, bf16[16,3584]{1,0:T(8,128)(2,1)}, u32[]{:S(2)}) copy-start(bf16[16,3584]{1,0:T(8,128)(2,1)} %hidden_ref.1) | copy-start | bytes 344068
  3.5 9.1 %copy-start.4 = (bf16[1,3584,2,128]{3,2,1,0:T(2,128)(2,1)S(1)}, bf16[1,3584,2,128]{3,2,1,0:T(2,128)(2,1)}, u32[]{:S(2)}) copy-start(bf16[1,3584,2,128]{3,2,1,0:T(2,128)(2,1)} %param.17) | copy-start | bytes 5505028
  4.6 30.2 %all-to-all-start = ((bf16[8,96,448]{2,1,0:T(8,128)(2,1)}), bf16[8,96,448]{2,1,0:T(8,128)(2,1)S(1)}, u32[]{:S(2)}, u32[]{:S(2)}) async-start(bf16[8,96,448]{2,1,0:T(8,128)(2,1)} %copy.71), calls=%async_computation | async-start | bytes 1572864 | tf_op jit(solution)/shard_map/all_to_all | solution.py:171
  36.5 28.0 %all-to-all-start.1 = ((bf16[8,64,512]{2,1,0:T(8,128)(2,1)}), bf16[8,64,512]{2,1,0:T(8,128)(2,1)S(1)}, u32[]{:S(2)}, u32[]{:S(2)}) async-start(bf16[8,64,512]{2,1,0:T(8,128)(2,1)} %copy.75), calls=%async_computation.1 | async-start | bytes 1048576 | tf_op jit(solution)/shard_map/all_to_all | solution.py:189
  46.9 3.8 %collective-permute-start = (bf16[8,64,448]{2,1,0:T(8,128)(2,1)S(1)}, bf16[8,64,448]{2,1,0:T(8,128)(2,1)S(1)}, u32[]{:S(2)}, u32[]{:S(2)}) collective-permute-start(bf16[8,64,448]{2,1,0:T(8,128)(2,1)S(1)} %slice.57), channel_id=1, source_target_pairs={{0,128},{128,0},{1,129},{129,1},{2,130},{130,2},{3,131},{131,3},{4... | collective-permute-start | bytes 1376264 | tf_op jit(solution)/shard_map/ppermute | solution.py:175
  50.8 15.0 %copy-start.6 = (bf16[8,128,448]{2,1,0:T(8,128)(2,1)}, bf16[8,128,448]{2,1,0:T(8,128)(2,1)S(1)}, u32[]{:S(2)}) copy-start(bf16[8,128,448]{2,1,0:T(8,128)(2,1)S(1)} %pad_maximum_fusion) | copy-start | bytes 2752516
  64.6 15.0 %copy-start.13 = (s32[128]{0:T(128)S(1)}, s32[128]{0:T(128)}, u32[]{:S(2)}) copy-start(s32[128]{0:T(128)} %param.19) | copy-start | bytes 1540
  65.8 22.2 %copy-start.10 = (bf16[128,128]{1,0:T(8,128)(2,1)S(1)}, bf16[128,128]{1,0:T(8,128)(2,1)}, u32[]{:S(2)}) copy-start(bf16[128,128]{1,0:T(8,128)(2,1)} %param.20) | copy-start | bytes 98308
  65.9 22.2 %all-to-all-start.2 = ((f16[8,128,256]{2,1,0:T(8,128)(2,1)}), f16[8,128,256]{2,1,0:T(8,128)(2,1)S(1)}, u32[]{:S(2)}, u32[]{:S(2)}) async-start(f16[8,128,256]{2,1,0:T(8,128)(2,1)} %bitcast.71), calls=%async_computation.2 | async-start | bytes 1048576 | tf_op jit(solution)/shard_map/all_to_all | solution.py:203
  69.8 11.9 %collective-permute-start.1 = (bf16[64,1792]{1,0:T(8,128)(2,1)S(1)}, bf16[64,1792]{1,0:T(8,128)(2,1)S(1)}, u32[]{:S(2)}, u32[]{:S(2)}) collective-permute-start(bf16[64,1792]{1,0:T(8,128)(2,1)S(1)} %reshape.135.refs_0_), channel_id=1, source_target_pairs={{0,1},{1,0},{256,257},{257,256},{2,3},{3,2},{258,259},{259,258},{4... | collective-permute-start | bytes 688136 | tf_op jit(solution)/shard_map/ppermute | solution.py:205
  73.1 10.3 %collective-permute-start.2 = (bf16[64,1792]{1,0:T(8,128)(2,1)S(1)}, bf16[64,1792]{1,0:T(8,128)(2,1)S(1)}, u32[]{:S(2)}, u32[]{:S(2)}) collective-permute-start(bf16[64,1792]{1,0:T(8,128)(2,1)S(1)} %reshape.135.refs_0_), channel_id=1, source_target_pairs={{0,256},{1,257},{256,0},{257,1},{2,258},{3,259},{258,2},{259,3},{4... | collective-permute-start | bytes 688136 | tf_op jit(solution)/shard_map/ppermute | solution.py:205
  75.0 10.9 %collective-permute-start.3 = (bf16[64,1792]{1,0:T(8,128)(2,1)S(1)}, bf16[64,1792]{1,0:T(8,128)(2,1)S(1)}, u32[]{:S(2)}, u32[]{:S(2)}) collective-permute-start(bf16[64,1792]{1,0:T(8,128)(2,1)S(1)} %reshape.135.refs_0_), channel_id=1, source_target_pairs={{0,257},{1,256},{256,1},{257,0},{2,259},{3,258},{258,3},{259,2},{4... | collective-permute-start | bytes 688136 | tf_op jit(solution)/shard_map/ppermute | solution.py:205
  86.0 10.1 %collective-permute-start.4 = (bf16[256,1792]{1,0:T(8,128)(2,1)S(1)}, bf16[256,1792]{1,0:T(8,128)(2,1)}, u32[]{:S(2)}, u32[]{:S(2)}) collective-permute-start(bf16[256,1792]{1,0:T(8,128)(2,1)S(1)} %stack_rows.1), channel_id=1, source_target_pairs={{0,128},{128,0},{1,129},{129,1},{2,130},{130,2},{3,131},{131,3},{4... | collective-permute-start | bytes 2752520 | tf_op jit(solution)/shard_map/ppermute | solution.py:222
  89.1 25.2 %all-to-all-start.3 = ((bf16[8,128,256]{2,1,0:T(8,128)(2,1)}), bf16[8,128,256]{2,1,0:T(8,128)(2,1)S(1)}, u32[]{:S(2)}, u32[]{:S(2)}) async-start(bf16[8,128,256]{2,1,0:T(8,128)(2,1)} %broadcast_in_dim.9), calls=%async_computation.3 | async-start | bytes 1048576 | tf_op jit(solution)/shard_map/all_to_all | solution.py:39
  96.1 2.1 %copy-start.5 = (bf16[448,8,2,128]{3,1,2,0:T(8,128)(2,1)S(1)}, bf16[448,8,2,128]{3,1,2,0:T(8,128)(2,1)}, u32[]{:S(2)}) copy-start(bf16[448,8,2,128]{3,1,2,0:T(8,128)(2,1)} %copy.95) | copy-start | bytes 5505028
  114.3 19.1 %copy-start.7 = (f32[56,2,128]{2,1,0:T(2,128)S(1)}, f32[56,2,128]{2,1,0:T(2,128)}, u32[]{:S(2)}) copy-start(f32[56,2,128]{2,1,0:T(2,128)} %param.21) | copy-start | bytes 172036
  114.3 19.1 %copy-start.8 = (f32[56,2,128]{2,1,0:T(2,128)S(1)}, f32[56,2,128]{2,1,0:T(2,128)}, u32[]{:S(2)}) copy-start(f32[56,2,128]{2,1,0:T(2,128)} %param.22) | copy-start | bytes 172036
  114.3 19.1 %copy-start.9 = (f32[56,2,128]{2,1,0:T(2,128)S(1)}, f32[56,2,128]{2,1,0:T(2,128)}, u32[]{:S(2)}) copy-start(f32[56,2,128]{2,1,0:T(2,128)} %param.23) | copy-start | bytes 172036
  116.8 22.1 %copy-start.12 = (f32[16,8]{0,1:T(8,128)S(1)}, f32[16,8]{0,1:T(8,128)}, u32[]{:S(2)}) copy-start(f32[16,8]{0,1:T(8,128)} %param.16) | copy-start | bytes 1540
  116.8 16.5 %all-to-all-start.4 = ((bf16[8,72,256]{2,1,0:T(8,128)(2,1)}), bf16[8,72,256]{2,1,0:T(8,128)(2,1)S(1)}, u32[]{:S(2)}, u32[]{:S(2)}) async-start(bf16[8,72,256]{2,1,0:T(8,128)(2,1)} %pad_maximum_fusion.2), calls=%async_computation.4 | async-start | bytes 589824 | tf_op jit(solution)/shard_map/all_to_all | solution.py:247
  135.1 16.4 %all-to-all-start.5 = ((bf16[8,72,256]{2,1,0:T(8,128)(2,1)}), bf16[8,72,256]{2,1,0:T(8,128)(2,1)S(1)}, u32[]{:S(2)}, u32[]{:S(2)}) async-start(bf16[8,72,256]{2,1,0:T(8,128)(2,1)} %pad_maximum_fusion.3), calls=%async_computation.5 | async-start | bytes 589824 | tf_op jit(solution)/shard_map/all_to_all | solution.py:265

commit v6 on v5

--- a/solution.py
+++ b/solution.py
@@ -43,25 +43,31 @@
 
 def stack_kernel(*refs):
     blocks, stacked = refs[:-1], refs[-1]
-    rows = blocks[0].shape[0]
+    rows = blocks[0].shape[1]
     for k, block in enumerate(blocks):
-        stacked[k * rows : (k + 1) * rows] = block[...]
+        stacked[:, k * rows : (k + 1) * rows] = block[...]
 
 
 def stack_rows(blocks):
-    rows, columns = blocks[0].shape
+    outer, rows, columns = blocks[0].shape
     count = len(blocks)
     return pl.pallas_call(
         stack_kernel,
-        out_shape=jax.ShapeDtypeStruct((count * rows, columns), blocks[0].dtype),
+        out_shape=jax.ShapeDtypeStruct((outer, count * rows, columns), blocks[0].dtype),
         in_specs=[pl.BlockSpec(memory_space=pltpu.VMEM)] * count,
         out_specs=pl.BlockSpec(memory_space=pltpu.VMEM),
-        compiler_params=pltpu.CompilerParams(vmem_limit_bytes=16 * 1024 * 1024),
+        compiler_params=pltpu.CompilerParams(vmem_limit_bytes=4 * 1024 * 1024),
         name="stack_rows",
         cost_estimate=pl.CostEstimate(
-            flops=0, bytes_accessed=4 * count * rows * columns, transcendentals=0
+            flops=0, bytes_accessed=4 * count * outer * rows * columns, transcendentals=0
         ),
     )(*blocks)
+
+
+def with_neighbours(block):
+    return [block] + [
+        lax.ppermute(block, ALONG_X, [(i, i ^ k) for i in range(4)]) for k in range(1, 4)
+    ]
 
 
 def route_kernel(hidden_ref, beam_ref, gain_ref, ids_ref, out_ref):
@@ -108,7 +114,7 @@
         out_shape=jax.ShapeDtypeStruct((EXPERTS, width // 2), jnp.bfloat16),
         in_specs=[pl.BlockSpec(memory_space=pltpu.VMEM)] * 4,
         out_specs=pl.BlockSpec(memory_space=pltpu.VMEM),
-        compiler_params=pltpu.CompilerParams(vmem_limit_bytes=16 * 1024 * 1024),
+        compiler_params=pltpu.CompilerParams(vmem_limit_bytes=4 * 1024 * 1024),
         name="route_rows",
         cost_estimate=pl.CostEstimate(
             flops=2 * EXPERTS * rows * width, bytes_accessed=1 << 19, transcendentals=rows
@@ -135,17 +141,15 @@
     wide = 2 * hid_local
     n_y, n_z = lax.axis_size("y"), lax.axis_size("z")
 
-    half = learn_tokens.shape[0] // 2
+    tokens = learn_tokens.shape[0]
+    quarter = tokens // 4
     core = lax.axis_index("core")
 
     def own_first(block):
-        return jnp.concatenate(
-            [
-                lax.dynamic_slice_in_dim(block, core * half, half, 0),
-                lax.dynamic_slice_in_dim(block, (1 - core) * half, half, 0),
-            ],
-            axis=0,
-        )
+        block = block.reshape(2, 2, quarter, block.shape[1])
+        for place, axis in enumerate(("core", "xl")):
+            block = jnp.where(lax.axis_index(axis) == 1, jnp.flip(block, place), block)
+        return block.reshape(tokens, block.shape[3])
 
     rows_dev, width = hidden_rows.shape
     flat_ids = route_ids.reshape(rows_dev * TOP)
@@ -160,10 +164,12 @@
     outgoing = route_rows(hidden_rows, parent_beam, norm_gain, route_ids)
     features = width // n_y
     chunks = span // features
-    tokens_half = lax.dynamic_slice_in_dim(learn_tokens, core * half, half, 0)
+    tokens_part = lax.dynamic_slice_in_dim(
+        learn_tokens, lax.axis_index(("core", "xl")) * quarter, quarter, 0
+    )
     along_y = jnp.concatenate(
         [
-            tokens_half.reshape(half, n_y, features).transpose(1, 0, 2),
+            tokens_part.reshape(quarter, n_y, features).transpose(1, 0, 2),
             outgoing.reshape(n_y, n_z * chunks, features),
         ],
         axis=1,
@@ -171,13 +177,13 @@
     along_y = lax.all_to_all(along_y, "y", split_axis=0, concat_axis=0, tiled=True)
     local_weight = expert_weight.reshape(width, wide)
     along_y, local_weight = lax.optimization_barrier((along_y, local_weight))
-    own_slice = along_y[:, :half]
+    own_slice = along_y[:, :quarter]
+    own_slice = stack_rows([own_slice, lax.ppermute(own_slice, "xl", SWAP)])
     other_slice = lax.ppermute(own_slice, "core", SWAP)
-    token_slice = jnp.concatenate([own_slice, other_slice], axis=1)
-    token_slice = token_slice.reshape(n_y * 2 * half, features)
+    token_slice = jnp.concatenate([own_slice, other_slice], axis=1).reshape(n_y * tokens, features)
     lanes = 2 * wide
     tall = n_z * chunks
-    routed = along_y[:, half:].reshape(n_y, n_z, chunks, features).transpose(1, 0, 2, 3)
+    routed = along_y[:, quarter:].reshape(n_y, n_z, chunks, features).transpose(1, 0, 2, 3)
     routed = jnp.pad(
         routed.reshape(n_z, n_y * chunks, features), ((0, 0), (0, 0), (0, lanes - features))
     )
@@ -199,11 +205,9 @@
     partial_pre = to_half(
         jnp.dot(token_slice, weights, preferred_element_type=jnp.float32), pre_scale
     )
-    partial_pre = partial_pre.reshape(n_y, 2 * half, wide)
+    partial_pre = partial_pre.reshape(n_y, tokens, wide)
     pre_parts = lax.all_to_all(partial_pre, "y", split_axis=0, concat_axis=0, tiled=True)
-    pieces = [arrived] + [
-        lax.ppermute(arrived, ALONG_X, [(i, i ^ k) for i in range(CAP)]) for k in range(1, CAP)
-    ]
+    pieces = with_neighbours(arrived[None])
     projected = jnp.sum(pre_parts.astype(jnp.float32), axis=0) * (1.0 / pre_scale)
     gate_pre = projected[:, :hid_local]
     up_pre = projected[:, hid_local:]
@@ -217,8 +221,7 @@
     ).astype(jnp.bfloat16)
 
     grad_all = gather_by_exchange(grad_pre, "y").reshape(token_slice.shape[0], wide)
-    pieces, _ = lax.optimization_barrier((pieces, grad_pre))
-    pieces = stack_rows(pieces)
+    pieces = stack_rows(pieces)[0]
     other_pieces = lax.ppermute(pieces, "core", SWAP)
     projected_rows = jnp.dot(
         jnp.where(core == 0, pieces, other_pieces),

time: 185 us -> 181 us (0.978)
  waiting for transfers between devices: 82.7 us -> 75.3 us
  starting transfers between devices: 48.7 us -> 51.3 us
    all_to_all x2, waiting for transfers between devices: 26.5 us -> 16.7 us  [shards(): lax.all_to_all(along_z, 'z', split_axis=0, concat_axis=0, tiled=True)]
    ppermute x3 -> x4, waiting for transfers between devices: 6.23 us -> 13.3 us  [the longest x1 7.1 us: shards(): own_slice = stack_rows([own_slice, lax.ppermute(own_slice, 'xl', SWAP)])]
    all_to_all x2, waiting for transfers between devices: 33.1 us -> 28.3 us  [shards(): lax.all_to_all(along_y, 'y', split_axis=0, concat_axis=0, tiled=True)]
    ppermute x3 -> x4, starting transfers between devices: 9.82 us -> 12.5 us  [the longest x3 9.82 us: with_neighbours(): lax.ppermute(block, ALONG_X, [(i, i ^ k) for i in range(4)])]
    unnamed x35 -> x37, local copies, waits for them, and re-layouts: 2.84 us -> 5.13 us
    concatenate x2 -> x0, local copies, waits for them, and re-layouts: 2.07 us -> none  [the longest x1 1.12 us: shards(): jnp.concatenate([tokens_half.reshape(half, n_y, features).transpose(1, 0,...]
  transfers between devices with their start and end apart: 11 -> 12, of which waited for: 9 -> 10; matrix products, arithmetic and copies ran while one was open for 4% -> 4% of each run, Pallas kernels for 0% -> 0%
where the time goes in v6:
time: 181 us; the launch traced here: 180 us
  waiting for transfers between devices  75.3 us (42%)
  starting transfers between devices  51.3 us (28%)
  blocking collectives  29.2 us (16%)
  local copies, waits for them, and re-layouts  10.6 us (6%)
  matrix products  6.03 us (3%)
  other arithmetic  5.69 us (3%)
    all_gather x1, blocking collectives, shards(): fresh = lax.all_gather(fresh_rows, 'z', axis=0, tiled=True)  29.2 us
    all_to_all x2, waiting for transfers between devices, shards(): lax.all_to_all(along_y, 'y', split_axis=0, concat_axis=0, tiled=True)  28.3 us
    all_to_all x2, waiting for transfers between devices, shards(): lax.all_to_all(along_z, 'z', split_axis=0, concat_axis=0, tiled=True)  16.7 us
    all_to_all x1, waiting for transfers between devices, gather_by_exchange(): lax.all_to_all(jnp.broadcast_to(block[None], (count,) + block.shape), axi...  15.2 us
    all_to_all x2, starting transfers between devices, shards(): lax.all_to_all(along_z, 'z', split_axis=0, concat_axis=0, tiled=True)  13.9 us
    all_to_all x2, starting transfers between devices, shards(): lax.all_to_all(along_y, 'y', split_axis=0, concat_axis=0, tiled=True)  10.5 us
    ppermute x3, starting transfers between devices, with_neighbours(): lax.ppermute(block, ALONG_X, [(i, i ^ k) for i in range(4)])  9.82 us
    ppermute x1, waiting for transfers between devices, shards(): own_slice = stack_rows([own_slice, lax.ppermute(own_slice, 'xl', SWAP)])  7.1 us
  transfers between devices with their start and end apart: 12, of which 10 were waited for; matrix products, arithmetic and copies ran while one was open for 4% of the time, Pallas kernels for 0%

profile of v6, /device:TPU:6, one launch (start us, length us, event | category | flops | bytes accessed | tf_op | source)
XLA Modules:
  0.0 179.8 jit_solution(18019038714430659669)
XLA Ops:
  0.7 1.2 copy-done
  1.8 0.3 reshape.127
  2.2 0.7 reshape.129.gain_ref
  3.0 0.9 copy-done.1
  3.9 0.7 copy-done.2
  4.6 0.7 copy-done.4
  5.2 0.4 route_rows.1
  5.7 0.3 reshape.130
  6.0 0.9 pad_maximum_fusion.1
  6.8 7.1 %all-to-all-start = ((bf16[8,64,448]{2,1,0:T(8,128)(2,1)}), bf16[8,64,448]{2,1,0:T(8,128)(2,1)S(1)}, u32[]{:S(2)}, u32[]{:S(2)}) async-start(bf16[8,64,448]{2,1,0:T(8,128)(2,1)} %pad_maximum_fusion.1), calls=%async_computation | async-start | bytes 1048576 | tf_op jit(solution)/shard_map/all_to_all | solution.py:177
  14.0 1.5 copy.61
  15.5 15.9 %all-to-all-done = bf16[8,64,448]{2,1,0:T(8,128)(2,1)S(1)} async-done(((bf16[8,64,448]{2,1,0:T(8,128)(2,1)}), bf16[8,64,448]{2,1,0:T(8,128)(2,1)S(1)}, u32[]{:S(2)}, u32[]{:S(2)}) %all-to-all-start) | async-done | bytes 458784 | tf_op jit(solution)/shard_map/all_to_all | solution.py:177
  31.8 0.8 fusion.11
  32.7 10.3 %all-to-all-start.1 = ((bf16[8,64,512]{2,1,0:T(8,128)(2,1)}), bf16[8,64,512]{2,1,0:T(8,128)(2,1)S(1)}, u32[]{:S(2)}, u32[]{:S(2)}) async-start(bf16[8,64,512]{2,1,0:T(8,128)(2,1)} %fusion.11), calls=%async_computation.1 | async-start | bytes 1048576 | tf_op jit(solution)/shard_map/all_to_all | solution.py:195
  43.0 2.7 %collective-permute-start = (bf16[8,32,448]{2,1,0:T(8,128)(2,1)S(1)}, bf16[8,32,448]{2,1,0:T(8,128)(2,1)S(1)}, u32[]{:S(2)}, u32[]{:S(2)}) collective-permute-start(bf16[8,32,448]{2,1,0:T(8,128)(2,1)S(1)} %get-tuple-element.18.refs_0_), channel_id=1, source_target_pairs={{0,256},{256,0},{1,257},{257,1},{2,258},{258,2},{3,259},{259,3},{4... | collective-permute-start | bytes 688136 | tf_op jit(solution)/shard_map/ppermute | solution.py:181
  45.7 7.1 %collective-permute-done.refs_1_ = bf16[8,32,448]{2,1,0:T(8,128)(2,1)S(1)} collective-permute-done((bf16[8,32,448]{2,1,0:T(8,128)(2,1)S(1)}, bf16[8,32,448]{2,1,0:T(8,128)(2,1)S(1)}, u32[]{:S(2)}, u32[]{:S(2)}) %collective-permute-start) | collective-permute-done | bytes 229408 | tf_op jit(solution)/shard_map/ppermute | solution.py:181
  52.9 1.9 %collective-permute-start.1 = (bf16[8,64,448]{2,1,0:T(8,128)(2,1)S(1)}, bf16[8,64,448]{2,1,0:T(8,128)(2,1)S(1)}, u32[]{:S(2)}, u32[]{:S(2)}) collective-permute-start(bf16[8,64,448]{2,1,0:T(8,128)(2,1)S(1)} %stack_rows.2), channel_id=1, source_target_pairs={{0,128},{128,0},{1,129},{129,1},{2,130},{130,2},{3,131},{131,3},{4... | collective-permute-start | bytes 1376264 | tf_op jit(solution)/shard_map/ppermute | solution.py:182
  54.8 1.9 %collective-permute-done.1 = bf16[8,64,448]{2,1,0:T(8,128)(2,1)S(1)} collective-permute-done((bf16[8,64,448]{2,1,0:T(8,128)(2,1)S(1)}, bf16[8,64,448]{2,1,0:T(8,128)(2,1)S(1)}, u32[]{:S(2)}, u32[]{:S(2)}) %collective-permute-start.1) | collective-permute-done | bytes 458784 | tf_op jit(solution)/shard_map/ppermute | solution.py:182
  56.8 3.8 %all-to-all-done.1 = bf16[8,64,512]{2,1,0:T(8,128)(2,1)S(1)} async-done(((bf16[8,64,512]{2,1,0:T(8,128)(2,1)}), bf16[8,64,512]{2,1,0:T(8,128)(2,1)S(1)}, u32[]{:S(2)}, u32[]{:S(2)}) %all-to-all-start.1) | async-done | bytes 524320 | tf_op jit(solution)/shard_map/all_to_all | solution.py:195
  60.7 1.3 fusion
  62.0 3.5 %all-to-all-start.2 = ((f16[8,128,256]{2,1,0:T(8,128)(2,1)}), f16[8,128,256]{2,1,0:T(8,128)(2,1)S(1)}, u32[]{:S(2)}, u32[]{:S(2)}) async-start(f16[8,128,256]{2,1,0:T(8,128)(2,1)} %bitcast.8), calls=%async_computation.2 | async-start | bytes 1048576 | tf_op jit(solution)/shard_map/all_to_all | solution.py:209
  65.7 0.3 broadcast_in_dim_reshape.2.refs_0_
  65.9 3.3 %collective-permute-start.2 = (bf16[1,64,1792]{2,1,0:T(8,128)(2,1)S(1)}, bf16[1,64,1792]{2,1,0:T(8,128)(2,1)S(1)}, u32[]{:S(2)}, u32[]{:S(2)}) collective-permute-start(bf16[1,64,1792]{2,1,0:T(8,128)(2,1)S(1)} %broadcast_in_dim_reshape.2.refs_0_), channel_id=1, source_target_pairs={{0,1},{1,0},{256,257},{257,256},{2,3},{3,2},{258,259},{259,258},{4... | collective-permute-start | bytes 688136 | tf_op jit(solution)/shard_map/ppermute | solution.py:69
  69.3 1.9 %collective-permute-start.3 = (bf16[1,64,1792]{2,1,0:T(8,128)(2,1)S(1)}, bf16[1,64,1792]{2,1,0:T(8,128)(2,1)S(1)}, u32[]{:S(2)}, u32[]{:S(2)}) collective-permute-start(bf16[1,64,1792]{2,1,0:T(8,128)(2,1)S(1)} %broadcast_in_dim_reshape.2.refs_0_), channel_id=1, source_target_pairs={{0,256},{1,257},{256,0},{257,1},{2,258},{3,259},{258,2},{259,3},{4... | collective-permute-start | bytes 688136 | tf_op jit(solution)/shard_map/ppermute | solution.py:69
  71.2 4.6 %collective-permute-start.4 = (bf16[1,64,1792]{2,1,0:T(8,128)(2,1)S(1)}, bf16[1,64,1792]{2,1,0:T(8,128)(2,1)S(1)}, u32[]{:S(2)}, u32[]{:S(2)}) collective-permute-start(bf16[1,64,1792]{2,1,0:T(8,128)(2,1)S(1)} %broadcast_in_dim_reshape.2.refs_0_), channel_id=1, source_target_pairs={{0,257},{1,256},{256,1},{257,0},{2,259},{3,258},{258,3},{259,2},{4... | collective-permute-start | bytes 688136 | tf_op jit(solution)/shard_map/ppermute | solution.py:69
  75.9 1.9 %collective-permute-done.2.refs_1_ = bf16[1,64,1792]{2,1,0:T(8,128)(2,1)S(1)} collective-permute-done((bf16[1,64,1792]{2,1,0:T(8,128)(2,1)S(1)}, bf16[1,64,1792]{2,1,0:T(8,128)(2,1)S(1)}, u32[]{:S(2)}, u32[]{:S(2)}) %collective-permute-start.2) | collective-permute-done | bytes 229408 | tf_op jit(solution)/shard_map/ppermute | solution.py:69
  77.8 1.8 collective-permute-done.3.refs_2_
  79.6 2.6 %collective-permute-done.4.refs_3_ = bf16[1,64,1792]{2,1,0:T(8,128)(2,1)S(1)} collective-permute-done((bf16[1,64,1792]{2,1,0:T(8,128)(2,1)S(1)}, bf16[1,64,1792]{2,1,0:T(8,128)(2,1)S(1)}, u32[]{:S(2)}, u32[]{:S(2)}) %collective-permute-start.4) | collective-permute-done | bytes 229408 | tf_op jit(solution)/shard_map/ppermute | solution.py:69
  82.2 1.9 %collective-permute-start.5 = (bf16[256,1792]{1,0:T(8,128)(2,1)S(1)}, bf16[256,1792]{1,0:T(8,128)(2,1)}, u32[]{:S(2)}, u32[]{:S(2)}) collective-permute-start(bf16[256,1792]{1,0:T(8,128)(2,1)S(1)} %bitcast.65), channel_id=1, source_target_pairs={{0,128},{128,0},{1,129},{129,1},{2,130},{130,2},{3,131},{131,3},{4... | collective-permute-start | bytes 2752520 | tf_op jit(solution)/shard_map/ppermute | solution.py:225
  84.4 0.8 broadcast_in_dim.9
  85.2 7.0 %all-to-all-start.3 = ((bf16[8,128,256]{2,1,0:T(8,128)(2,1)}), bf16[8,128,256]{2,1,0:T(8,128)(2,1)}, u32[]{:S(2)}, u32[]{:S(2)}) async-start(bf16[8,128,256]{2,1,0:T(8,128)(2,1)} %broadcast_in_dim.9), calls=%async_computation.3 | async-start | bytes 1048576 | tf_op jit(solution)/shard_map/all_to_all | solution.py:39
  92.2 2.0 %fusion.4 = f32[256,256]{1,0:T(8,128)S(1)} fusion(bf16[3584,256]{1,0:T(8,128)(2,1)} %bitcast.71, bf16[256,1792]{1,0:T(8,128)(2,1)} %collective-permute-done.5, pred[]{:T(512)S(6)} %eq.51, bf16[1,256,1792]{2,1,0:T(8,128)(2,1)S(1)} %stack_rows.3), kind=kOutput, calls=%fused_computation.13 | convolution fusion | flops 235339776 | bytes 3014657 | tf_op jit(solution)/shard_map/dot_general | solution.py:230
  94.3 0.4 convolution_add_fusion
  94.8 0.3 rev.28
  95.4 15.2 %all-to-all-done.3 = bf16[8,128,256]{2,1,0:T(8,128)(2,1)} async-done(((bf16[8,128,256]{2,1,0:T(8,128)(2,1)}), bf16[8,128,256]{2,1,0:T(8,128)(2,1)}, u32[]{:S(2)}, u32[]{:S(2)}) %all-to-all-start.3) | async-done | bytes 524320 | tf_op jit(solution)/shard_map/all_to_all | solution.py:39
  110.5 1.5 convolution_convert_fusion
  112.1 0.7 pad_maximum_fusion.2
  112.8 3.6 %all-to-all-start.4 = ((bf16[8,72,256]{2,1,0:T(8,128)(2,1)}), bf16[8,72,256]{2,1,0:T(8,128)(2,1)S(1)}, u32[]{:S(2)}, u32[]{:S(2)}) async-start(bf16[8,72,256]{2,1,0:T(8,128)(2,1)} %pad_maximum_fusion.2), calls=%async_computation.4 | async-start | bytes 589824 | tf_op jit(solution)/shard_map/all_to_all | solution.py:250
  116.5 12.8 %all-to-all-done.4 = bf16[8,72,256]{2,1,0:T(8,128)(2,1)S(1)} async-done(((bf16[8,72,256]{2,1,0:T(8,128)(2,1)}), bf16[8,72,256]{2,1,0:T(8,128)(2,1)S(1)}, u32[]{:S(2)}, u32[]{:S(2)}) %all-to-all-start.4) | async-done | bytes 294944 | tf_op jit(solution)/shard_map/all_to_all | solution.py:250
  129.4 0.8 fusion.26
  130.4 0.7 pad_maximum_fusion.3
  131.1 3.4 %all-to-all-start.5 = ((bf16[8,72,256]{2,1,0:T(8,128)(2,1)}), bf16[8,72,256]{2,1,0:T(8,128)(2,1)S(1)}, u32[]{:S(2)}, u32[]{:S(2)}) async-start(bf16[8,72,256]{2,1,0:T(8,128)(2,1)} %pad_maximum_fusion.3), calls=%async_computation.5 | async-start | bytes 589824 | tf_op jit(solution)/shard_map/all_to_all | solution.py:268
  135.0 0.2 select_reduce_fusion
  135.2 12.3 %all-to-all-done.5 = bf16[8,72,256]{2,1,0:T(8,128)(2,1)S(1)} async-done(((bf16[8,72,256]{2,1,0:T(8,128)(2,1)}), bf16[8,72,256]{2,1,0:T(8,128)(2,1)S(1)}, u32[]{:S(2)}, u32[]{:S(2)}) %all-to-all-start.5) | async-done | bytes 294944 | tf_op jit(solution)/shard_map/all_to_all | solution.py:268
  147.6 29.2 %all-gather.1 = f16[3584,256]{1,0:T(8,128)(2,1)S(1)} all-gather(f16[448,256]{1,0:T(8,128)(2,1)S(1)} %bitcast.77), channel_id=1, replica_groups=mesh['xl'=2,'core'=2,'y'=8,'z'=8,'xh'=2] {'z'}, dimensions={0}, use_global_device_ids=true | all-gather | bytes 2064384 | tf_op jit(solution)/shard_map/all_gather | solution.py:271
  176.8 0.5 multiply_convert_fusion
  177.4 1.5 reshape.150
  179.0 0.8 fusion.2
  (85 shorter events, 2.7 us)
Async XLA Ops:
  0.6 1.2 copy-start
  3.0 0.9 copy-start.1
  3.9 0.7 copy-start.2
  4.6 0.7 copy-start.4
  5.2 8.8 %copy-start.5 = (bf16[1,3584,2,128]{3,2,1,0:T(2,128)(2,1)S(1)}, bf16[1,3584,2,128]{3,2,1,0:T(2,128)(2,1)}, u32[]{:S(2)}) copy-start(bf16[1,3584,2,128]{3,2,1,0:T(2,128)(2,1)} %param.17) | copy-start | bytes 5505028
  5.9 8.0 %copy-start.9 = (f32[56,2,128]{2,1,0:T(2,128)S(1)}, f32[56,2,128]{2,1,0:T(2,128)}, u32[]{:S(2)}) copy-start(f32[56,2,128]{2,1,0:T(2,128)} %param.21) | copy-start | bytes 172036
  6.8 24.6 %all-to-all-start = ((bf16[8,64,448]{2,1,0:T(8,128)(2,1)}), bf16[8,64,448]{2,1,0:T(8,128)(2,1)S(1)}, u32[]{:S(2)}, u32[]{:S(2)}) async-start(bf16[8,64,448]{2,1,0:T(8,128)(2,1)} %pad_maximum_fusion.1), calls=%async_computation | async-start | bytes 1048576 | tf_op jit(solution)/shard_map/all_to_all | solution.py:177
  32.7 28.0 %all-to-all-start.1 = ((bf16[8,64,512]{2,1,0:T(8,128)(2,1)}), bf16[8,64,512]{2,1,0:T(8,128)(2,1)S(1)}, u32[]{:S(2)}, u32[]{:S(2)}) async-start(bf16[8,64,512]{2,1,0:T(8,128)(2,1)} %fusion.11), calls=%async_computation.1 | async-start | bytes 1048576 | tf_op jit(solution)/shard_map/all_to_all | solution.py:195
  43.0 9.8 %collective-permute-start = (bf16[8,32,448]{2,1,0:T(8,128)(2,1)S(1)}, bf16[8,32,448]{2,1,0:T(8,128)(2,1)S(1)}, u32[]{:S(2)}, u32[]{:S(2)}) collective-permute-start(bf16[8,32,448]{2,1,0:T(8,128)(2,1)S(1)} %get-tuple-element.18.refs_0_), channel_id=1, source_target_pairs={{0,256},{256,0},{1,257},{257,1},{2,258},{258,2},{3,259},{259,3},{4... | collective-permute-start | bytes 688136 | tf_op jit(solution)/shard_map/ppermute | solution.py:181
  52.9 3.8 %collective-permute-start.1 = (bf16[8,64,448]{2,1,0:T(8,128)(2,1)S(1)}, bf16[8,64,448]{2,1,0:T(8,128)(2,1)S(1)}, u32[]{:S(2)}, u32[]{:S(2)}) collective-permute-start(bf16[8,64,448]{2,1,0:T(8,128)(2,1)S(1)} %stack_rows.2), channel_id=1, source_target_pairs={{0,128},{128,0},{1,129},{129,1},{2,130},{130,2},{3,131},{131,3},{4... | collective-permute-start | bytes 1376264 | tf_op jit(solution)/shard_map/ppermute | solution.py:182
  56.8 5.2 %copy-start.7 = (bf16[8,128,448]{2,1,0:T(8,128)(2,1)}, bf16[8,128,448]{2,1,0:T(8,128)(2,1)S(1)}, u32[]{:S(2)}) copy-start(bf16[8,128,448]{2,1,0:T(8,128)(2,1)S(1)} %pad_maximum_fusion) | copy-start | bytes 2752516
  60.7 4.8 %copy-start.14 = (s32[128]{0:T(128)S(1)}, s32[128]{0:T(128)}, u32[]{:S(2)}) copy-start(s32[128]{0:T(128)} %param.19) | copy-start | bytes 1540
  60.7 15.1 %copy-start.12 = (bf16[128,128]{1,0:T(8,128)(2,1)S(1)}, bf16[128,128]{1,0:T(8,128)(2,1)}, u32[]{:S(2)}) copy-start(bf16[128,128]{1,0:T(8,128)(2,1)} %param.20) | copy-start | bytes 98308
  62.0 22.1 %all-to-all-start.2 = ((f16[8,128,256]{2,1,0:T(8,128)(2,1)}), f16[8,128,256]{2,1,0:T(8,128)(2,1)S(1)}, u32[]{:S(2)}, u32[]{:S(2)}) async-start(f16[8,128,256]{2,1,0:T(8,128)(2,1)} %bitcast.8), calls=%async_computation.2 | async-start | bytes 1048576 | tf_op jit(solution)/shard_map/all_to_all | solution.py:209
  65.9 11.9 %collective-permute-start.2 = (bf16[1,64,1792]{2,1,0:T(8,128)(2,1)S(1)}, bf16[1,64,1792]{2,1,0:T(8,128)(2,1)S(1)}, u32[]{:S(2)}, u32[]{:S(2)}) collective-permute-start(bf16[1,64,1792]{2,1,0:T(8,128)(2,1)S(1)} %broadcast_in_dim_reshape.2.refs_0_), channel_id=1, source_target_pairs={{0,1},{1,0},{256,257},{257,256},{2,3},{3,2},{258,259},{259,258},{4... | collective-permute-start | bytes 688136 | tf_op jit(solution)/shard_map/ppermute | solution.py:69
  69.3 10.3 %collective-permute-start.3 = (bf16[1,64,1792]{2,1,0:T(8,128)(2,1)S(1)}, bf16[1,64,1792]{2,1,0:T(8,128)(2,1)S(1)}, u32[]{:S(2)}, u32[]{:S(2)}) collective-permute-start(bf16[1,64,1792]{2,1,0:T(8,128)(2,1)S(1)} %broadcast_in_dim_reshape.2.refs_0_), channel_id=1, source_target_pairs={{0,256},{1,257},{256,0},{257,1},{2,258},{3,259},{258,2},{259,3},{4... | collective-permute-start | bytes 688136 | tf_op jit(solution)/shard_map/ppermute | solution.py:69
  71.2 10.9 %collective-permute-start.4 = (bf16[1,64,1792]{2,1,0:T(8,128)(2,1)S(1)}, bf16[1,64,1792]{2,1,0:T(8,128)(2,1)S(1)}, u32[]{:S(2)}, u32[]{:S(2)}) collective-permute-start(bf16[1,64,1792]{2,1,0:T(8,128)(2,1)S(1)} %broadcast_in_dim_reshape.2.refs_0_), channel_id=1, source_target_pairs={{0,257},{1,256},{256,1},{257,0},{2,259},{3,258},{258,3},{259,2},{4... | collective-permute-start | bytes 688136 | tf_op jit(solution)/shard_map/ppermute | solution.py:69
  82.2 10.0 %collective-permute-start.5 = (bf16[256,1792]{1,0:T(8,128)(2,1)S(1)}, bf16[256,1792]{1,0:T(8,128)(2,1)}, u32[]{:S(2)}, u32[]{:S(2)}) collective-permute-start(bf16[256,1792]{1,0:T(8,128)(2,1)S(1)} %bitcast.65), channel_id=1, source_target_pairs={{0,128},{128,0},{1,129},{129,1},{2,130},{130,2},{3,131},{131,3},{4... | collective-permute-start | bytes 2752520 | tf_op jit(solution)/shard_map/ppermute | solution.py:225
  85.2 25.3 %all-to-all-start.3 = ((bf16[8,128,256]{2,1,0:T(8,128)(2,1)}), bf16[8,128,256]{2,1,0:T(8,128)(2,1)}, u32[]{:S(2)}, u32[]{:S(2)}) async-start(bf16[8,128,256]{2,1,0:T(8,128)(2,1)} %broadcast_in_dim.9), calls=%async_computation.3 | async-start | bytes 1048576 | tf_op jit(solution)/shard_map/all_to_all | solution.py:39
  92.2 2.1 %copy-start.6 = (bf16[448,8,2,128]{3,1,2,0:T(8,128)(2,1)S(1)}, bf16[448,8,2,128]{3,1,2,0:T(8,128)(2,1)}, u32[]{:S(2)}) copy-start(bf16[448,8,2,128]{3,1,2,0:T(8,128)(2,1)} %copy.61) | copy-start | bytes 5505028
  94.3 16.3 %copy-start.8 = (bf16[8,128,448]{2,1,0:T(8,128)(2,1)S(1)}, bf16[8,128,448]{2,1,0:T(8,128)(2,1)}, u32[]{:S(2)}) copy-start(bf16[8,128,448]{2,1,0:T(8,128)(2,1)} %copy-done.7) | copy-start | bytes 2752516
  95.3 21.1 %copy-start.3 = (s32[16,8]{0,1:T(8,128)S(1)}, s32[16,8]{0,1:T(8,128)}, u32[]{:S(2)}) copy-start(s32[16,8]{0,1:T(8,128)} %param.15) | copy-start | bytes 1540
  110.5 18.9 %copy-start.10 = (f32[56,2,128]{2,1,0:T(2,128)S(1)}, f32[56,2,128]{2,1,0:T(2,128)}, u32[]{:S(2)}) copy-start(f32[56,2,128]{2,1,0:T(2,128)} %param.22) | copy-start | bytes 172036
  110.5 18.9 %copy-start.11 = (f32[56,2,128]{2,1,0:T(2,128)S(1)}, f32[56,2,128]{2,1,0:T(2,128)}, u32[]{:S(2)}) copy-start(f32[56,2,128]{2,1,0:T(2,128)} %param.23) | copy-start | bytes 172036
  112.8 22.0 %copy-start.13 = (f32[16,8]{0,1:T(8,128)S(1)}, f32[16,8]{0,1:T(8,128)}, u32[]{:S(2)}) copy-start(f32[16,8]{0,1:T(8,128)} %param.16) | copy-start | bytes 1540
  112.8 16.5 %all-to-all-start.4 = ((bf16[8,72,256]{2,1,0:T(8,128)(2,1)}), bf16[8,72,256]{2,1,0:T(8,128)(2,1)S(1)}, u32[]{:S(2)}, u32[]{:S(2)}) async-start(bf16[8,72,256]{2,1,0:T(8,128)(2,1)} %pad_maximum_fusion.2), calls=%async_computation.4 | async-start | bytes 589824 | tf_op jit(solution)/shard_map/all_to_all | solution.py:250
  131.1 16.4 %all-to-all-start.5 = ((bf16[8,72,256]{2,1,0:T(8,128)(2,1)}), bf16[8,72,256]{2,1,0:T(8,128)(2,1)S(1)}, u32[]{:S(2)}, u32[]{:S(2)}) async-start(bf16[8,72,256]{2,1,0:T(8,128)(2,1)} %pad_maximum_fusion.3), calls=%async_computation.5 | async-start | bytes 589824 | tf_op jit(solution)/shard_map/all_to_all | solution.py:268

commit v7 on v6

--- a/solution.py
+++ b/solution.py
@@ -141,15 +141,15 @@
     wide = 2 * hid_local
     n_y, n_z = lax.axis_size("y"), lax.axis_size("z")
 
-    tokens = learn_tokens.shape[0]
-    quarter = tokens // 4
+    eighth = learn_tokens.shape[0] // 8
+    tall_tokens = 8 * eighth
     core = lax.axis_index("core")
 
     def own_first(block):
-        block = block.reshape(2, 2, quarter, block.shape[1])
-        for place, axis in enumerate(("core", "xl")):
+        block = block.reshape(2, 2, 2, eighth, block.shape[1])
+        for place, axis in enumerate(("core", "xl", "xh")):
             block = jnp.where(lax.axis_index(axis) == 1, jnp.flip(block, place), block)
-        return block.reshape(tokens, block.shape[3])
+        return block.reshape(tall_tokens, block.shape[4])
 
     rows_dev, width = hidden_rows.shape
     flat_ids = route_ids.reshape(rows_dev * TOP)
@@ -165,11 +165,11 @@
     features = width // n_y
     chunks = span // features
     tokens_part = lax.dynamic_slice_in_dim(
-        learn_tokens, lax.axis_index(("core", "xl")) * quarter, quarter, 0
+        learn_tokens, (core * 4 + lax.axis_index(ALONG_X)) * eighth, eighth, 0
     )
     along_y = jnp.concatenate(
         [
-            tokens_part.reshape(quarter, n_y, features).transpose(1, 0, 2),
+            tokens_part.reshape(eighth, n_y, features).transpose(1, 0, 2),
             outgoing.reshape(n_y, n_z * chunks, features),
         ],
         axis=1,
@@ -177,13 +177,12 @@
     along_y = lax.all_to_all(along_y, "y", split_axis=0, concat_axis=0, tiled=True)
     local_weight = expert_weight.reshape(width, wide)
     along_y, local_weight = lax.optimization_barrier((along_y, local_weight))
-    own_slice = along_y[:, :quarter]
-    own_slice = stack_rows([own_slice, lax.ppermute(own_slice, "xl", SWAP)])
+    own_slice = stack_rows(with_neighbours(along_y[:, :eighth]))
     other_slice = lax.ppermute(own_slice, "core", SWAP)
-    token_slice = jnp.concatenate([own_slice, other_slice], axis=1).reshape(n_y * tokens, features)
+    token_slice = jnp.concatenate([own_slice, other_slice], axis=1).reshape(n_y * tall_tokens, features)
     lanes = 2 * wide
     tall = n_z * chunks
-    routed = along_y[:, quarter:].reshape(n_y, n_z, chunks, features).transpose(1, 0, 2, 3)
+    routed = along_y[:, eighth:].reshape(n_y, n_z, chunks, features).transpose(1, 0, 2, 3)
     routed = jnp.pad(
         routed.reshape(n_z, n_y * chunks, features), ((0, 0), (0, 0), (0, lanes - features))
     )
@@ -205,7 +204,7 @@
     partial_pre = to_half(
         jnp.dot(token_slice, weights, preferred_element_type=jnp.float32), pre_scale
     )
-    partial_pre = partial_pre.reshape(n_y, tokens, wide)
+    partial_pre = partial_pre.reshape(n_y, tall_tokens, wide)
     pre_parts = lax.all_to_all(partial_pre, "y", split_axis=0, concat_axis=0, tiled=True)
     pieces = with_neighbours(arrived[None])
     projected = jnp.sum(pre_parts.astype(jnp.float32), axis=0) * (1.0 / pre_scale)

time: 181 us -> 180 us (level)
  starting transfers between devices: 51.3 us -> 62 us
  waiting for transfers between devices: 75.3 us -> 64.6 us
    ppermute x3 -> x6, starting transfers between devices: 9.82 us -> 19.6 us  [with_neighbours(): lax.ppermute(block, ALONG_X, [(i, i ^ k) for i in range(4)])]
    ppermute x1 -> x0, waiting for transfers between devices: 7.1 us -> none  [shards(): own_slice = stack_rows([own_slice, lax.ppermute(own_slice, 'xl', SWAP)])]
    ppermute x3 -> x6, waiting for transfers between devices: 6.23 us -> 11.1 us  [with_neighbours(): lax.ppermute(block, ALONG_X, [(i, i ^ k) for i in range(4)])]
    all_to_all x2, waiting for transfers between devices: 28.3 us -> 24.1 us  [shards(): lax.all_to_all(along_y, 'y', split_axis=0, concat_axis=0, tiled=True)]
    all_to_all x2, waiting for transfers between devices: 16.7 us -> 12.6 us  [shards(): lax.all_to_all(along_z, 'z', split_axis=0, concat_axis=0, tiled=True)]
    all_to_all x2, starting transfers between devices: 13.9 us -> 17.6 us  [shards(): lax.all_to_all(along_z, 'z', split_axis=0, concat_axis=0, tiled=True)]
    ppermute x1 -> x0, starting transfers between devices: 2.72 us -> none  [shards(): own_slice = stack_rows([own_slice, lax.ppermute(own_slice, 'xl', SWAP)])]
  transfers between devices with their start and end apart: 12 -> 14, of which waited for: 10 -> 10; matrix products, arithmetic and copies ran while one was open for 4% -> 4% of each run, Pallas kernels for 0% -> 0%
where the time goes in v7:
time: 180 us; the launch traced here: 179 us
  waiting for transfers between devices  64.6 us (36%)
  starting transfers between devices  62 us (34%)
  blocking collectives  28.4 us (16%)
  local copies, waits for them, and re-layouts  10.4 us (6%)
  matrix products  6.22 us (3%)
  other arithmetic  5.63 us (3%)
    all_gather x1, blocking collectives, shards(): fresh = lax.all_gather(fresh_rows, 'z', axis=0, tiled=True)  28.4 us
    all_to_all x2, waiting for transfers between devices, shards(): lax.all_to_all(along_y, 'y', split_axis=0, concat_axis=0, tiled=True)  24.1 us
    ppermute x6, starting transfers between devices, with_neighbours(): lax.ppermute(block, ALONG_X, [(i, i ^ k) for i in range(4)])  19.6 us
    all_to_all x2, starting transfers between devices, shards(): lax.all_to_all(along_z, 'z', split_axis=0, concat_axis=0, tiled=True)  17.6 us
    all_to_all x1, waiting for transfers between devices, gather_by_exchange(): lax.all_to_all(jnp.broadcast_to(block[None], (count,) + block.shape), axi...  15.1 us
    all_to_all x2, waiting for transfers between devices, shards(): lax.all_to_all(along_z, 'z', split_axis=0, concat_axis=0, tiled=True)  12.6 us
    ppermute x6, waiting for transfers between devices, with_neighbours(): lax.ppermute(block, ALONG_X, [(i, i ^ k) for i in range(4)])  11.1 us
    all_to_all x2, starting transfers between devices, shards(): lax.all_to_all(along_y, 'y', split_axis=0, concat_axis=0, tiled=True)  10.5 us
  transfers between devices with their start and end apart: 14, of which 10 were waited for; matrix products, arithmetic and copies ran while one was open for 4% of the time, Pallas kernels for 0%

profile of v7, /device:TPU:6, one launch (start us, length us, event | category | flops | bytes accessed | tf_op | source)
XLA Modules:
  0.0 179.0 jit_solution(16594311953270700792)
XLA Ops:
  0.7 1.1 copy-done
  2.0 0.7 reshape.129.gain_ref
  2.8 0.9 copy-done.1
  3.7 0.7 copy-done.2
  4.4 0.7 copy-done.4
  5.0 0.4 route_rows.1
  5.5 0.3 reshape.130
  5.8 0.8 pad_maximum_fusion.1
  6.5 7.1 %all-to-all-start = ((bf16[8,48,448]{2,1,0:T(8,128)(2,1)}), bf16[8,48,448]{2,1,0:T(8,128)(2,1)S(1)}, u32[]{:S(2)}, u32[]{:S(2)}) async-start(bf16[8,48,448]{2,1,0:T(8,128)(2,1)} %pad_maximum_fusion.1), calls=%async_computation | async-start | bytes 786432 | tf_op jit(solution)/shard_map/all_to_all | solution.py:177
  13.7 1.5 copy.61
  15.2 13.1 %all-to-all-done = bf16[8,48,448]{2,1,0:T(8,128)(2,1)S(1)} async-done(((bf16[8,48,448]{2,1,0:T(8,128)(2,1)}), bf16[8,48,448]{2,1,0:T(8,128)(2,1)S(1)}, u32[]{:S(2)}, u32[]{:S(2)}) %all-to-all-start) | async-done | bytes 344096 | tf_op jit(solution)/shard_map/all_to_all | solution.py:177
  28.7 0.9 fusion.11
  29.6 10.3 %all-to-all-start.1 = ((bf16[8,64,512]{2,1,0:T(8,128)(2,1)}), bf16[8,64,512]{2,1,0:T(8,128)(2,1)S(1)}, u32[]{:S(2)}, u32[]{:S(2)}) async-start(bf16[8,64,512]{2,1,0:T(8,128)(2,1)} %fusion.11), calls=%async_computation.1 | async-start | bytes 1048576 | tf_op jit(solution)/shard_map/all_to_all | solution.py:194
  39.9 3.3 %collective-permute-start = (bf16[8,16,448]{2,1,0:T(8,128)(2,1)S(1)}, bf16[8,16,448]{2,1,0:T(8,128)(2,1)S(1)}, u32[]{:S(2)}, u32[]{:S(2)}) collective-permute-start(bf16[8,16,448]{2,1,0:T(8,128)(2,1)S(1)} %slice.57.refs_0_), channel_id=1, source_target_pairs={{0,1},{1,0},{256,257},{257,256},{2,3},{3,2},{258,259},{259,258},{4... | collective-permute-start | bytes 344072 | tf_op jit(solution)/shard_map/ppermute | solution.py:69
  43.2 1.9 %collective-permute-start.1 = (bf16[8,16,448]{2,1,0:T(8,128)(2,1)S(1)}, bf16[8,16,448]{2,1,0:T(8,128)(2,1)S(1)}, u32[]{:S(2)}, u32[]{:S(2)}) collective-permute-start(bf16[8,16,448]{2,1,0:T(8,128)(2,1)S(1)} %slice.57.refs_0_), channel_id=1, source_target_pairs={{0,256},{1,257},{256,0},{257,1},{2,258},{3,259},{258,2},{259,3},{4... | collective-permute-start | bytes 344072 | tf_op jit(solution)/shard_map/ppermute | solution.py:69
  45.1 4.6 %collective-permute-start.2 = (bf16[8,16,448]{2,1,0:T(8,128)(2,1)S(1)}, bf16[8,16,448]{2,1,0:T(8,128)(2,1)S(1)}, u32[]{:S(2)}, u32[]{:S(2)}) collective-permute-start(bf16[8,16,448]{2,1,0:T(8,128)(2,1)S(1)} %slice.57.refs_0_), channel_id=1, source_target_pairs={{0,257},{1,256},{256,1},{257,0},{2,259},{3,258},{258,3},{259,2},{4... | collective-permute-start | bytes 344072 | tf_op jit(solution)/shard_map/ppermute | solution.py:69
  49.7 0.3 collective-permute-done.1.refs_2_
  50.1 3.1 %collective-permute-done.2.refs_3_ = bf16[8,16,448]{2,1,0:T(8,128)(2,1)S(1)} collective-permute-done((bf16[8,16,448]{2,1,0:T(8,128)(2,1)S(1)}, bf16[8,16,448]{2,1,0:T(8,128)(2,1)S(1)}, u32[]{:S(2)}, u32[]{:S(2)}) %collective-permute-start.2) | collective-permute-done | bytes 114720 | tf_op jit(solution)/shard_map/ppermute | solution.py:69
  53.3 1.9 %collective-permute-start.3 = (bf16[8,64,448]{2,1,0:T(8,128)(2,1)S(1)}, bf16[8,64,448]{2,1,0:T(8,128)(2,1)S(1)}, u32[]{:S(2)}, u32[]{:S(2)}) collective-permute-start(bf16[8,64,448]{2,1,0:T(8,128)(2,1)S(1)} %stack_rows.2), channel_id=1, source_target_pairs={{0,128},{128,0},{1,129},{129,1},{2,130},{130,2},{3,131},{131,3},{4... | collective-permute-start | bytes 1376264 | tf_op jit(solution)/shard_map/ppermute | solution.py:181
  55.3 1.8 collective-permute-done.3
  57.3 1.3 fusion
  58.6 3.5 %all-to-all-start.2 = ((f16[8,128,256]{2,1,0:T(8,128)(2,1)}), f16[8,128,256]{2,1,0:T(8,128)(2,1)S(1)}, u32[]{:S(2)}, u32[]{:S(2)}) async-start(f16[8,128,256]{2,1,0:T(8,128)(2,1)} %bitcast.8), calls=%async_computation.2 | async-start | bytes 1048576 | tf_op jit(solution)/shard_map/all_to_all | solution.py:208
  62.2 0.3 broadcast_in_dim_reshape.2.refs_0_
  62.4 4.2 %collective-permute-start.4 = (bf16[1,64,1792]{2,1,0:T(8,128)(2,1)S(1)}, bf16[1,64,1792]{2,1,0:T(8,128)(2,1)S(1)}, u32[]{:S(2)}, u32[]{:S(2)}) collective-permute-start(bf16[1,64,1792]{2,1,0:T(8,128)(2,1)S(1)} %broadcast_in_dim_reshape.2.refs_0_), channel_id=1, source_target_pairs={{0,1},{1,0},{256,257},{257,256},{2,3},{3,2},{258,259},{259,258},{4... | collective-permute-start | bytes 688136 | tf_op jit(solution)/shard_map/ppermute | solution.py:69
  66.7 3.1 %collective-permute-start.5 = (bf16[1,64,1792]{2,1,0:T(8,128)(2,1)S(1)}, bf16[1,64,1792]{2,1,0:T(8,128)(2,1)S(1)}, u32[]{:S(2)}, u32[]{:S(2)}) collective-permute-start(bf16[1,64,1792]{2,1,0:T(8,128)(2,1)S(1)} %broadcast_in_dim_reshape.2.refs_0_), channel_id=1, source_target_pairs={{0,256},{1,257},{256,0},{257,1},{2,258},{3,259},{258,2},{259,3},{4... | collective-permute-start | bytes 688136 | tf_op jit(solution)/shard_map/ppermute | solution.py:69
  69.8 2.5 %collective-permute-start.6 = (bf16[1,64,1792]{2,1,0:T(8,128)(2,1)S(1)}, bf16[1,64,1792]{2,1,0:T(8,128)(2,1)S(1)}, u32[]{:S(2)}, u32[]{:S(2)}) collective-permute-start(bf16[1,64,1792]{2,1,0:T(8,128)(2,1)S(1)} %broadcast_in_dim_reshape.2.refs_0_), channel_id=1, source_target_pairs={{0,257},{1,256},{256,1},{257,0},{2,259},{3,258},{258,3},{259,2},{4... | collective-permute-start | bytes 688136 | tf_op jit(solution)/shard_map/ppermute | solution.py:69
  72.4 1.9 %collective-permute-done.4.refs_1_ = bf16[1,64,1792]{2,1,0:T(8,128)(2,1)S(1)} collective-permute-done((bf16[1,64,1792]{2,1,0:T(8,128)(2,1)S(1)}, bf16[1,64,1792]{2,1,0:T(8,128)(2,1)S(1)}, u32[]{:S(2)}, u32[]{:S(2)}) %collective-permute-start.4) | collective-permute-done | bytes 229408 | tf_op jit(solution)/shard_map/ppermute | solution.py:69
  74.3 4.1 %collective-permute-done.5.refs_2_ = bf16[1,64,1792]{2,1,0:T(8,128)(2,1)S(1)} collective-permute-done((bf16[1,64,1792]{2,1,0:T(8,128)(2,1)S(1)}, bf16[1,64,1792]{2,1,0:T(8,128)(2,1)S(1)}, u32[]{:S(2)}, u32[]{:S(2)}) %collective-permute-start.5) | collective-permute-done | bytes 229408 | tf_op jit(solution)/shard_map/ppermute | solution.py:69
  78.4 1.6 collective-permute-done.6.refs_3_
  80.0 1.9 %collective-permute-start.7 = (bf16[256,1792]{1,0:T(8,128)(2,1)S(1)}, bf16[256,1792]{1,0:T(8,128)(2,1)}, u32[]{:S(2)}, u32[]{:S(2)}) collective-permute-start(bf16[256,1792]{1,0:T(8,128)(2,1)S(1)} %bitcast.65), channel_id=1, source_target_pairs={{0,128},{128,0},{1,129},{129,1},{2,130},{130,2},{3,131},{131,3},{4... | collective-permute-start | bytes 2752520 | tf_op jit(solution)/shard_map/ppermute | solution.py:224
  82.2 0.8 broadcast_in_dim.9
  83.1 6.8 %all-to-all-start.3 = ((bf16[8,128,256]{2,1,0:T(8,128)(2,1)}), bf16[8,128,256]{2,1,0:T(8,128)(2,1)S(1)}, u32[]{:S(2)}, u32[]{:S(2)}) async-start(bf16[8,128,256]{2,1,0:T(8,128)(2,1)} %broadcast_in_dim.9), calls=%async_computation.3 | async-start | bytes 1048576 | tf_op jit(solution)/shard_map/all_to_all | solution.py:39
  89.9 2.0 %fusion.4 = f32[256,256]{1,0:T(8,128)S(1)} fusion(bf16[3584,256]{1,0:T(8,128)(2,1)} %bitcast.71, bf16[256,1792]{1,0:T(8,128)(2,1)} %collective-permute-done.7, pred[]{:T(512)S(6)} %eq.53, bf16[1,256,1792]{2,1,0:T(8,128)(2,1)S(1)} %stack_rows.3), kind=kOutput, calls=%fused_computation.13 | convolution fusion | flops 235339776 | bytes 3014657 | tf_op jit(solution)/shard_map/dot_general | solution.py:229
  91.9 0.4 convolution_add_fusion
  92.5 0.3 rev.38
  93.0 15.1 %all-to-all-done.3 = bf16[8,128,256]{2,1,0:T(8,128)(2,1)S(1)} async-done(((bf16[8,128,256]{2,1,0:T(8,128)(2,1)}), bf16[8,128,256]{2,1,0:T(8,128)(2,1)S(1)}, u32[]{:S(2)}, u32[]{:S(2)}) %all-to-all-start.3) | async-done | bytes 524320 | tf_op jit(solution)/shard_map/all_to_all | solution.py:39
  108.1 1.7 convolution_convert_fusion
  109.8 0.7 pad_maximum_fusion.2
  110.6 7.3 %all-to-all-start.4 = ((bf16[8,72,256]{2,1,0:T(8,128)(2,1)}), bf16[8,72,256]{2,1,0:T(8,128)(2,1)S(1)}, u32[]{:S(2)}, u32[]{:S(2)}) async-start(bf16[8,72,256]{2,1,0:T(8,128)(2,1)} %pad_maximum_fusion.2), calls=%async_computation.4 | async-start | bytes 589824 | tf_op jit(solution)/shard_map/all_to_all | solution.py:249
  118.1 12.6 %all-to-all-done.4 = bf16[8,72,256]{2,1,0:T(8,128)(2,1)S(1)} async-done(((bf16[8,72,256]{2,1,0:T(8,128)(2,1)}), bf16[8,72,256]{2,1,0:T(8,128)(2,1)S(1)}, u32[]{:S(2)}, u32[]{:S(2)}) %all-to-all-start.4) | async-done | bytes 294944 | tf_op jit(solution)/shard_map/all_to_all | solution.py:249
  130.8 0.8 fusion.26
  131.8 0.7 pad_maximum_fusion.3
  132.5 3.4 %all-to-all-start.5 = ((bf16[8,72,256]{2,1,0:T(8,128)(2,1)}), bf16[8,72,256]{2,1,0:T(8,128)(2,1)S(1)}, u32[]{:S(2)}, u32[]{:S(2)}) async-start(bf16[8,72,256]{2,1,0:T(8,128)(2,1)} %pad_maximum_fusion.3), calls=%async_computation.5 | async-start | bytes 589824 | tf_op jit(solution)/shard_map/all_to_all | solution.py:267
  136.6 11.0 %all-to-all-done.5 = bf16[8,72,256]{2,1,0:T(8,128)(2,1)S(1)} async-done(((bf16[8,72,256]{2,1,0:T(8,128)(2,1)}), bf16[8,72,256]{2,1,0:T(8,128)(2,1)S(1)}, u32[]{:S(2)}, u32[]{:S(2)}) %all-to-all-start.5) | async-done | bytes 294944 | tf_op jit(solution)/shard_map/all_to_all | solution.py:267
  147.6 28.4 %all-gather.1 = f16[3584,256]{1,0:T(8,128)(2,1)S(1)} all-gather(f16[448,256]{1,0:T(8,128)(2,1)S(1)} %bitcast.76), channel_id=1, replica_groups=mesh['xl'=2,'core'=2,'y'=8,'z'=8,'xh'=2] {'z'}, dimensions={0}, use_global_device_ids=true | all-gather | bytes 2064384 | tf_op jit(solution)/shard_map/all_gather | solution.py:270
  176.0 0.5 multiply_convert_fusion
  176.6 1.5 reshape.150
  178.1 0.8 fusion.2
  (92 shorter events, 3.0 us)
Async XLA Ops:
  0.6 1.2 copy-start
  0.6 13.0 %copy-start.8 = (f32[56,2,128]{2,1,0:T(2,128)S(1)}, f32[56,2,128]{2,1,0:T(2,128)}, u32[]{:S(2)}) copy-start(f32[56,2,128]{2,1,0:T(2,128)} %param.21) | copy-start | bytes 172036
  2.8 0.9 copy-start.1
  3.7 0.7 copy-start.2
  4.4 0.7 copy-start.4
  5.0 8.7 %copy-start.5 = (bf16[1,3584,2,128]{3,2,1,0:T(2,128)(2,1)S(1)}, bf16[1,3584,2,128]{3,2,1,0:T(2,128)(2,1)}, u32[]{:S(2)}) copy-start(bf16[1,3584,2,128]{3,2,1,0:T(2,128)(2,1)} %param.17) | copy-start | bytes 5505028
  6.5 21.8 %all-to-all-start = ((bf16[8,48,448]{2,1,0:T(8,128)(2,1)}), bf16[8,48,448]{2,1,0:T(8,128)(2,1)S(1)}, u32[]{:S(2)}, u32[]{:S(2)}) async-start(bf16[8,48,448]{2,1,0:T(8,128)(2,1)} %pad_maximum_fusion.1), calls=%async_computation | async-start | bytes 786432 | tf_op jit(solution)/shard_map/all_to_all | solution.py:177
  28.7 26.5 %copy-start.14 = (s32[128]{0:T(128)S(1)}, s32[128]{0:T(128)}, u32[]{:S(2)}) copy-start(s32[128]{0:T(128)} %param.19) | copy-start | bytes 1540
  29.6 27.7 %all-to-all-start.1 = ((bf16[8,64,512]{2,1,0:T(8,128)(2,1)}), bf16[8,64,512]{2,1,0:T(8,128)(2,1)S(1)}, u32[]{:S(2)}, u32[]{:S(2)}) async-start(bf16[8,64,512]{2,1,0:T(8,128)(2,1)} %fusion.11), calls=%async_computation.1 | async-start | bytes 1048576 | tf_op jit(solution)/shard_map/all_to_all | solution.py:194
  39.9 9.8 %collective-permute-start = (bf16[8,16,448]{2,1,0:T(8,128)(2,1)S(1)}, bf16[8,16,448]{2,1,0:T(8,128)(2,1)S(1)}, u32[]{:S(2)}, u32[]{:S(2)}) collective-permute-start(bf16[8,16,448]{2,1,0:T(8,128)(2,1)S(1)} %slice.57.refs_0_), channel_id=1, source_target_pairs={{0,1},{1,0},{256,257},{257,256},{2,3},{3,2},{258,259},{259,258},{4... | collective-permute-start | bytes 344072 | tf_op jit(solution)/shard_map/ppermute | solution.py:69
  43.2 6.9 %collective-permute-start.1 = (bf16[8,16,448]{2,1,0:T(8,128)(2,1)S(1)}, bf16[8,16,448]{2,1,0:T(8,128)(2,1)S(1)}, u32[]{:S(2)}, u32[]{:S(2)}) collective-permute-start(bf16[8,16,448]{2,1,0:T(8,128)(2,1)S(1)} %slice.57.refs_0_), channel_id=1, source_target_pairs={{0,256},{1,257},{256,0},{257,1},{2,258},{3,259},{258,2},{259,3},{4... | collective-permute-start | bytes 344072 | tf_op jit(solution)/shard_map/ppermute | solution.py:69
  45.1 8.1 %collective-permute-start.2 = (bf16[8,16,448]{2,1,0:T(8,128)(2,1)S(1)}, bf16[8,16,448]{2,1,0:T(8,128)(2,1)S(1)}, u32[]{:S(2)}, u32[]{:S(2)}) collective-permute-start(bf16[8,16,448]{2,1,0:T(8,128)(2,1)S(1)} %slice.57.refs_0_), channel_id=1, source_target_pairs={{0,257},{1,256},{256,1},{257,0},{2,259},{3,258},{258,3},{259,2},{4... | collective-permute-start | bytes 344072 | tf_op jit(solution)/shard_map/ppermute | solution.py:69
  53.3 3.8 %collective-permute-start.3 = (bf16[8,64,448]{2,1,0:T(8,128)(2,1)S(1)}, bf16[8,64,448]{2,1,0:T(8,128)(2,1)S(1)}, u32[]{:S(2)}, u32[]{:S(2)}) collective-permute-start(bf16[8,64,448]{2,1,0:T(8,128)(2,1)S(1)} %stack_rows.2), channel_id=1, source_target_pairs={{0,128},{128,0},{1,129},{129,1},{2,130},{130,2},{3,131},{131,3},{4... | collective-permute-start | bytes 1376264 | tf_op jit(solution)/shard_map/ppermute | solution.py:181
  57.2 5.2 %copy-start.7 = (bf16[8,128,448]{2,1,0:T(8,128)(2,1)}, bf16[8,128,448]{2,1,0:T(8,128)(2,1)S(1)}, u32[]{:S(2)}) copy-start(bf16[8,128,448]{2,1,0:T(8,128)(2,1)S(1)} %pad_maximum_fusion) | copy-start | bytes 2752516
  57.3 4.9 %copy-start.12 = (bf16[128,128]{1,0:T(8,128)(2,1)S(1)}, bf16[128,128]{1,0:T(8,128)(2,1)}, u32[]{:S(2)}) copy-start(bf16[128,128]{1,0:T(8,128)(2,1)} %param.20) | copy-start | bytes 98308
  58.6 23.4 %all-to-all-start.2 = ((f16[8,128,256]{2,1,0:T(8,128)(2,1)}), f16[8,128,256]{2,1,0:T(8,128)(2,1)S(1)}, u32[]{:S(2)}, u32[]{:S(2)}) async-start(f16[8,128,256]{2,1,0:T(8,128)(2,1)} %bitcast.8), calls=%async_computation.2 | async-start | bytes 1048576 | tf_op jit(solution)/shard_map/all_to_all | solution.py:208
  62.4 11.8 %collective-permute-start.4 = (bf16[1,64,1792]{2,1,0:T(8,128)(2,1)S(1)}, bf16[1,64,1792]{2,1,0:T(8,128)(2,1)S(1)}, u32[]{:S(2)}, u32[]{:S(2)}) collective-permute-start(bf16[1,64,1792]{2,1,0:T(8,128)(2,1)S(1)} %broadcast_in_dim_reshape.2.refs_0_), channel_id=1, source_target_pairs={{0,1},{1,0},{256,257},{257,256},{2,3},{3,2},{258,259},{259,258},{4... | collective-permute-start | bytes 688136 | tf_op jit(solution)/shard_map/ppermute | solution.py:69
  66.7 11.7 %collective-permute-start.5 = (bf16[1,64,1792]{2,1,0:T(8,128)(2,1)S(1)}, bf16[1,64,1792]{2,1,0:T(8,128)(2,1)S(1)}, u32[]{:S(2)}, u32[]{:S(2)}) collective-permute-start(bf16[1,64,1792]{2,1,0:T(8,128)(2,1)S(1)} %broadcast_in_dim_reshape.2.refs_0_), channel_id=1, source_target_pairs={{0,256},{1,257},{256,0},{257,1},{2,258},{3,259},{258,2},{259,3},{4... | collective-permute-start | bytes 688136 | tf_op jit(solution)/shard_map/ppermute | solution.py:69
  69.8 10.2 %collective-permute-start.6 = (bf16[1,64,1792]{2,1,0:T(8,128)(2,1)S(1)}, bf16[1,64,1792]{2,1,0:T(8,128)(2,1)S(1)}, u32[]{:S(2)}, u32[]{:S(2)}) collective-permute-start(bf16[1,64,1792]{2,1,0:T(8,128)(2,1)S(1)} %broadcast_in_dim_reshape.2.refs_0_), channel_id=1, source_target_pairs={{0,257},{1,256},{256,1},{257,0},{2,259},{3,258},{258,3},{259,2},{4... | collective-permute-start | bytes 688136 | tf_op jit(solution)/shard_map/ppermute | solution.py:69
  80.0 9.9 %collective-permute-start.7 = (bf16[256,1792]{1,0:T(8,128)(2,1)S(1)}, bf16[256,1792]{1,0:T(8,128)(2,1)}, u32[]{:S(2)}, u32[]{:S(2)}) collective-permute-start(bf16[256,1792]{1,0:T(8,128)(2,1)S(1)} %bitcast.65), channel_id=1, source_target_pairs={{0,128},{128,0},{1,129},{129,1},{2,130},{130,2},{3,131},{131,3},{4... | collective-permute-start | bytes 2752520 | tf_op jit(solution)/shard_map/ppermute | solution.py:224
  83.1 25.0 %all-to-all-start.3 = ((bf16[8,128,256]{2,1,0:T(8,128)(2,1)}), bf16[8,128,256]{2,1,0:T(8,128)(2,1)S(1)}, u32[]{:S(2)}, u32[]{:S(2)}) async-start(bf16[8,128,256]{2,1,0:T(8,128)(2,1)} %broadcast_in_dim.9), calls=%async_computation.3 | async-start | bytes 1048576 | tf_op jit(solution)/shard_map/all_to_all | solution.py:39
  89.9 2.1 %copy-start.6 = (bf16[448,8,2,128]{3,1,2,0:T(8,128)(2,1)S(1)}, bf16[448,8,2,128]{3,1,2,0:T(8,128)(2,1)}, u32[]{:S(2)}) copy-start(bf16[448,8,2,128]{3,1,2,0:T(8,128)(2,1)} %copy.61) | copy-start | bytes 5505028
  93.0 24.9 %copy-start.3 = (s32[16,8]{0,1:T(8,128)S(1)}, s32[16,8]{0,1:T(8,128)}, u32[]{:S(2)}) copy-start(s32[16,8]{0,1:T(8,128)} %param.15) | copy-start | bytes 1540
  108.1 22.7 %copy-start.9 = (f32[56,2,128]{2,1,0:T(2,128)S(1)}, f32[56,2,128]{2,1,0:T(2,128)}, u32[]{:S(2)}) copy-start(f32[56,2,128]{2,1,0:T(2,128)} %param.21) | copy-start | bytes 172036
  108.1 22.7 %copy-start.10 = (f32[56,2,128]{2,1,0:T(2,128)S(1)}, f32[56,2,128]{2,1,0:T(2,128)}, u32[]{:S(2)}) copy-start(f32[56,2,128]{2,1,0:T(2,128)} %param.22) | copy-start | bytes 172036
  108.1 22.7 %copy-start.11 = (f32[56,2,128]{2,1,0:T(2,128)S(1)}, f32[56,2,128]{2,1,0:T(2,128)}, u32[]{:S(2)}) copy-start(f32[56,2,128]{2,1,0:T(2,128)} %param.23) | copy-start | bytes 172036
  110.6 25.6 %copy-start.13 = (f32[16,8]{0,1:T(8,128)S(1)}, f32[16,8]{0,1:T(8,128)}, u32[]{:S(2)}) copy-start(f32[16,8]{0,1:T(8,128)} %param.16) | copy-start | bytes 1540
  110.6 20.1 %all-to-all-start.4 = ((bf16[8,72,256]{2,1,0:T(8,128)(2,1)}), bf16[8,72,256]{2,1,0:T(8,128)(2,1)S(1)}, u32[]{:S(2)}, u32[]{:S(2)}) async-start(bf16[8,72,256]{2,1,0:T(8,128)(2,1)} %pad_maximum_fusion.2), calls=%async_computation.4 | async-start | bytes 589824 | tf_op jit(solution)/shard_map/all_to_all | solution.py:249
  132.5 15.0 %all-to-all-start.5 = ((bf16[8,72,256]{2,1,0:T(8,128)(2,1)}), bf16[8,72,256]{2,1,0:T(8,128)(2,1)S(1)}, u32[]{:S(2)}, u32[]{:S(2)}) async-start(bf16[8,72,256]{2,1,0:T(8,128)(2,1)} %pad_maximum_fusion.3), calls=%async_computation.5 | async-start | bytes 589824 | tf_op jit(solution)/shard_map/all_to_all | solution.py:267

commit v8 on v7

--- a/solution.py
+++ b/solution.py
@@ -70,7 +70,7 @@
     ]
 
 
-def route_kernel(hidden_ref, beam_ref, gain_ref, ids_ref, out_ref):
+def route_kernel(hidden_ref, gain_ref, ids_ref, out_ref):
     rows, width = hidden_ref.shape
     core = lax.axis_index("core")
     slot = (lax.axis_index("xl") * 2 + lax.axis_index("xh")).astype(jnp.float32)
@@ -88,7 +88,7 @@
         named, (first < second).astype(jnp.float32), preferred_element_type=jnp.float32
     )
     sends = jnp.where(earlier == slot, named, 0.0)
-    parent = second - (second & (BEAMS - 1)) + beam_ref[...]
+    parent = second - (second & (BEAMS - 1)) + ids[TOP : TOP + 1, :]
     source = (first == parent).astype(jnp.float32)
     table = lax.dot_general(
         sends, source, (((1,), (1,)), ((), ())), preferred_element_type=jnp.float32
@@ -112,14 +112,18 @@
     return pl.pallas_call(
         route_kernel,
         out_shape=jax.ShapeDtypeStruct((EXPERTS, width // 2), jnp.bfloat16),
-        in_specs=[pl.BlockSpec(memory_space=pltpu.VMEM)] * 4,
+        in_specs=[pl.BlockSpec(memory_space=pltpu.VMEM)] * 3,
         out_specs=pl.BlockSpec(memory_space=pltpu.VMEM),
         compiler_params=pltpu.CompilerParams(vmem_limit_bytes=4 * 1024 * 1024),
         name="route_rows",
         cost_estimate=pl.CostEstimate(
             flops=2 * EXPERTS * rows * width, bytes_accessed=1 << 19, transcendentals=rows
         ),
-    )(hidden_rows, parent_beam.reshape(1, rows), norm_gain.reshape(1, width), route_ids.T)
+    )(
+        hidden_rows,
+        norm_gain.reshape(1, width),
+        jnp.concatenate([route_ids.T, parent_beam.reshape(1, rows)], axis=0),
+    )
 
 
 def shards(

time: 180 us -> 178 us (0.989)
    unnamed x37 -> x35, local copies, waits for them, and re-layouts: 5.11 us -> 3.78 us
where the time goes in v8:
time: 178 us; the launch traced here: 177 us
  waiting for transfers between devices  64.6 us (36%)
  starting transfers between devices  62 us (35%)
  blocking collectives  28.4 us (16%)
  local copies, waits for them, and re-layouts  9.04 us (5%)
  other arithmetic  6.34 us (4%)
  matrix products  4.99 us (3%)
    all_gather x1, blocking collectives, shards(): fresh = lax.all_gather(fresh_rows, 'z', axis=0, tiled=True)  28.4 us
    all_to_all x2, waiting for transfers between devices, shards(): lax.all_to_all(along_y, 'y', split_axis=0, concat_axis=0, tiled=True)  24.1 us
    ppermute x6, starting transfers between devices, with_neighbours(): lax.ppermute(block, ALONG_X, [(i, i ^ k) for i in range(4)])  19.6 us
    all_to_all x2, starting transfers between devices, shards(): lax.all_to_all(along_z, 'z', split_axis=0, concat_axis=0, tiled=True)  17.7 us
    all_to_all x1, waiting for transfers between devices, gather_by_exchange(): lax.all_to_all(jnp.broadcast_to(block[None], (count,) + block.shape), axi...  15.1 us
    all_to_all x2, waiting for transfers between devices, shards(): lax.all_to_all(along_z, 'z', split_axis=0, concat_axis=0, tiled=True)  12.6 us
    ppermute x6, waiting for transfers between devices, with_neighbours(): lax.ppermute(block, ALONG_X, [(i, i ^ k) for i in range(4)])  11.1 us
    all_to_all x2, starting transfers between devices, shards(): lax.all_to_all(along_y, 'y', split_axis=0, concat_axis=0, tiled=True)  10.5 us
  transfers between devices with their start and end apart: 14, of which 10 were waited for; matrix products, arithmetic and copies ran while one was open for 4% of the time, Pallas kernels for 0%

profile of v8, /device:TPU:6, one launch (start us, length us, event | category | flops | bytes accessed | tf_op | source)
XLA Modules:
  0.0 177.2 jit_solution(579087888251801353)
XLA Ops:
  0.7 1.1 copy-done
  2.0 0.7 reshape.128.gain_ref
  2.8 0.7 pad_add_fusion.ids_ref
  3.5 0.9 copy-done.1
  4.4 0.4 route_rows.1
  4.8 0.3 reshape.130
  5.1 0.8 pad_maximum_fusion.1
  5.9 7.1 %all-to-all-start = ((bf16[8,48,448]{2,1,0:T(8,128)(2,1)}), bf16[8,48,448]{2,1,0:T(8,128)(2,1)S(1)}, u32[]{:S(2)}, u32[]{:S(2)}) async-start(bf16[8,48,448]{2,1,0:T(8,128)(2,1)} %pad_maximum_fusion.1), calls=%async_computation | async-start | bytes 786432 | tf_op jit(solution)/shard_map/all_to_all | solution.py:181
  13.1 1.5 copy.61
  14.6 13.1 %all-to-all-done = bf16[8,48,448]{2,1,0:T(8,128)(2,1)S(1)} async-done(((bf16[8,48,448]{2,1,0:T(8,128)(2,1)}), bf16[8,48,448]{2,1,0:T(8,128)(2,1)S(1)}, u32[]{:S(2)}, u32[]{:S(2)}) %all-to-all-start) | async-done | bytes 344096 | tf_op jit(solution)/shard_map/all_to_all | solution.py:181
  28.1 0.8 fusion.11
  28.9 10.3 %all-to-all-start.1 = ((bf16[8,64,512]{2,1,0:T(8,128)(2,1)}), bf16[8,64,512]{2,1,0:T(8,128)(2,1)S(1)}, u32[]{:S(2)}, u32[]{:S(2)}) async-start(bf16[8,64,512]{2,1,0:T(8,128)(2,1)} %fusion.11), calls=%async_computation.1 | async-start | bytes 1048576 | tf_op jit(solution)/shard_map/all_to_all | solution.py:198
  39.3 3.3 %collective-permute-start = (bf16[8,16,448]{2,1,0:T(8,128)(2,1)S(1)}, bf16[8,16,448]{2,1,0:T(8,128)(2,1)S(1)}, u32[]{:S(2)}, u32[]{:S(2)}) collective-permute-start(bf16[8,16,448]{2,1,0:T(8,128)(2,1)S(1)} %slice.57.refs_0_), channel_id=1, source_target_pairs={{0,1},{1,0},{256,257},{257,256},{2,3},{3,2},{258,259},{259,258},{4... | collective-permute-start | bytes 344072 | tf_op jit(solution)/shard_map/ppermute | solution.py:69
  42.6 1.9 %collective-permute-start.1 = (bf16[8,16,448]{2,1,0:T(8,128)(2,1)S(1)}, bf16[8,16,448]{2,1,0:T(8,128)(2,1)S(1)}, u32[]{:S(2)}, u32[]{:S(2)}) collective-permute-start(bf16[8,16,448]{2,1,0:T(8,128)(2,1)S(1)} %slice.57.refs_0_), channel_id=1, source_target_pairs={{0,256},{1,257},{256,0},{257,1},{2,258},{3,259},{258,2},{259,3},{4... | collective-permute-start | bytes 344072 | tf_op jit(solution)/shard_map/ppermute | solution.py:69
  44.5 4.6 %collective-permute-start.2 = (bf16[8,16,448]{2,1,0:T(8,128)(2,1)S(1)}, bf16[8,16,448]{2,1,0:T(8,128)(2,1)S(1)}, u32[]{:S(2)}, u32[]{:S(2)}) collective-permute-start(bf16[8,16,448]{2,1,0:T(8,128)(2,1)S(1)} %slice.57.refs_0_), channel_id=1, source_target_pairs={{0,257},{1,256},{256,1},{257,0},{2,259},{3,258},{258,3},{259,2},{4... | collective-permute-start | bytes 344072 | tf_op jit(solution)/shard_map/ppermute | solution.py:69
  49.1 0.3 collective-permute-done.1.refs_2_
  49.4 3.1 %collective-permute-done.2.refs_3_ = bf16[8,16,448]{2,1,0:T(8,128)(2,1)S(1)} collective-permute-done((bf16[8,16,448]{2,1,0:T(8,128)(2,1)S(1)}, bf16[8,16,448]{2,1,0:T(8,128)(2,1)S(1)}, u32[]{:S(2)}, u32[]{:S(2)}) %collective-permute-start.2) | collective-permute-done | bytes 114720 | tf_op jit(solution)/shard_map/ppermute | solution.py:69
  52.6 1.9 %collective-permute-start.3 = (bf16[8,64,448]{2,1,0:T(8,128)(2,1)S(1)}, bf16[8,64,448]{2,1,0:T(8,128)(2,1)S(1)}, u32[]{:S(2)}, u32[]{:S(2)}) collective-permute-start(bf16[8,64,448]{2,1,0:T(8,128)(2,1)S(1)} %stack_rows.2), channel_id=1, source_target_pairs={{0,128},{128,0},{1,129},{129,1},{2,130},{130,2},{3,131},{131,3},{4... | collective-permute-start | bytes 1376264 | tf_op jit(solution)/shard_map/ppermute | solution.py:185
  54.7 1.8 collective-permute-done.3
  56.7 1.3 fusion
  57.9 3.5 %all-to-all-start.2 = ((f16[8,128,256]{2,1,0:T(8,128)(2,1)}), f16[8,128,256]{2,1,0:T(8,128)(2,1)S(1)}, u32[]{:S(2)}, u32[]{:S(2)}) async-start(f16[8,128,256]{2,1,0:T(8,128)(2,1)} %bitcast.8), calls=%async_computation.2 | async-start | bytes 1048576 | tf_op jit(solution)/shard_map/all_to_all | solution.py:212
  61.5 0.3 broadcast_in_dim_reshape.2.refs_0_
  61.8 4.2 %collective-permute-start.4 = (bf16[1,64,1792]{2,1,0:T(8,128)(2,1)S(1)}, bf16[1,64,1792]{2,1,0:T(8,128)(2,1)S(1)}, u32[]{:S(2)}, u32[]{:S(2)}) collective-permute-start(bf16[1,64,1792]{2,1,0:T(8,128)(2,1)S(1)} %broadcast_in_dim_reshape.2.refs_0_), channel_id=1, source_target_pairs={{0,1},{1,0},{256,257},{257,256},{2,3},{3,2},{258,259},{259,258},{4... | collective-permute-start | bytes 688136 | tf_op jit(solution)/shard_map/ppermute | solution.py:69
  66.0 3.1 %collective-permute-start.5 = (bf16[1,64,1792]{2,1,0:T(8,128)(2,1)S(1)}, bf16[1,64,1792]{2,1,0:T(8,128)(2,1)S(1)}, u32[]{:S(2)}, u32[]{:S(2)}) collective-permute-start(bf16[1,64,1792]{2,1,0:T(8,128)(2,1)S(1)} %broadcast_in_dim_reshape.2.refs_0_), channel_id=1, source_target_pairs={{0,256},{1,257},{256,0},{257,1},{2,258},{3,259},{258,2},{259,3},{4... | collective-permute-start | bytes 688136 | tf_op jit(solution)/shard_map/ppermute | solution.py:69
  69.2 2.5 %collective-permute-start.6 = (bf16[1,64,1792]{2,1,0:T(8,128)(2,1)S(1)}, bf16[1,64,1792]{2,1,0:T(8,128)(2,1)S(1)}, u32[]{:S(2)}, u32[]{:S(2)}) collective-permute-start(bf16[1,64,1792]{2,1,0:T(8,128)(2,1)S(1)} %broadcast_in_dim_reshape.2.refs_0_), channel_id=1, source_target_pairs={{0,257},{1,256},{256,1},{257,0},{2,259},{3,258},{258,3},{259,2},{4... | collective-permute-start | bytes 688136 | tf_op jit(solution)/shard_map/ppermute | solution.py:69
  71.7 1.9 %collective-permute-done.4.refs_1_ = bf16[1,64,1792]{2,1,0:T(8,128)(2,1)S(1)} collective-permute-done((bf16[1,64,1792]{2,1,0:T(8,128)(2,1)S(1)}, bf16[1,64,1792]{2,1,0:T(8,128)(2,1)S(1)}, u32[]{:S(2)}, u32[]{:S(2)}) %collective-permute-start.4) | collective-permute-done | bytes 229408 | tf_op jit(solution)/shard_map/ppermute | solution.py:69
  73.6 4.1 %collective-permute-done.5.refs_2_ = bf16[1,64,1792]{2,1,0:T(8,128)(2,1)S(1)} collective-permute-done((bf16[1,64,1792]{2,1,0:T(8,128)(2,1)S(1)}, bf16[1,64,1792]{2,1,0:T(8,128)(2,1)S(1)}, u32[]{:S(2)}, u32[]{:S(2)}) %collective-permute-start.5) | collective-permute-done | bytes 229408 | tf_op jit(solution)/shard_map/ppermute | solution.py:69
  77.7 1.6 collective-permute-done.6.refs_3_
  79.4 1.9 %collective-permute-start.7 = (bf16[256,1792]{1,0:T(8,128)(2,1)S(1)}, bf16[256,1792]{1,0:T(8,128)(2,1)}, u32[]{:S(2)}, u32[]{:S(2)}) collective-permute-start(bf16[256,1792]{1,0:T(8,128)(2,1)S(1)} %bitcast.65), channel_id=1, source_target_pairs={{0,128},{128,0},{1,129},{129,1},{2,130},{130,2},{3,131},{131,3},{4... | collective-permute-start | bytes 2752520 | tf_op jit(solution)/shard_map/ppermute | solution.py:228
  81.6 0.9 broadcast_in_dim.9
  82.4 6.8 %all-to-all-start.3 = ((bf16[8,128,256]{2,1,0:T(8,128)(2,1)}), bf16[8,128,256]{2,1,0:T(8,128)(2,1)S(1)}, u32[]{:S(2)}, u32[]{:S(2)}) async-start(bf16[8,128,256]{2,1,0:T(8,128)(2,1)} %broadcast_in_dim.9), calls=%async_computation.3 | async-start | bytes 1048576 | tf_op jit(solution)/shard_map/all_to_all | solution.py:39
  89.3 2.0 %fusion.4 = f32[256,256]{1,0:T(8,128)S(1)} fusion(bf16[3584,256]{1,0:T(8,128)(2,1)} %bitcast.69, bf16[256,1792]{1,0:T(8,128)(2,1)} %collective-permute-done.7, pred[]{:T(512)S(6)} %eq.53, bf16[1,256,1792]{2,1,0:T(8,128)(2,1)S(1)} %stack_rows.3), kind=kOutput, calls=%fused_computation.13 | convolution fusion | flops 235339776 | bytes 3014657 | tf_op jit(solution)/shard_map/dot_general | solution.py:233
  91.3 0.4 convolution_add_fusion
  91.9 0.3 rev.38
  92.4 15.1 %all-to-all-done.3 = bf16[8,128,256]{2,1,0:T(8,128)(2,1)S(1)} async-done(((bf16[8,128,256]{2,1,0:T(8,128)(2,1)}), bf16[8,128,256]{2,1,0:T(8,128)(2,1)S(1)}, u32[]{:S(2)}, u32[]{:S(2)}) %all-to-all-start.3) | async-done | bytes 524320 | tf_op jit(solution)/shard_map/all_to_all | solution.py:39
  107.5 0.5 convolution_convert_fusion
  108.0 0.7 pad_maximum_fusion.2
  108.7 7.3 %all-to-all-start.4 = ((bf16[8,72,256]{2,1,0:T(8,128)(2,1)}), bf16[8,72,256]{2,1,0:T(8,128)(2,1)S(1)}, u32[]{:S(2)}, u32[]{:S(2)}) async-start(bf16[8,72,256]{2,1,0:T(8,128)(2,1)} %pad_maximum_fusion.2), calls=%async_computation.4 | async-start | bytes 589824 | tf_op jit(solution)/shard_map/all_to_all | solution.py:253
  116.2 12.6 %all-to-all-done.4 = bf16[8,72,256]{2,1,0:T(8,128)(2,1)S(1)} async-done(((bf16[8,72,256]{2,1,0:T(8,128)(2,1)}), bf16[8,72,256]{2,1,0:T(8,128)(2,1)S(1)}, u32[]{:S(2)}, u32[]{:S(2)}) %all-to-all-start.4) | async-done | bytes 294944 | tf_op jit(solution)/shard_map/all_to_all | solution.py:253
  128.9 0.8 fusion.26
  129.9 0.7 pad_maximum_fusion.3
  130.7 3.4 %all-to-all-start.5 = ((bf16[8,72,256]{2,1,0:T(8,128)(2,1)}), bf16[8,72,256]{2,1,0:T(8,128)(2,1)S(1)}, u32[]{:S(2)}, u32[]{:S(2)}) async-start(bf16[8,72,256]{2,1,0:T(8,128)(2,1)} %pad_maximum_fusion.3), calls=%async_computation.5 | async-start | bytes 589824 | tf_op jit(solution)/shard_map/all_to_all | solution.py:271
  134.5 0.2 select_reduce_fusion
  134.7 11.0 %all-to-all-done.5 = bf16[8,72,256]{2,1,0:T(8,128)(2,1)S(1)} async-done(((bf16[8,72,256]{2,1,0:T(8,128)(2,1)}), bf16[8,72,256]{2,1,0:T(8,128)(2,1)S(1)}, u32[]{:S(2)}, u32[]{:S(2)}) %all-to-all-start.5) | async-done | bytes 294944 | tf_op jit(solution)/shard_map/all_to_all | solution.py:271
  145.8 28.4 %all-gather.1 = f16[3584,256]{1,0:T(8,128)(2,1)S(1)} all-gather(f16[448,256]{1,0:T(8,128)(2,1)S(1)} %bitcast.74), channel_id=1, replica_groups=mesh['xl'=2,'core'=2,'y'=8,'z'=8,'xh'=2] {'z'}, dimensions={0}, use_global_device_ids=true | all-gather | bytes 2064384 | tf_op jit(solution)/shard_map/all_gather | solution.py:274
  174.2 0.5 multiply_convert_fusion
  174.9 1.5 reshape.150
  176.4 0.8 fusion.2
  (91 shorter events, 2.8 us)
Async XLA Ops:
  0.6 1.2 copy-start
  0.6 12.4 %copy-start.6 = (f32[56,2,128]{2,1,0:T(2,128)S(1)}, f32[56,2,128]{2,1,0:T(2,128)}, u32[]{:S(2)}) copy-start(f32[56,2,128]{2,1,0:T(2,128)} %param.21) | copy-start | bytes 172036
  3.5 0.9 copy-start.1
  4.4 8.7 %copy-start.2 = (bf16[1,3584,2,128]{3,2,1,0:T(2,128)(2,1)S(1)}, bf16[1,3584,2,128]{3,2,1,0:T(2,128)(2,1)}, u32[]{:S(2)}) copy-start(bf16[1,3584,2,128]{3,2,1,0:T(2,128)(2,1)} %param.17) | copy-start | bytes 5505028
  5.9 21.8 %all-to-all-start = ((bf16[8,48,448]{2,1,0:T(8,128)(2,1)}), bf16[8,48,448]{2,1,0:T(8,128)(2,1)S(1)}, u32[]{:S(2)}, u32[]{:S(2)}) async-start(bf16[8,48,448]{2,1,0:T(8,128)(2,1)} %pad_maximum_fusion.1), calls=%async_computation | async-start | bytes 786432 | tf_op jit(solution)/shard_map/all_to_all | solution.py:181
  28.0 26.5 %copy-start.13 = (s32[128]{0:T(128)S(1)}, s32[128]{0:T(128)}, u32[]{:S(2)}) copy-start(s32[128]{0:T(128)} %param.19) | copy-start | bytes 1540
  28.9 27.6 %all-to-all-start.1 = ((bf16[8,64,512]{2,1,0:T(8,128)(2,1)}), bf16[8,64,512]{2,1,0:T(8,128)(2,1)S(1)}, u32[]{:S(2)}, u32[]{:S(2)}) async-start(bf16[8,64,512]{2,1,0:T(8,128)(2,1)} %fusion.11), calls=%async_computation.1 | async-start | bytes 1048576 | tf_op jit(solution)/shard_map/all_to_all | solution.py:198
  39.3 9.8 %collective-permute-start = (bf16[8,16,448]{2,1,0:T(8,128)(2,1)S(1)}, bf16[8,16,448]{2,1,0:T(8,128)(2,1)S(1)}, u32[]{:S(2)}, u32[]{:S(2)}) collective-permute-start(bf16[8,16,448]{2,1,0:T(8,128)(2,1)S(1)} %slice.57.refs_0_), channel_id=1, source_target_pairs={{0,1},{1,0},{256,257},{257,256},{2,3},{3,2},{258,259},{259,258},{4... | collective-permute-start | bytes 344072 | tf_op jit(solution)/shard_map/ppermute | solution.py:69
  42.6 6.9 %collective-permute-start.1 = (bf16[8,16,448]{2,1,0:T(8,128)(2,1)S(1)}, bf16[8,16,448]{2,1,0:T(8,128)(2,1)S(1)}, u32[]{:S(2)}, u32[]{:S(2)}) collective-permute-start(bf16[8,16,448]{2,1,0:T(8,128)(2,1)S(1)} %slice.57.refs_0_), channel_id=1, source_target_pairs={{0,256},{1,257},{256,0},{257,1},{2,258},{3,259},{258,2},{259,3},{4... | collective-permute-start | bytes 344072 | tf_op jit(solution)/shard_map/ppermute | solution.py:69
  44.5 8.1 %collective-permute-start.2 = (bf16[8,16,448]{2,1,0:T(8,128)(2,1)S(1)}, bf16[8,16,448]{2,1,0:T(8,128)(2,1)S(1)}, u32[]{:S(2)}, u32[]{:S(2)}) collective-permute-start(bf16[8,16,448]{2,1,0:T(8,128)(2,1)S(1)} %slice.57.refs_0_), channel_id=1, source_target_pairs={{0,257},{1,256},{256,1},{257,0},{2,259},{3,258},{258,3},{259,2},{4... | collective-permute-start | bytes 344072 | tf_op jit(solution)/shard_map/ppermute | solution.py:69
  52.6 3.8 %collective-permute-start.3 = (bf16[8,64,448]{2,1,0:T(8,128)(2,1)S(1)}, bf16[8,64,448]{2,1,0:T(8,128)(2,1)S(1)}, u32[]{:S(2)}, u32[]{:S(2)}) collective-permute-start(bf16[8,64,448]{2,1,0:T(8,128)(2,1)S(1)} %stack_rows.2), channel_id=1, source_target_pairs={{0,128},{128,0},{1,129},{129,1},{2,130},{130,2},{3,131},{131,3},{4... | collective-permute-start | bytes 1376264 | tf_op jit(solution)/shard_map/ppermute | solution.py:185
  56.6 1.4 copy-start.4
  56.6 4.9 %copy-start.10 = (bf16[128,128]{1,0:T(8,128)(2,1)S(1)}, bf16[128,128]{1,0:T(8,128)(2,1)}, u32[]{:S(2)}) copy-start(bf16[128,128]{1,0:T(8,128)(2,1)} %param.20) | copy-start | bytes 98308
  57.9 23.4 %all-to-all-start.2 = ((f16[8,128,256]{2,1,0:T(8,128)(2,1)}), f16[8,128,256]{2,1,0:T(8,128)(2,1)S(1)}, u32[]{:S(2)}, u32[]{:S(2)}) async-start(f16[8,128,256]{2,1,0:T(8,128)(2,1)} %bitcast.8), calls=%async_computation.2 | async-start | bytes 1048576 | tf_op jit(solution)/shard_map/all_to_all | solution.py:212
  61.8 11.8 %collective-permute-start.4 = (bf16[1,64,1792]{2,1,0:T(8,128)(2,1)S(1)}, bf16[1,64,1792]{2,1,0:T(8,128)(2,1)S(1)}, u32[]{:S(2)}, u32[]{:S(2)}) collective-permute-start(bf16[1,64,1792]{2,1,0:T(8,128)(2,1)S(1)} %broadcast_in_dim_reshape.2.refs_0_), channel_id=1, source_target_pairs={{0,1},{1,0},{256,257},{257,256},{2,3},{3,2},{258,259},{259,258},{4... | collective-permute-start | bytes 688136 | tf_op jit(solution)/shard_map/ppermute | solution.py:69
  66.0 11.7 %collective-permute-start.5 = (bf16[1,64,1792]{2,1,0:T(8,128)(2,1)S(1)}, bf16[1,64,1792]{2,1,0:T(8,128)(2,1)S(1)}, u32[]{:S(2)}, u32[]{:S(2)}) collective-permute-start(bf16[1,64,1792]{2,1,0:T(8,128)(2,1)S(1)} %broadcast_in_dim_reshape.2.refs_0_), channel_id=1, source_target_pairs={{0,256},{1,257},{256,0},{257,1},{2,258},{3,259},{258,2},{259,3},{4... | collective-permute-start | bytes 688136 | tf_op jit(solution)/shard_map/ppermute | solution.py:69
  69.2 10.2 %collective-permute-start.6 = (bf16[1,64,1792]{2,1,0:T(8,128)(2,1)S(1)}, bf16[1,64,1792]{2,1,0:T(8,128)(2,1)S(1)}, u32[]{:S(2)}, u32[]{:S(2)}) collective-permute-start(bf16[1,64,1792]{2,1,0:T(8,128)(2,1)S(1)} %broadcast_in_dim_reshape.2.refs_0_), channel_id=1, source_target_pairs={{0,257},{1,256},{256,1},{257,0},{2,259},{3,258},{258,3},{259,2},{4... | collective-permute-start | bytes 688136 | tf_op jit(solution)/shard_map/ppermute | solution.py:69
  79.4 9.9 %collective-permute-start.7 = (bf16[256,1792]{1,0:T(8,128)(2,1)S(1)}, bf16[256,1792]{1,0:T(8,128)(2,1)}, u32[]{:S(2)}, u32[]{:S(2)}) collective-permute-start(bf16[256,1792]{1,0:T(8,128)(2,1)S(1)} %bitcast.65), channel_id=1, source_target_pairs={{0,128},{128,0},{1,129},{129,1},{2,130},{130,2},{3,131},{131,3},{4... | collective-permute-start | bytes 2752520 | tf_op jit(solution)/shard_map/ppermute | solution.py:228
  82.4 25.0 %all-to-all-start.3 = ((bf16[8,128,256]{2,1,0:T(8,128)(2,1)}), bf16[8,128,256]{2,1,0:T(8,128)(2,1)S(1)}, u32[]{:S(2)}, u32[]{:S(2)}) async-start(bf16[8,128,256]{2,1,0:T(8,128)(2,1)} %broadcast_in_dim.9), calls=%async_computation.3 | async-start | bytes 1048576 | tf_op jit(solution)/shard_map/all_to_all | solution.py:39
  89.3 2.1 %copy-start.3 = (bf16[448,8,2,128]{3,1,2,0:T(8,128)(2,1)S(1)}, bf16[448,8,2,128]{3,1,2,0:T(8,128)(2,1)}, u32[]{:S(2)}) copy-start(bf16[448,8,2,128]{3,1,2,0:T(8,128)(2,1)} %copy.61) | copy-start | bytes 5505028
  91.3 16.2 %copy-start.5 = (bf16[8,128,448]{2,1,0:T(8,128)(2,1)S(1)}, bf16[8,128,448]{2,1,0:T(8,128)(2,1)}, u32[]{:S(2)}) copy-start(bf16[8,128,448]{2,1,0:T(8,128)(2,1)} %copy-done.4) | copy-start | bytes 2752516
  92.3 23.7 %copy-start.11 = (s32[16,8]{0,1:T(8,128)S(1)}, s32[16,8]{0,1:T(8,128)}, u32[]{:S(2)}) copy-start(s32[16,8]{0,1:T(8,128)} %param.15) | copy-start | bytes 1540
  107.5 21.5 %copy-start.7 = (f32[56,2,128]{2,1,0:T(2,128)S(1)}, f32[56,2,128]{2,1,0:T(2,128)}, u32[]{:S(2)}) copy-start(f32[56,2,128]{2,1,0:T(2,128)} %param.21) | copy-start | bytes 172036
  107.5 21.5 %copy-start.8 = (f32[56,2,128]{2,1,0:T(2,128)S(1)}, f32[56,2,128]{2,1,0:T(2,128)}, u32[]{:S(2)}) copy-start(f32[56,2,128]{2,1,0:T(2,128)} %param.22) | copy-start | bytes 172036
  107.5 21.5 %copy-start.9 = (f32[56,2,128]{2,1,0:T(2,128)S(1)}, f32[56,2,128]{2,1,0:T(2,128)}, u32[]{:S(2)}) copy-start(f32[56,2,128]{2,1,0:T(2,128)} %param.23) | copy-start | bytes 172036
  108.7 25.6 %copy-start.12 = (f32[16,8]{0,1:T(8,128)S(1)}, f32[16,8]{0,1:T(8,128)}, u32[]{:S(2)}) copy-start(f32[16,8]{0,1:T(8,128)} %param.16) | copy-start | bytes 1540
  108.7 20.1 %all-to-all-start.4 = ((bf16[8,72,256]{2,1,0:T(8,128)(2,1)}), bf16[8,72,256]{2,1,0:T(8,128)(2,1)S(1)}, u32[]{:S(2)}, u32[]{:S(2)}) async-start(bf16[8,72,256]{2,1,0:T(8,128)(2,1)} %pad_maximum_fusion.2), calls=%async_computation.4 | async-start | bytes 589824 | tf_op jit(solution)/shard_map/all_to_all | solution.py:253
  130.7 15.1 %all-to-all-start.5 = ((bf16[8,72,256]{2,1,0:T(8,128)(2,1)}), bf16[8,72,256]{2,1,0:T(8,128)(2,1)S(1)}, u32[]{:S(2)}, u32[]{:S(2)}) async-start(bf16[8,72,256]{2,1,0:T(8,128)(2,1)} %pad_maximum_fusion.3), calls=%async_computation.5 | async-start | bytes 589824 | tf_op jit(solution)/shard_map/all_to_all | solution.py:271
